TPU v7x, 512 devices: a whole 4x8x8 slice. The times are simulated.
512 devices in a mesh: chan: 32 (over x_hi, z, core), pair: 8 (over y), integ: 2 (over x_lo).
Axes of the slice: x: 4 (x_hi: 2, x_lo: 2; x = x_hi * 2 + x_lo), y: 8, z: 8, core: 2. Of those that a mesh axis runs over, the one named last changes fastest.
Arguments:
- spectra: bfloat16 [2, 32, 2048, 2048], P(None, None, ('chan', 'integ'), 'pair'), may hold values from -8 to 8
- pair_table: int32 [136, 2], P('pair'), may hold values from 0 to 15, as said below
Outputs:
- visibility: float32 [136, 32, 2, 128, 128], P('pair', 'chan', None, 'integ')
Inputs may be any that keep to these rules, and one draw needn't show every extreme that they name: `pair_table`: each row names two antenna blocks a <= b (column 0 is a); every such pair of the 16 blocks stands in exactly one row.
All inputs are finite; a program needn't handle non-finite values.
Results may differ from a plain program's by a relative error of at most 0.0003.
Values may be sent and summed in bfloat16 or wider, within the bound.
No kernel may reach another device: no remote copies, remote signals or barrier semaphores. Data moves between devices by JAX's collectives and lax.ppermute only.
A program may use at most 64 MiB of HBM per device.

v0:
```python
import jax
import jax.numpy as jnp
from jax import lax
from jax.sharding import PartitionSpec as P

BLOCK = 128
TIME = 2048


def body(spectra, pair_table):
    turned = lax.all_to_all(spectra, "chan", split_axis=1, concat_axis=2, tiled=True)
    gathered = lax.all_gather(turned, "pair", axis=3, tiled=True)
    width = BLOCK

    def pair_tile(entry):
        left = lax.dynamic_slice_in_dim(gathered, entry[0] * width, width, 3)
        right = lax.dynamic_slice_in_dim(gathered, entry[1] * width, width, 3)
        real_part = jnp.einsum(
            "ctr,cts->crs", left[0], right[0], preferred_element_type=jnp.float32
        ) + jnp.einsum("ctr,cts->crs", left[1], right[1], preferred_element_type=jnp.float32)
        imag_part = jnp.einsum(
            "ctr,cts->crs", left[0], right[1], preferred_element_type=jnp.float32
        ) - jnp.einsum("ctr,cts->crs", left[1], right[0], preferred_element_type=jnp.float32)
        return jnp.stack([real_part, imag_part], 1)

    partial_sums = lax.map(pair_tile, pair_table)
    summed = lax.psum_scatter(partial_sums, "integ", scatter_dimension=3, tiled=True)
    return summed * (1.0 / TIME)


def solution(mesh):
    in_specs = (P(None, None, ("chan", "integ"), "pair"), P("pair", None))
    out_specs = P("pair", "chan", None, "integ", None)
    return jax.shard_map(body, mesh=mesh, in_specs=in_specs, out_specs=out_specs, check_vma=False)
```

profile of v0, /device:TPU:1, one launch (start us, length us, event | category | flops | bytes accessed | tf_op | source)
XLA Modules:
  0.0 345.5 jit_solution(17829757188923659367)
XLA Ops:
  7.9 42.0 %all_to_all.12 = bf16[2,32,32,256]{3,2,0,1:T(8,128)(2,1)S(1)} all-to-all(bf16[2,32,32,256]{3,2,0,1:T(8,128)(2,1)S(1)} %copy.4), channel_id=1, replica_groups=mesh['chan'=32,'pair'=8,'integ'=2] {'chan'}, dimensions={1} | all-to-all | bytes 2097152 | tf_op jit(solution)/shard_map/all_to_all | solution.py:11
  51.0 97.9 %all-gather.2.cloned.1.call-done = bf16[2,1,1024,2048]{3,2,0,1:T(8,128)(2,1)} async-done(((bf16[2,1,1024,256]{3,2,0,1:T(8,128)(2,1)}), bf16[2,1,1024,2048]{3,2,0,1:T(8,128)(2,1)}) %all-gather.2.cloned.1.call-update) | async-done | bytes 8388624 | tf_op jit(solution)/shard_map/all_gather | solution.py:12
  148.9 144.5 %while.10 = (s32[]{:T(128)}, f32[17,1,2,128,128]{4,3,2,1,0:T(8,128)}, s32[17,2]{0,1:T(2,128)}, bf16[2,1,1024,2048]{3,2,1,0:T(8,128)(2,1)}, s32[]{:T(128)}, /*index=5*/s32[1,1]{0,1:T(1,128)}, s32[]{:T(128)}, s32[]{:T(128)}, s32[]{}) while((s32[]{:T(128)}, f32[17,1,2,128,128]{4,3,2,1,0:T(8,128)}, s32[17,2]{0,1:T(2,128)}, ...), condition=%wide.region_1.2_spmd, body=%wide.region_0.1_spmd.sunk | while | flops 134283264 | bytes 2755337 | solution.py:26
  152.7 1.3 fusion.20
  154.1 1.3 fusion.17
  155.4 1.3 fusion.18
  161.2 1.3 fusion.20
  162.6 1.3 fusion.17
  163.9 1.3 fusion.18
  169.7 1.3 fusion.20
  171.1 1.3 fusion.17
  172.4 1.3 fusion.18
  178.2 1.3 fusion.20
  179.6 1.3 fusion.17
  180.9 1.3 fusion.18
  186.7 1.3 fusion.20
  188.1 1.3 fusion.17
  189.4 1.3 fusion.18
  195.2 1.3 fusion.20
  196.5 1.3 fusion.17
  197.9 1.3 fusion.18
  203.7 1.3 fusion.20
  205.1 1.3 fusion.17
  206.4 1.3 fusion.18
  212.3 1.3 fusion.20
  213.6 1.3 fusion.17
  214.9 1.3 fusion.18
  220.7 1.3 fusion.20
  223.4 1.3 fusion.18
  229.2 1.3 fusion.20
  231.9 1.3 fusion.18
  237.7 1.3 fusion.20
  239.1 1.3 fusion.17
  240.4 1.3 fusion.18
  246.2 1.3 fusion.20
  248.9 1.3 fusion.18
  254.7 1.3 fusion.20
  257.4 1.3 fusion.18
  263.2 1.3 fusion.20
  265.9 1.3 fusion.18
  271.7 1.3 fusion.20
  274.4 1.3 fusion.18
  280.2 1.3 fusion.20
  282.9 1.3 fusion.18
  288.7 1.3 fusion.20
  291.4 1.3 fusion.18
  293.4 42.9 %reduce-scatter.2.cloned.1.call-done = f32[17,1,2,64,128]{4,3,2,1,0:T(8,128)} async-done(((f32[17,1,2,128,128]{4,3,2,1,0:T(8,128)}), f32[17,1,2,64,128]{4,3,2,1,0:T(8,128)}) %reduce-scatter.2.cloned.1.call-update) | async-done | bytes 1114128 | tf_op jit(solution)/shard_map/reduce_scatter | solution.py:27
  336.3 2.4 broadcast_multiply_fusion
  (83 shorter events, 68.1 us)
Async XLA Ops:
  6.5 142.3 %all-gather.2.cloned.1.call-start = ((), (), s32[]{:S(2)}) async-start(), calls=%async_computation.2 | async-start | bytes 9437184 | tf_op jit(solution)/shard_map/all_gather | solution.py:12
  50.9 285.4 %reduce-scatter.2.cloned.1.call-start = ((), (), s32[]{:S(2)}) async-start(), calls=%async_computation.3 | async-start | bytes 3342336 | tf_op jit(solution)/shard_map/reduce_scatter | solution.py:27
Sparse Core Ops, SparseCore 0:
  51.0 97.8 all-gather.1
  293.5 42.7 reduce-scatter.1
where the time goes:
time: 348 us; the launch traced here: 345 us
  waiting for transfers between devices  141 us (41%)
  matrix products  89.1 us (26%)
  blocking collectives  42 us (12%)
  local copies, waits for them, and re-layouts  24.1 us (7%)
  loops' own time  22.4 us (6%)
  other arithmetic  13.7 us (4%)
  between operations  13.4 us (4%)
    all_gather x1, waiting for transfers between devices, body(): gathered = lax.all_gather(turned, 'pair', axis=3, tiled=True)  97.9 us
    reduce_scatter x1, waiting for transfers between devices, body(): lax.psum_scatter(partial_sums, 'integ', scatter_dimension=3, tiled=True)  42.9 us
    all_to_all x1, blocking collectives, body(): lax.all_to_all(spectra, 'chan', split_axis=1, concat_axis=2, tiled=True)  42 us
    another operation x1, loops' own time, body(): partial_sums = lax.map(pair_tile, pair_table)  22.4 us
    dot_general x17, matrix products, pair_tile(): jnp.einsum('ctr,cts->crs', left[1], right[1], preferred_element_type=jnp....  22.3 us
    dot_general x17, matrix products, pair_tile(): jnp.einsum('ctr,cts->crs', left[0], right[1], preferred_element_type=jnp....  22.3 us
    dot_general x17, matrix products, pair_tile(): jnp.einsum('ctr,cts->crs', left[1], right[0], preferred_element_type=jnp....  22.3 us
    dot_general x17, matrix products, pair_tile(): jnp.einsum('ctr,cts->crs', left[0], right[0], preferred_element_type=jnp....  22.2 us
  transfers between devices with their start and end apart: 2, of which 2 were waited for; matrix products, arithmetic and copies ran while one was open for 0% of the time, Pallas kernels for 0%

commit v1 on v0

v1 whole, which is shorter than its diff:
```python
import functools

import jax
import jax.numpy as jnp
from jax import lax
from jax.experimental import pallas as pl
from jax.experimental.pallas import tpu as pltpu
from jax.sharding import PartitionSpec as P

BLOCK = 128
TIME = 2048


def tiles_kernel(place, table, gathered, keep, send, whole):
    half = BLOCK // 2
    samples = gathered.shape[1] * gathered.shape[3]

    def both_parts(block):
        owner, lane = block // 2, pl.multiple_of(block % 2 * BLOCK, BLOCK)
        parts = [gathered[owner, :, i, :, pl.ds(lane, BLOCK)].reshape(samples, BLOCK) for i in range(2)]
        return jnp.concatenate(parts, axis=1)

    def tile(k, carry):
        left, right = both_parts(table[k, 0]), both_parts(table[k, 1])
        product = lax.dot_general(left, right, (((0,), (0,)), ((), ())), preferred_element_type=jnp.float32)
        whole[0] = product[:BLOCK, :BLOCK] + product[BLOCK:, BLOCK:]
        whole[1] = product[:BLOCK, BLOCK:] - product[BLOCK:, :BLOCK]
        keep[k] = whole[:, pl.ds(pl.multiple_of(place[0] * half, half), half), :]
        send[k] = whole[:, pl.ds(pl.multiple_of((1 - place[0]) * half, half), half), :]
        return carry

    lax.fori_loop(0, table.shape[0], tile, 0)


def tiles(place, table, gathered):
    count = table.shape[0]
    part = jax.ShapeDtypeStruct((count, 2, BLOCK // 2, BLOCK), jnp.float32)
    return pl.pallas_call(
        tiles_kernel,
        out_shape=(part, part),
        in_specs=[pl.BlockSpec(memory_space=pltpu.SMEM)] * 2 + [pl.BlockSpec(memory_space=pltpu.VMEM)],
        out_specs=(pl.BlockSpec(memory_space=pltpu.VMEM),) * 2,
        scratch_shapes=[pltpu.VMEM((2, BLOCK, BLOCK), jnp.float32)],
        compiler_params=pltpu.CompilerParams(vmem_limit_bytes=40 * 2**20),
        name="tiles",
    )(place, table, gathered)


def body(spectra, pair_table):
    by_channel = spectra.transpose(1, 0, 2, 3)
    turned = lax.all_to_all(by_channel, "chan", split_axis=0, concat_axis=0, tiled=True)
    gathered = lax.all_gather(turned, "pair", axis=0)
    place = lax.axis_index("integ")[None].astype(jnp.int32)
    keep, send = tiles(place, pair_table, gathered)
    other = lax.ppermute(send, "integ", [(0, 1), (1, 0)])
    return ((keep + other) * (1.0 / TIME))[:, None]


def solution(mesh):
    in_specs = (P(None, None, ("chan", "integ"), "pair"), P("pair", None))
    out_specs = P("pair", "chan", None, "integ", None)
    return jax.shard_map(body, mesh=mesh, in_specs=in_specs, out_specs=out_specs, check_vma=False)
```

time: 348 us -> 190 us (0.55)
  the two profiles are of different devices: /device:TPU:1 before, /device:TPU:2 now
where the time goes in v1:
time: 190 us
  waiting for transfers between devices  119 us (63%)
  blocking collectives  42 us (22%)
  between operations  13.4 us (7%)
  Pallas kernels  6.97 us (4%)
  local copies, waits for them, and re-layouts  4.79 us (3%)
  starting transfers between devices  2.46 us (1%)
    all_gather x1, waiting for transfers between devices, body(): gathered = lax.all_gather(turned, 'pair', axis=0)  93 us
    all_to_all x1, blocking collectives, body(): lax.all_to_all(by_channel, 'chan', split_axis=0, concat_axis=0, tiled=True)  42 us
    ppermute x1, waiting for transfers between devices, body(): other = lax.ppermute(send, 'integ', [(0, 1), (1, 0)])  25.7 us
    pallas_call x1, Pallas kernels, tiles(): pl.pallas_call(tiles_kernel, out_shape=(part, part), in_specs=[pl.BlockSp...  6.97 us
    unnamed x6, local copies, waits for them, and re-layouts  4.79 us
  transfers between devices with their start and end apart: 2, of which 2 were waited for; matrix products, arithmetic and copies ran while one was open for 0% of the time, Pallas kernels for 0%

profile of v1, /device:TPU:2, one launch (start us, length us, event | category | flops | bytes accessed | tf_op | source)
XLA Modules:
  0.0 189.6 jit_solution(5912984500942094219)
XLA Ops:
  6.5 0.0 all-gather.3.cloned.1.call-start
  6.5 1.3 copy.13
  7.9 0.0 copy-start.1
  7.9 42.0 %all_to_all.5 = bf16[32,2,32,256]{3,2,1,0:T(8,128)(2,1)} all-to-all(bf16[32,2,32,256]{3,2,1,0:T(8,128)(2,1)S(1)} %bitcast.10), channel_id=1, replica_groups=mesh['chan'=32,'pair'=8,'integ'=2] {'chan'}, dimensions={0} | all-to-all | bytes 2097152 | tf_op jit(solution)/shard_map/all_to_all | solution.py:51
  49.9 0.0 all-gather.3.cloned.1.call-update
  49.9 0.0 copy-done.1
  50.0 0.1 copy.10.table
  50.1 93.0 %all-gather.3.cloned.1.call-done = bf16[256,2,32,256]{3,2,1,0:T(8,128)(2,1)} async-done(((bf16[32,2,32,256]{3,2,1,0:T(8,128)(2,1)}), bf16[256,2,32,256]{3,2,1,0:T(8,128)(2,1)}) %all-gather.3.cloned.1.call-update) | async-done | bytes 8388624 | tf_op jit(solution)/shard_map/all_gather | solution.py:52
  143.0 0.0 copy-start
  143.0 3.4 %copy-done = bf16[256,2,32,256]{3,2,1,0:T(8,128)(2,1)S(1)} copy-done((bf16[256,2,32,256]{3,2,1,0:T(8,128)(2,1)S(1)}, bf16[256,2,32,256]{3,2,1,0:T(8,128)(2,1)}, u32[]{:S(2)}) %copy-start) | copy-done | bytes 8388632
  146.4 7.0 %tiles.1 = (f32[17,2,64,128]{3,2,1,0:T(8,128)S(1)}, f32[17,2,64,128]{3,2,1,0:T(8,128)S(1)}) custom-call(s32[1]{0:T(128)} %bitcast.place, s32[17,2]{1,0:T(8,128)S(1)} %copy.10.table, bf16[8,32,2,32,256]{4,3,2,1,0:T(8,128)(2,1)S(1)} %bitcast.9), custom_call_target="tpu_custom_call" | custom-call | tf_op jit(solution)/shard_map/tiles/pallas_call | solution.py:38
  153.4 2.5 %collective-permute-start = (f32[17,2,64,128]{3,2,1,0:T(8,128)S(1)}, f32[17,2,64,128]{3,2,1,0:T(8,128)S(1)}, u32[]{:S(2)}, u32[]{:S(2)}) collective-permute-start(f32[17,2,64,128]{3,2,1,0:T(8,128)S(1)} %get-tuple-element.8), channel_id=1, source_target_pairs={{0,1},{1,0},{2,3},{3,2},{4,5},{5,4},{6,7},{7,6},{8,9},{9,8},{10,11... | collective-permute-start | bytes 3342344 | tf_op jit(solution)/shard_map/ppermute | solution.py:55
  155.8 25.7 %collective-permute-done = f32[17,2,64,128]{3,2,1,0:T(8,128)S(1)} collective-permute-done((f32[17,2,64,128]{3,2,1,0:T(8,128)S(1)}, f32[17,2,64,128]{3,2,1,0:T(8,128)S(1)}, u32[]{:S(2)}, u32[]{:S(2)}) %collective-permute-start) | collective-permute-done | bytes 1114144 | tf_op jit(solution)/shard_map/ppermute | solution.py:55
  181.6 1.2 multiply_bitcast_fusion
Async XLA Ops:
  6.5 136.5 %all-gather.3.cloned.1.call-start = ((), (), s32[]{:S(2)}) async-start(), calls=%async_computation.1 | async-start | bytes 9437184 | tf_op jit(solution)/shard_map/all_gather | solution.py:52
  7.9 42.1 %copy-start.1 = (s32[17,2]{0,1:T(2,128)S(1)}, s32[17,2]{0,1:T(2,128)}, u32[]{:S(2)}) copy-start(s32[17,2]{0,1:T(2,128)} %param.3) | copy-start | bytes 412
  143.0 3.4 %copy-start = (bf16[256,2,32,256]{3,2,1,0:T(8,128)(2,1)S(1)}, bf16[256,2,32,256]{3,2,1,0:T(8,128)(2,1)}, u32[]{:S(2)}) copy-start(bf16[256,2,32,256]{3,2,1,0:T(8,128)(2,1)} %all-gather.3.cloned.1.call-done) | copy-start | bytes 25165828
  153.4 28.2 %collective-permute-start = (f32[17,2,64,128]{3,2,1,0:T(8,128)S(1)}, f32[17,2,64,128]{3,2,1,0:T(8,128)S(1)}, u32[]{:S(2)}, u32[]{:S(2)}) collective-permute-start(f32[17,2,64,128]{3,2,1,0:T(8,128)S(1)} %get-tuple-element.8), channel_id=1, source_target_pairs={{0,1},{1,0},{2,3},{3,2},{4,5},{5,4},{6,7},{7,6},{8,9},{9,8},{10,11... | collective-permute-start | bytes 3342344 | tf_op jit(solution)/shard_map/ppermute | solution.py:55
Sparse Core Ops, SparseCore 0:
  50.1 92.9 all-gather.2

commit v2 on v1

v2 whole, which is shorter than its diff:
```python
import jax
import jax.numpy as jnp
from jax import lax
from jax.experimental import pallas as pl
from jax.experimental.pallas import tpu as pltpu
from jax.sharding import PartitionSpec as P

BLOCK = 128
TIME = 2048
CHAINS = (11, 11, 10)
ROUND = [(c * 8 + y, c * 8 + (y + 1 - 2 * (c % 2)) % 8) for c in range(32) for y in range(8)]


def put_kernel(step, *refs):
    pieces, (held, token, arrived) = refs[-3 - len(CHAINS) : -3], refs[-3:]
    token[...] = jnp.zeros_like(token)
    copies, begin = [], 0
    for i, piece in enumerate(pieces):
        copies.append(pltpu.make_async_copy(piece, held.at[step, pl.ds(begin, piece.shape[0])], arrived.at[i]))
        begin += piece.shape[0]
    for copy in copies:
        copy.start()
    for copy in copies:
        copy.wait()


def put(step, held, token, pieces, early=()):
    sources = sum(piece.shape[0] for piece in pieces)
    operands = [*early, *pieces] if held is None else [held, token, *pieces]
    return pl.pallas_call(
        lambda *refs: put_kernel(step, *refs),
        out_shape=(
            jax.ShapeDtypeStruct((8, sources) + pieces[0].shape[1:], jnp.bfloat16),
            jax.ShapeDtypeStruct((8, 128), jnp.float32),
        ),
        in_specs=[pl.BlockSpec(memory_space=pltpu.SMEM)] * len(early)
        + [pl.BlockSpec(memory_space=pl.ANY)] * (len(operands) - len(early)),
        out_specs=(pl.BlockSpec(memory_space=pl.ANY), pl.BlockSpec(memory_space=pltpu.VMEM)),
        scratch_shapes=[pltpu.SemaphoreType.DMA((len(pieces),))],
        input_output_aliases={} if held is None else {0: 0},
        compiler_params=pltpu.CompilerParams(vmem_limit_bytes=2**20),
        cost_estimate=pl.CostEstimate(flops=0, bytes_accessed=2 * 2**20, transcendentals=0),
        name="put",
    )(*operands)


def rings(blocks, early):
    ends = [sum(CHAINS[:i]) for i in range(len(CHAINS) + 1)]
    now = [blocks[i:j] for i, j in zip(ends, ends[1:])]
    held = token = None
    for step in range(7):
        if held is not None:
            now[0], token = lax.optimization_barrier((now[0], token))
        passed = [lax.ppermute(piece, ("chan", "pair"), ROUND) for piece in now]
        (held, token), now = put(step, held, token, now, early if step == 0 else ()), passed
    return put(7, held, token, now)[0]


def tiles_kernel(where, table, held, keep, send, scale, whole):
    half = BLOCK // 2

    def columns(block):
        slot = lax.rem((block // 2 - where[0]) * where[2] + 8, 8)
        lane = pl.ds(pl.multiple_of(block % 2 * BLOCK, BLOCK), BLOCK)
        return jnp.concatenate([held[slot, :, i, :, lane].reshape(-1, BLOCK) for i in range(2)], axis=1)

    def tile(k, carry):
        left, right = columns(table[k, 0]), columns(table[k, 1])
        out = lax.dot_general(left, right, (((0,), (0,)), ((), ())), preferred_element_type=jnp.float32)
        whole[0] = (out[:BLOCK, :BLOCK] + out[BLOCK:, BLOCK:]) * (1.0 / TIME)
        whole[1] = (out[:BLOCK, BLOCK:] - out[BLOCK:, :BLOCK]) * (1.0 / TIME)
        keep[k] = whole[:, pl.ds(pl.multiple_of(where[1] * half, half), half), :]
        other = whole[:, pl.ds(pl.multiple_of((1 - where[1]) * half, half), half), :]
        most = jnp.max(jnp.abs(other), axis=1, keepdims=True)
        scale[k] = (most * (1.0 / 32767.0))[:, 0]
        send[k] = jnp.round(other * jnp.where(most > 0, 32767.0 / most, 0.0)).astype(jnp.int32).astype(jnp.int16)
        return carry

    lax.fori_loop(0, table.shape[0], tile, 0, unroll=True)


def tiles(where, table, held):
    count = table.shape[0]
    smem, vmem = (pl.BlockSpec(memory_space=s) for s in (pltpu.SMEM, pltpu.VMEM))
    part = jax.ShapeDtypeStruct((count, 2, BLOCK // 2, BLOCK), jnp.float32)
    return pl.pallas_call(
        tiles_kernel,
        out_shape=(
            part,
            jax.ShapeDtypeStruct(part.shape, jnp.int16),
            jax.ShapeDtypeStruct((count, 2, BLOCK), jnp.float32),
        ),
        in_specs=[smem, smem, vmem],
        out_specs=(vmem, vmem, vmem),
        scratch_shapes=[pltpu.VMEM((2, BLOCK, BLOCK), jnp.float32)],
        compiler_params=pltpu.CompilerParams(vmem_limit_bytes=4 * 2**20),
        cost_estimate=pl.CostEstimate(flops=count * 2 * 256 * 256 * 1024, bytes_accessed=10 * 2**20, transcendentals=0),
        name="tiles",
    )(where, table, held)


def body(spectra, pair_table):
    way = 2 * (lax.axis_index("chan") % 2) - 1
    where = jnp.stack([lax.axis_index("pair"), lax.axis_index("integ"), way]).astype(jnp.int32)
    turned = lax.all_to_all(spectra.transpose(1, 0, 2, 3), "chan", split_axis=0, concat_axis=0, tiled=True)
    keep, send, scale = tiles(where, pair_table, rings(turned, (where, pair_table)))
    send, scale = (lax.ppermute(half, "integ", [(0, 1), (1, 0)]) for half in (send, scale))
    return (keep + send.astype(jnp.float32) * scale[:, :, None])[:, None]


def solution(mesh):
    in_specs = (P(None, None, ("chan", "integ"), "pair"), P("pair", None))
    out_specs = P("pair", "chan", None, "integ", None)
    return jax.shard_map(body, mesh=mesh, in_specs=in_specs, out_specs=out_specs, check_vma=False)
```

time: 190 us -> 152 us (0.80)
  the two profiles are of different devices: /device:TPU:2 before, /device:TPU:64 now
where the time goes in v2:
time: 152 us; the launch traced here: 151 us
  starting transfers between devices  66.3 us (44%)
  blocking collectives  42.9 us (28%)
  waiting for transfers between devices  29.9 us (20%)
  Pallas kernels  8.36 us (6%)
  local copies, waits for them, and re-layouts  2.15 us (1%)
    ppermute x21, starting transfers between devices, rings(): passed = [lax.ppermute(piece, ('chan', 'pair'), ROUND) for piece in now]  60.5 us
    all_to_all x1, blocking collectives, body(): lax.all_to_all(spectra.transpose(1, 0, 2, 3), 'chan', split_axis=0, conca...  42.9 us
    ppermute x21, waiting for transfers between devices, rings(): passed = [lax.ppermute(piece, ('chan', 'pair'), ROUND) for piece in now]  22.1 us
    ppermute x2, waiting for transfers between devices, body(): lax.ppermute(half, 'integ', [(0, 1), (1, 0)])  7.72 us
    ppermute x2, starting transfers between devices, body(): lax.ppermute(half, 'integ', [(0, 1), (1, 0)])  5.84 us
    pallas_call x8, Pallas kernels, put(): pl.pallas_call(lambda *refs: put_kernel(step, *refs), out_shape=(jax.Shap...  4.72 us
    pallas_call x1, Pallas kernels, tiles(): pl.pallas_call(tiles_kernel, out_shape=(part, jax.ShapeDtypeStruct(part.s...  3.64 us
  transfers between devices with their start and end apart: 23, of which 17 were waited for; matrix products, arithmetic and copies ran while one was open for 1% of the time, Pallas kernels for 2%

profile of v2, /device:TPU:64, one launch (start us, length us, event | category | flops | bytes accessed | tf_op | source)
XLA Modules:
  0.0 151.2 jit_solution(10248467684535652153)
XLA Ops:
  0.0 1.3 copy.15
  1.3 42.9 %all_to_all.5 = bf16[32,2,32,256]{3,2,1,0:T(8,128)(2,1)S(1)} all-to-all(bf16[32,2,32,256]{3,2,1,0:T(8,128)(2,1)S(1)} %bitcast.10), channel_id=1, replica_groups=mesh['chan'=32,'pair'=8,'integ'=2] {'chan'}, dimensions={0} | all-to-all | bytes 2097152 | tf_op jit(solution)/shard_map/all_to_all | solution.py:105
  44.3 3.5 %collective-permute-start = (bf16[11,2,32,256]{3,2,1,0:T(8,128)(2,1)S(1)}, bf16[11,2,32,256]{3,2,1,0:T(8,128)(2,1)S(1)}, u32[]{:S(2)}, u32[]{:S(2)}) collective-permute-start(bf16[11,2,32,256]{3,2,1,0:T(8,128)(2,1)S(1)} %get-tuple-element.66.refs_2_), channel_id=1, source_target_pairs={{0,2},{2,4},{4,6},{6,8},{8,10},{10,12},{12,14},{14,0},{16,30},{18,... | collective-permute-start | bytes 1081352 | tf_op jit(solution)/shard_map/ppermute | solution.py:54
  47.7 3.5 %collective-permute-start.1 = (bf16[11,2,32,256]{3,2,1,0:T(8,128)(2,1)S(1)}, bf16[11,2,32,256]{3,2,1,0:T(8,128)(2,1)S(1)}, u32[]{:S(2)}, u32[]{:S(2)}) collective-permute-start(bf16[11,2,32,256]{3,2,1,0:T(8,128)(2,1)S(1)} %get-tuple-element.65.refs_3_), channel_id=1, source_target_pairs={{0,2},{2,4},{4,6},{6,8},{8,10},{10,12},{12,14},{14,0},{16,30},{18,... | collective-permute-start | bytes 1081352 | tf_op jit(solution)/shard_map/ppermute | solution.py:54
  51.3 3.5 %collective-permute-start.2 = (bf16[10,2,32,256]{3,2,1,0:T(8,128)(2,1)S(1)}, bf16[10,2,32,256]{3,2,1,0:T(8,128)(2,1)S(1)}, u32[]{:S(2)}, u32[]{:S(2)}) collective-permute-start(bf16[10,2,32,256]{3,2,1,0:T(8,128)(2,1)S(1)} %slice.14.refs_4_), channel_id=1, source_target_pairs={{0,2},{2,4},{4,6},{6,8},{8,10},{10,12},{12,14},{14,0},{16,30},{18,... | collective-permute-start | bytes 983048 | tf_op jit(solution)/shard_map/ppermute | solution.py:54
  54.8 0.8 copy.12.refs_1_.table
  55.6 1.2 put.8
  56.8 4.7 %collective-permute-start.3 = (bf16[11,2,32,256]{3,2,1,0:T(8,128)(2,1)S(1)}, bf16[11,2,32,256]{3,2,1,0:T(8,128)(2,1)S(1)}, u32[]{:S(2)}, u32[]{:S(2)}) collective-permute-start(bf16[11,2,32,256]{3,2,1,0:T(8,128)(2,1)S(1)} %collective-permute-done.refs_2_), channel_id=1, source_target_pairs={{0,2},{2,4},{4,6},{6,8},{8,10},{10,12},{12,14},{14,0},{16,30},{18,... | collective-permute-start | bytes 1081352 | tf_op jit(solution)/shard_map/ppermute | solution.py:54
  61.5 2.6 %collective-permute-start.4 = (bf16[11,2,32,256]{3,2,1,0:T(8,128)(2,1)S(1)}, bf16[11,2,32,256]{3,2,1,0:T(8,128)(2,1)S(1)}, u32[]{:S(2)}, u32[]{:S(2)}) collective-permute-start(bf16[11,2,32,256]{3,2,1,0:T(8,128)(2,1)S(1)} %collective-permute-done.1.refs_3_), channel_id=1, source_target_pairs={{0,2},{2,4},{4,6},{6,8},{8,10},{10,12},{12,14},{14,0},{16,30},{18,... | collective-permute-start | bytes 1081352 | tf_op jit(solution)/shard_map/ppermute | solution.py:54
  64.1 2.6 %collective-permute-start.5 = (bf16[10,2,32,256]{3,2,1,0:T(8,128)(2,1)S(1)}, bf16[10,2,32,256]{3,2,1,0:T(8,128)(2,1)S(1)}, u32[]{:S(2)}, u32[]{:S(2)}) collective-permute-start(bf16[10,2,32,256]{3,2,1,0:T(8,128)(2,1)S(1)} %collective-permute-done.2.refs_4_), channel_id=1, source_target_pairs={{0,2},{2,4},{4,6},{6,8},{8,10},{10,12},{12,14},{14,0},{16,30},{18,... | collective-permute-start | bytes 983048 | tf_op jit(solution)/shard_map/ppermute | solution.py:54
  66.7 0.4 put.9
  67.3 3.5 %collective-permute-start.6 = (bf16[11,2,32,256]{3,2,1,0:T(8,128)(2,1)S(1)}, bf16[11,2,32,256]{3,2,1,0:T(8,128)(2,1)S(1)}, u32[]{:S(2)}, u32[]{:S(2)}) collective-permute-start(bf16[11,2,32,256]{3,2,1,0:T(8,128)(2,1)S(1)} %collective-permute-done.3.refs_2_), channel_id=1, source_target_pairs={{0,2},{2,4},{4,6},{6,8},{8,10},{10,12},{12,14},{14,0},{16,30},{18,... | collective-permute-start | bytes 1081352 | tf_op jit(solution)/shard_map/ppermute | solution.py:54
  70.8 1.2 collective-permute-done.4.refs_3_
  72.0 2.6 %collective-permute-start.7 = (bf16[11,2,32,256]{3,2,1,0:T(8,128)(2,1)S(1)}, bf16[11,2,32,256]{3,2,1,0:T(8,128)(2,1)S(1)}, u32[]{:S(2)}, u32[]{:S(2)}) collective-permute-start(bf16[11,2,32,256]{3,2,1,0:T(8,128)(2,1)S(1)} %collective-permute-done.4.refs_3_), channel_id=1, source_target_pairs={{0,2},{2,4},{4,6},{6,8},{8,10},{10,12},{12,14},{14,0},{16,30},{18,... | collective-permute-start | bytes 1081352 | tf_op jit(solution)/shard_map/ppermute | solution.py:54
  74.7 0.9 collective-permute-done.5.refs_4_
  75.6 2.6 %collective-permute-start.8 = (bf16[10,2,32,256]{3,2,1,0:T(8,128)(2,1)S(1)}, bf16[10,2,32,256]{3,2,1,0:T(8,128)(2,1)S(1)}, u32[]{:S(2)}, u32[]{:S(2)}) collective-permute-start(bf16[10,2,32,256]{3,2,1,0:T(8,128)(2,1)S(1)} %collective-permute-done.5.refs_4_), channel_id=1, source_target_pairs={{0,2},{2,4},{4,6},{6,8},{8,10},{10,12},{12,14},{14,0},{16,30},{18,... | collective-permute-start | bytes 983048 | tf_op jit(solution)/shard_map/ppermute | solution.py:54
  78.2 0.4 put.10
  78.6 0.8 collective-permute-done.6.refs_2_
  79.4 2.6 %collective-permute-start.9 = (bf16[11,2,32,256]{3,2,1,0:T(8,128)(2,1)S(1)}, bf16[11,2,32,256]{3,2,1,0:T(8,128)(2,1)S(1)}, u32[]{:S(2)}, u32[]{:S(2)}) collective-permute-start(bf16[11,2,32,256]{3,2,1,0:T(8,128)(2,1)S(1)} %collective-permute-done.6.refs_2_), channel_id=1, source_target_pairs={{0,2},{2,4},{4,6},{6,8},{8,10},{10,12},{12,14},{14,0},{16,30},{18,... | collective-permute-start | bytes 1081352 | tf_op jit(solution)/shard_map/ppermute | solution.py:54
  82.0 1.2 collective-permute-done.7.refs_3_
  83.3 2.6 %collective-permute-start.10 = (bf16[11,2,32,256]{3,2,1,0:T(8,128)(2,1)S(1)}, bf16[11,2,32,256]{3,2,1,0:T(8,128)(2,1)S(1)}, u32[]{:S(2)}, u32[]{:S(2)}) collective-permute-start(bf16[11,2,32,256]{3,2,1,0:T(8,128)(2,1)S(1)} %collective-permute-done.7.refs_3_), channel_id=1, source_target_pairs={{0,2},{2,4},{4,6},{6,8},{8,10},{10,12},{12,14},{14,0},{16,30},{18,... | collective-permute-start | bytes 1081352 | tf_op jit(solution)/shard_map/ppermute | solution.py:54
  85.9 0.9 collective-permute-done.8.refs_4_
  86.8 2.6 %collective-permute-start.11 = (bf16[10,2,32,256]{3,2,1,0:T(8,128)(2,1)S(1)}, bf16[10,2,32,256]{3,2,1,0:T(8,128)(2,1)S(1)}, u32[]{:S(2)}, u32[]{:S(2)}) collective-permute-start(bf16[10,2,32,256]{3,2,1,0:T(8,128)(2,1)S(1)} %collective-permute-done.8.refs_4_), channel_id=1, source_target_pairs={{0,2},{2,4},{4,6},{6,8},{8,10},{10,12},{12,14},{14,0},{16,30},{18,... | collective-permute-start | bytes 983048 | tf_op jit(solution)/shard_map/ppermute | solution.py:54
  89.9 0.8 collective-permute-done.9.refs_2_
  90.7 2.6 %collective-permute-start.12 = (bf16[11,2,32,256]{3,2,1,0:T(8,128)(2,1)S(1)}, bf16[11,2,32,256]{3,2,1,0:T(8,128)(2,1)S(1)}, u32[]{:S(2)}, u32[]{:S(2)}) collective-permute-start(bf16[11,2,32,256]{3,2,1,0:T(8,128)(2,1)S(1)} %collective-permute-done.9.refs_2_), channel_id=1, source_target_pairs={{0,2},{2,4},{4,6},{6,8},{8,10},{10,12},{12,14},{14,0},{16,30},{18,... | collective-permute-start | bytes 1081352 | tf_op jit(solution)/shard_map/ppermute | solution.py:54
  93.3 1.2 collective-permute-done.10.refs_3_
  94.5 2.6 %collective-permute-start.13 = (bf16[11,2,32,256]{3,2,1,0:T(8,128)(2,1)S(1)}, bf16[11,2,32,256]{3,2,1,0:T(8,128)(2,1)S(1)}, u32[]{:S(2)}, u32[]{:S(2)}) collective-permute-start(bf16[11,2,32,256]{3,2,1,0:T(8,128)(2,1)S(1)} %collective-permute-done.10.refs_3_), channel_id=1, source_target_pairs={{0,2},{2,4},{4,6},{6,8},{8,10},{10,12},{12,14},{14,0},{16,30},{18,... | collective-permute-start | bytes 1081352 | tf_op jit(solution)/shard_map/ppermute | solution.py:54
  97.1 0.9 collective-permute-done.11.refs_4_
  98.0 2.6 %collective-permute-start.14 = (bf16[10,2,32,256]{3,2,1,0:T(8,128)(2,1)S(1)}, bf16[10,2,32,256]{3,2,1,0:T(8,128)(2,1)S(1)}, u32[]{:S(2)}, u32[]{:S(2)}) collective-permute-start(bf16[10,2,32,256]{3,2,1,0:T(8,128)(2,1)S(1)} %collective-permute-done.11.refs_4_), channel_id=1, source_target_pairs={{0,2},{2,4},{4,6},{6,8},{8,10},{10,12},{12,14},{14,0},{16,30},{18,... | collective-permute-start | bytes 983048 | tf_op jit(solution)/shard_map/ppermute | solution.py:54
  101.1 0.8 collective-permute-done.12.refs_2_
  101.9 2.6 %collective-permute-start.15 = (bf16[11,2,32,256]{3,2,1,0:T(8,128)(2,1)S(1)}, bf16[11,2,32,256]{3,2,1,0:T(8,128)(2,1)S(1)}, u32[]{:S(2)}, u32[]{:S(2)}) collective-permute-start(bf16[11,2,32,256]{3,2,1,0:T(8,128)(2,1)S(1)} %collective-permute-done.12.refs_2_), channel_id=1, source_target_pairs={{0,2},{2,4},{4,6},{6,8},{8,10},{10,12},{12,14},{14,0},{16,30},{18,... | collective-permute-start | bytes 1081352 | tf_op jit(solution)/shard_map/ppermute | solution.py:54
  104.5 1.2 collective-permute-done.13.refs_3_
  105.8 2.6 %collective-permute-start.16 = (bf16[11,2,32,256]{3,2,1,0:T(8,128)(2,1)S(1)}, bf16[11,2,32,256]{3,2,1,0:T(8,128)(2,1)S(1)}, u32[]{:S(2)}, u32[]{:S(2)}) collective-permute-start(bf16[11,2,32,256]{3,2,1,0:T(8,128)(2,1)S(1)} %collective-permute-done.13.refs_3_), channel_id=1, source_target_pairs={{0,2},{2,4},{4,6},{6,8},{8,10},{10,12},{12,14},{14,0},{16,30},{18,... | collective-permute-start | bytes 1081352 | tf_op jit(solution)/shard_map/ppermute | solution.py:54
  108.4 0.9 collective-permute-done.14.refs_4_
  109.3 2.6 %collective-permute-start.17 = (bf16[10,2,32,256]{3,2,1,0:T(8,128)(2,1)S(1)}, bf16[10,2,32,256]{3,2,1,0:T(8,128)(2,1)S(1)}, u32[]{:S(2)}, u32[]{:S(2)}) collective-permute-start(bf16[10,2,32,256]{3,2,1,0:T(8,128)(2,1)S(1)} %collective-permute-done.14.refs_4_), channel_id=1, source_target_pairs={{0,2},{2,4},{4,6},{6,8},{8,10},{10,12},{12,14},{14,0},{16,30},{18,... | collective-permute-start | bytes 983048 | tf_op jit(solution)/shard_map/ppermute | solution.py:54
  112.3 0.8 collective-permute-done.15.refs_2_
  113.1 2.6 %collective-permute-start.18 = (bf16[11,2,32,256]{3,2,1,0:T(8,128)(2,1)S(1)}, bf16[11,2,32,256]{3,2,1,0:T(8,128)(2,1)S(1)}, u32[]{:S(2)}, u32[]{:S(2)}) collective-permute-start(bf16[11,2,32,256]{3,2,1,0:T(8,128)(2,1)S(1)} %collective-permute-done.15.refs_2_), channel_id=1, source_target_pairs={{0,2},{2,4},{4,6},{6,8},{8,10},{10,12},{12,14},{14,0},{16,30},{18,... | collective-permute-start | bytes 1081352 | tf_op jit(solution)/shard_map/ppermute | solution.py:54
  115.8 1.2 collective-permute-done.16.refs_3_
  117.0 2.6 %collective-permute-start.19 = (bf16[11,2,32,256]{3,2,1,0:T(8,128)(2,1)S(1)}, bf16[11,2,32,256]{3,2,1,0:T(8,128)(2,1)S(1)}, u32[]{:S(2)}, u32[]{:S(2)}) collective-permute-start(bf16[11,2,32,256]{3,2,1,0:T(8,128)(2,1)S(1)} %collective-permute-done.16.refs_3_), channel_id=1, source_target_pairs={{0,2},{2,4},{4,6},{6,8},{8,10},{10,12},{12,14},{14,0},{16,30},{18,... | collective-permute-start | bytes 1081352 | tf_op jit(solution)/shard_map/ppermute | solution.py:54
  119.6 0.9 collective-permute-done.17.refs_4_
  120.5 2.6 %collective-permute-start.20 = (bf16[10,2,32,256]{3,2,1,0:T(8,128)(2,1)S(1)}, bf16[10,2,32,256]{3,2,1,0:T(8,128)(2,1)S(1)}, u32[]{:S(2)}, u32[]{:S(2)}) collective-permute-start(bf16[10,2,32,256]{3,2,1,0:T(8,128)(2,1)S(1)} %collective-permute-done.17.refs_4_), channel_id=1, source_target_pairs={{0,2},{2,4},{4,6},{6,8},{8,10},{10,12},{12,14},{14,0},{16,30},{18,... | collective-permute-start | bytes 983048 | tf_op jit(solution)/shard_map/ppermute | solution.py:54
  123.6 8.2 %collective-permute-done.20.refs_4_ = bf16[10,2,32,256]{3,2,1,0:T(8,128)(2,1)S(1)} collective-permute-done((bf16[10,2,32,256]{3,2,1,0:T(8,128)(2,1)S(1)}, bf16[10,2,32,256]{3,2,1,0:T(8,128)(2,1)S(1)}, u32[]{:S(2)}, u32[]{:S(2)}) %collective-permute-start.20) | collective-permute-done | bytes 327712 | tf_op jit(solution)/shard_map/ppermute | solution.py:54
  131.7 1.0 put.15
  132.8 3.6 %tiles.1 = (f32[17,2,64,128]{3,2,1,0:T(8,128)S(1)}, s16[17,2,64,128]{3,2,1,0:T(8,128)(2,1)S(1)}, f32[17,2,128]{2,1,0:T(2,128)S(1)}) custom-call(s32[3]{0:T(128)S(1)} %pad_add_fusion.refs_0_.where, s32[17,2]{1,0:T(8,128)S(1)} %copy.12.refs_1_.table, bf16[8,32,2,32,256]{4,3,2,1,0:T(8,128)(2,1)S(1)} %get-tuple-element.61.held), custom_call_target="tpu_custom_call" | custom-call | flops 2281701376 | bytes 10485760 | tf_op jit(solution)/shard_map/tiles/pallas_call | solution.py:86
  136.4 2.5 %collective-permute-start.21 = (s16[17,2,64,128]{3,2,1,0:T(8,128)(2,1)S(1)}, s16[17,2,64,128]{3,2,1,0:T(8,128)(2,1)S(1)}, u32[]{:S(2)}, u32[]{:S(2)}) collective-permute-start(s16[17,2,64,128]{3,2,1,0:T(8,128)(2,1)S(1)} %get-tuple-element.63), channel_id=1, source_target_pairs={{0,1},{1,0},{2,3},{3,2},{4,5},{5,4},{6,7},{7,6},{8,9},{9,8},{10,11... | collective-permute-start | bytes 1671176 | tf_op jit(solution)/shard_map/ppermute | solution.py:107
  138.9 3.3 %collective-permute-start.22 = (f32[17,2,128]{2,1,0:T(2,128)S(1)}, f32[17,2,128]{2,1,0:T(2,128)S(1)}, u32[]{:S(2)}, u32[]{:S(2)}) collective-permute-start(f32[17,2,128]{2,1,0:T(2,128)S(1)} %get-tuple-element.64), channel_id=1, source_target_pairs={{0,1},{1,0},{2,3},{3,2},{4,5},{5,4},{6,7},{7,6},{8,9},{9,8},{10,11... | collective-permute-start | bytes 52232 | tf_op jit(solution)/shard_map/ppermute | solution.py:107
  142.3 7.7 %collective-permute-done.22 = f32[17,2,128]{2,1,0:T(2,128)S(1)} collective-permute-done((f32[17,2,128]{2,1,0:T(2,128)S(1)}, f32[17,2,128]{2,1,0:T(2,128)S(1)}, u32[]{:S(2)}, u32[]{:S(2)}) %collective-permute-start.22) | collective-permute-done | bytes 17440 | tf_op jit(solution)/shard_map/ppermute | solution.py:107
  150.0 1.2 add_bitcast_fusion
  (14 shorter events, 2.0 us)
Async XLA Ops:
  44.3 12.5 %collective-permute-start = (bf16[11,2,32,256]{3,2,1,0:T(8,128)(2,1)S(1)}, bf16[11,2,32,256]{3,2,1,0:T(8,128)(2,1)S(1)}, u32[]{:S(2)}, u32[]{:S(2)}) collective-permute-start(bf16[11,2,32,256]{3,2,1,0:T(8,128)(2,1)S(1)} %get-tuple-element.66.refs_2_), channel_id=1, source_target_pairs={{0,2},{2,4},{4,6},{6,8},{8,10},{10,12},{12,14},{14,0},{16,30},{18,... | collective-permute-start | bytes 1081352 | tf_op jit(solution)/shard_map/ppermute | solution.py:54
  47.7 13.8 %collective-permute-start.1 = (bf16[11,2,32,256]{3,2,1,0:T(8,128)(2,1)S(1)}, bf16[11,2,32,256]{3,2,1,0:T(8,128)(2,1)S(1)}, u32[]{:S(2)}, u32[]{:S(2)}) collective-permute-start(bf16[11,2,32,256]{3,2,1,0:T(8,128)(2,1)S(1)} %get-tuple-element.65.refs_3_), channel_id=1, source_target_pairs={{0,2},{2,4},{4,6},{6,8},{8,10},{10,12},{12,14},{14,0},{16,30},{18,... | collective-permute-start | bytes 1081352 | tf_op jit(solution)/shard_map/ppermute | solution.py:54
  51.3 12.8 %collective-permute-start.2 = (bf16[10,2,32,256]{3,2,1,0:T(8,128)(2,1)S(1)}, bf16[10,2,32,256]{3,2,1,0:T(8,128)(2,1)S(1)}, u32[]{:S(2)}, u32[]{:S(2)}) collective-permute-start(bf16[10,2,32,256]{3,2,1,0:T(8,128)(2,1)S(1)} %slice.14.refs_4_), channel_id=1, source_target_pairs={{0,2},{2,4},{4,6},{6,8},{8,10},{10,12},{12,14},{14,0},{16,30},{18,... | collective-permute-start | bytes 983048 | tf_op jit(solution)/shard_map/ppermute | solution.py:54
  56.8 10.5 %collective-permute-start.3 = (bf16[11,2,32,256]{3,2,1,0:T(8,128)(2,1)S(1)}, bf16[11,2,32,256]{3,2,1,0:T(8,128)(2,1)S(1)}, u32[]{:S(2)}, u32[]{:S(2)}) collective-permute-start(bf16[11,2,32,256]{3,2,1,0:T(8,128)(2,1)S(1)} %collective-permute-done.refs_2_), channel_id=1, source_target_pairs={{0,2},{2,4},{4,6},{6,8},{8,10},{10,12},{12,14},{14,0},{16,30},{18,... | collective-permute-start | bytes 1081352 | tf_op jit(solution)/shard_map/ppermute | solution.py:54
  61.5 10.5 %collective-permute-start.4 = (bf16[11,2,32,256]{3,2,1,0:T(8,128)(2,1)S(1)}, bf16[11,2,32,256]{3,2,1,0:T(8,128)(2,1)S(1)}, u32[]{:S(2)}, u32[]{:S(2)}) collective-permute-start(bf16[11,2,32,256]{3,2,1,0:T(8,128)(2,1)S(1)} %collective-permute-done.1.refs_3_), channel_id=1, source_target_pairs={{0,2},{2,4},{4,6},{6,8},{8,10},{10,12},{12,14},{14,0},{16,30},{18,... | collective-permute-start | bytes 1081352 | tf_op jit(solution)/shard_map/ppermute | solution.py:54
  64.1 11.4 %collective-permute-start.5 = (bf16[10,2,32,256]{3,2,1,0:T(8,128)(2,1)S(1)}, bf16[10,2,32,256]{3,2,1,0:T(8,128)(2,1)S(1)}, u32[]{:S(2)}, u32[]{:S(2)}) collective-permute-start(bf16[10,2,32,256]{3,2,1,0:T(8,128)(2,1)S(1)} %collective-permute-done.2.refs_4_), channel_id=1, source_target_pairs={{0,2},{2,4},{4,6},{6,8},{8,10},{10,12},{12,14},{14,0},{16,30},{18,... | collective-permute-start | bytes 983048 | tf_op jit(solution)/shard_map/ppermute | solution.py:54
  67.3 12.1 %collective-permute-start.6 = (bf16[11,2,32,256]{3,2,1,0:T(8,128)(2,1)S(1)}, bf16[11,2,32,256]{3,2,1,0:T(8,128)(2,1)S(1)}, u32[]{:S(2)}, u32[]{:S(2)}) collective-permute-start(bf16[11,2,32,256]{3,2,1,0:T(8,128)(2,1)S(1)} %collective-permute-done.3.refs_2_), channel_id=1, source_target_pairs={{0,2},{2,4},{4,6},{6,8},{8,10},{10,12},{12,14},{14,0},{16,30},{18,... | collective-permute-start | bytes 1081352 | tf_op jit(solution)/shard_map/ppermute | solution.py:54
  72.0 11.2 %collective-permute-start.7 = (bf16[11,2,32,256]{3,2,1,0:T(8,128)(2,1)S(1)}, bf16[11,2,32,256]{3,2,1,0:T(8,128)(2,1)S(1)}, u32[]{:S(2)}, u32[]{:S(2)}) collective-permute-start(bf16[11,2,32,256]{3,2,1,0:T(8,128)(2,1)S(1)} %collective-permute-done.4.refs_3_), channel_id=1, source_target_pairs={{0,2},{2,4},{4,6},{6,8},{8,10},{10,12},{12,14},{14,0},{16,30},{18,... | collective-permute-start | bytes 1081352 | tf_op jit(solution)/shard_map/ppermute | solution.py:54
  75.6 11.2 %collective-permute-start.8 = (bf16[10,2,32,256]{3,2,1,0:T(8,128)(2,1)S(1)}, bf16[10,2,32,256]{3,2,1,0:T(8,128)(2,1)S(1)}, u32[]{:S(2)}, u32[]{:S(2)}) collective-permute-start(bf16[10,2,32,256]{3,2,1,0:T(8,128)(2,1)S(1)} %collective-permute-done.5.refs_4_), channel_id=1, source_target_pairs={{0,2},{2,4},{4,6},{6,8},{8,10},{10,12},{12,14},{14,0},{16,30},{18,... | collective-permute-start | bytes 983048 | tf_op jit(solution)/shard_map/ppermute | solution.py:54
  79.4 11.2 %collective-permute-start.9 = (bf16[11,2,32,256]{3,2,1,0:T(8,128)(2,1)S(1)}, bf16[11,2,32,256]{3,2,1,0:T(8,128)(2,1)S(1)}, u32[]{:S(2)}, u32[]{:S(2)}) collective-permute-start(bf16[11,2,32,256]{3,2,1,0:T(8,128)(2,1)S(1)} %collective-permute-done.6.refs_2_), channel_id=1, source_target_pairs={{0,2},{2,4},{4,6},{6,8},{8,10},{10,12},{12,14},{14,0},{16,30},{18,... | collective-permute-start | bytes 1081352 | tf_op jit(solution)/shard_map/ppermute | solution.py:54
  83.3 11.2 %collective-permute-start.10 = (bf16[11,2,32,256]{3,2,1,0:T(8,128)(2,1)S(1)}, bf16[11,2,32,256]{3,2,1,0:T(8,128)(2,1)S(1)}, u32[]{:S(2)}, u32[]{:S(2)}) collective-permute-start(bf16[11,2,32,256]{3,2,1,0:T(8,128)(2,1)S(1)} %collective-permute-done.7.refs_3_), channel_id=1, source_target_pairs={{0,2},{2,4},{4,6},{6,8},{8,10},{10,12},{12,14},{14,0},{16,30},{18,... | collective-permute-start | bytes 1081352 | tf_op jit(solution)/shard_map/ppermute | solution.py:54
  86.8 11.2 %collective-permute-start.11 = (bf16[10,2,32,256]{3,2,1,0:T(8,128)(2,1)S(1)}, bf16[10,2,32,256]{3,2,1,0:T(8,128)(2,1)S(1)}, u32[]{:S(2)}, u32[]{:S(2)}) collective-permute-start(bf16[10,2,32,256]{3,2,1,0:T(8,128)(2,1)S(1)} %collective-permute-done.8.refs_4_), channel_id=1, source_target_pairs={{0,2},{2,4},{4,6},{6,8},{8,10},{10,12},{12,14},{14,0},{16,30},{18,... | collective-permute-start | bytes 983048 | tf_op jit(solution)/shard_map/ppermute | solution.py:54
  90.7 11.2 %collective-permute-start.12 = (bf16[11,2,32,256]{3,2,1,0:T(8,128)(2,1)S(1)}, bf16[11,2,32,256]{3,2,1,0:T(8,128)(2,1)S(1)}, u32[]{:S(2)}, u32[]{:S(2)}) collective-permute-start(bf16[11,2,32,256]{3,2,1,0:T(8,128)(2,1)S(1)} %collective-permute-done.9.refs_2_), channel_id=1, source_target_pairs={{0,2},{2,4},{4,6},{6,8},{8,10},{10,12},{12,14},{14,0},{16,30},{18,... | collective-permute-start | bytes 1081352 | tf_op jit(solution)/shard_map/ppermute | solution.py:54
  94.5 11.2 %collective-permute-start.13 = (bf16[11,2,32,256]{3,2,1,0:T(8,128)(2,1)S(1)}, bf16[11,2,32,256]{3,2,1,0:T(8,128)(2,1)S(1)}, u32[]{:S(2)}, u32[]{:S(2)}) collective-permute-start(bf16[11,2,32,256]{3,2,1,0:T(8,128)(2,1)S(1)} %collective-permute-done.10.refs_3_), channel_id=1, source_target_pairs={{0,2},{2,4},{4,6},{6,8},{8,10},{10,12},{12,14},{14,0},{16,30},{18,... | collective-permute-start | bytes 1081352 | tf_op jit(solution)/shard_map/ppermute | solution.py:54
  98.0 11.2 %collective-permute-start.14 = (bf16[10,2,32,256]{3,2,1,0:T(8,128)(2,1)S(1)}, bf16[10,2,32,256]{3,2,1,0:T(8,128)(2,1)S(1)}, u32[]{:S(2)}, u32[]{:S(2)}) collective-permute-start(bf16[10,2,32,256]{3,2,1,0:T(8,128)(2,1)S(1)} %collective-permute-done.11.refs_4_), channel_id=1, source_target_pairs={{0,2},{2,4},{4,6},{6,8},{8,10},{10,12},{12,14},{14,0},{16,30},{18,... | collective-permute-start | bytes 983048 | tf_op jit(solution)/shard_map/ppermute | solution.py:54
  101.9 11.2 %collective-permute-start.15 = (bf16[11,2,32,256]{3,2,1,0:T(8,128)(2,1)S(1)}, bf16[11,2,32,256]{3,2,1,0:T(8,128)(2,1)S(1)}, u32[]{:S(2)}, u32[]{:S(2)}) collective-permute-start(bf16[11,2,32,256]{3,2,1,0:T(8,128)(2,1)S(1)} %collective-permute-done.12.refs_2_), channel_id=1, source_target_pairs={{0,2},{2,4},{4,6},{6,8},{8,10},{10,12},{12,14},{14,0},{16,30},{18,... | collective-permute-start | bytes 1081352 | tf_op jit(solution)/shard_map/ppermute | solution.py:54
  105.8 11.2 %collective-permute-start.16 = (bf16[11,2,32,256]{3,2,1,0:T(8,128)(2,1)S(1)}, bf16[11,2,32,256]{3,2,1,0:T(8,128)(2,1)S(1)}, u32[]{:S(2)}, u32[]{:S(2)}) collective-permute-start(bf16[11,2,32,256]{3,2,1,0:T(8,128)(2,1)S(1)} %collective-permute-done.13.refs_3_), channel_id=1, source_target_pairs={{0,2},{2,4},{4,6},{6,8},{8,10},{10,12},{12,14},{14,0},{16,30},{18,... | collective-permute-start | bytes 1081352 | tf_op jit(solution)/shard_map/ppermute | solution.py:54
  109.3 11.2 %collective-permute-start.17 = (bf16[10,2,32,256]{3,2,1,0:T(8,128)(2,1)S(1)}, bf16[10,2,32,256]{3,2,1,0:T(8,128)(2,1)S(1)}, u32[]{:S(2)}, u32[]{:S(2)}) collective-permute-start(bf16[10,2,32,256]{3,2,1,0:T(8,128)(2,1)S(1)} %collective-permute-done.14.refs_4_), channel_id=1, source_target_pairs={{0,2},{2,4},{4,6},{6,8},{8,10},{10,12},{12,14},{14,0},{16,30},{18,... | collective-permute-start | bytes 983048 | tf_op jit(solution)/shard_map/ppermute | solution.py:54
  113.1 18.6 %collective-permute-start.18 = (bf16[11,2,32,256]{3,2,1,0:T(8,128)(2,1)S(1)}, bf16[11,2,32,256]{3,2,1,0:T(8,128)(2,1)S(1)}, u32[]{:S(2)}, u32[]{:S(2)}) collective-permute-start(bf16[11,2,32,256]{3,2,1,0:T(8,128)(2,1)S(1)} %collective-permute-done.15.refs_2_), channel_id=1, source_target_pairs={{0,2},{2,4},{4,6},{6,8},{8,10},{10,12},{12,14},{14,0},{16,30},{18,... | collective-permute-start | bytes 1081352 | tf_op jit(solution)/shard_map/ppermute | solution.py:54
  117.0 14.8 %collective-permute-start.19 = (bf16[11,2,32,256]{3,2,1,0:T(8,128)(2,1)S(1)}, bf16[11,2,32,256]{3,2,1,0:T(8,128)(2,1)S(1)}, u32[]{:S(2)}, u32[]{:S(2)}) collective-permute-start(bf16[11,2,32,256]{3,2,1,0:T(8,128)(2,1)S(1)} %collective-permute-done.16.refs_3_), channel_id=1, source_target_pairs={{0,2},{2,4},{4,6},{6,8},{8,10},{10,12},{12,14},{14,0},{16,30},{18,... | collective-permute-start | bytes 1081352 | tf_op jit(solution)/shard_map/ppermute | solution.py:54
  120.5 11.2 %collective-permute-start.20 = (bf16[10,2,32,256]{3,2,1,0:T(8,128)(2,1)S(1)}, bf16[10,2,32,256]{3,2,1,0:T(8,128)(2,1)S(1)}, u32[]{:S(2)}, u32[]{:S(2)}) collective-permute-start(bf16[10,2,32,256]{3,2,1,0:T(8,128)(2,1)S(1)} %collective-permute-done.17.refs_4_), channel_id=1, source_target_pairs={{0,2},{2,4},{4,6},{6,8},{8,10},{10,12},{12,14},{14,0},{16,30},{18,... | collective-permute-start | bytes 983048 | tf_op jit(solution)/shard_map/ppermute | solution.py:54
  136.4 13.6 %collective-permute-start.21 = (s16[17,2,64,128]{3,2,1,0:T(8,128)(2,1)S(1)}, s16[17,2,64,128]{3,2,1,0:T(8,128)(2,1)S(1)}, u32[]{:S(2)}, u32[]{:S(2)}) collective-permute-start(s16[17,2,64,128]{3,2,1,0:T(8,128)(2,1)S(1)} %get-tuple-element.63), channel_id=1, source_target_pairs={{0,1},{1,0},{2,3},{3,2},{4,5},{5,4},{6,7},{7,6},{8,9},{9,8},{10,11... | collective-permute-start | bytes 1671176 | tf_op jit(solution)/shard_map/ppermute | solution.py:107
  138.9 11.1 %collective-permute-start.22 = (f32[17,2,128]{2,1,0:T(2,128)S(1)}, f32[17,2,128]{2,1,0:T(2,128)S(1)}, u32[]{:S(2)}, u32[]{:S(2)}) collective-permute-start(f32[17,2,128]{2,1,0:T(2,128)S(1)} %get-tuple-element.64), channel_id=1, source_target_pairs={{0,1},{1,0},{2,3},{3,2},{4,5},{5,4},{6,7},{7,6},{8,9},{9,8},{10,11... | collective-permute-start | bytes 52232 | tf_op jit(solution)/shard_map/ppermute | solution.py:107

commit v3 on v2

v3 whole, which is shorter than its diff:
```python
import jax
import jax.numpy as jnp
from jax import lax
from jax.experimental import pallas as pl
from jax.experimental.pallas import tpu as pltpu
from jax.sharding import PartitionSpec as P

BLOCK = 128
TIME = 2048
CHAINS = (11, 11, 10)
ROUND = [(c * 8 + y, c * 8 + (y + 1 - 2 * (c % 2)) % 8) for c in range(32) for y in range(8)]


def lay(step, pieces, held, arrived):
    copies, begin = [], 0
    for i, piece in enumerate(pieces):
        copies.append(pltpu.make_async_copy(piece, held.at[step, pl.ds(begin, piece.shape[0])], arrived.at[i]))
        begin += piece.shape[0]
    return copies


def run(copies):
    for copy in copies:
        copy.start()
    for copy in copies:
        copy.wait()


def put_kernel(steps, *refs):
    count = len(steps) * len(CHAINS)
    pieces, (held, token, arrived) = refs[-3 - count : -3], refs[-3:]
    token[...] = jnp.zeros_like(token)
    copies = []
    for i, step in enumerate(steps):
        here = pl.ds(len(CHAINS) * i, len(CHAINS))
        copies += lay(step, pieces[len(CHAINS) * i : len(CHAINS) * (i + 1)], held, arrived.at[here])
    run(copies)


def put(steps, held, token, pieces):
    sources = sum(piece.shape[0] for piece in pieces[: len(CHAINS)])
    operands = list(pieces) if held is None else [held, token, *pieces]
    return pl.pallas_call(
        lambda *refs: put_kernel(steps, *refs),
        out_shape=(
            jax.ShapeDtypeStruct((8, sources) + pieces[0].shape[1:], jnp.bfloat16),
            jax.ShapeDtypeStruct((8, 128), jnp.float32),
        ),
        in_specs=[pl.BlockSpec(memory_space=pl.ANY)] * len(operands),
        out_specs=(pl.BlockSpec(memory_space=pl.ANY), pl.BlockSpec(memory_space=pltpu.VMEM)),
        scratch_shapes=[pltpu.SemaphoreType.DMA((len(pieces),))],
        input_output_aliases={} if held is None else {0: 0},
        compiler_params=pltpu.CompilerParams(vmem_limit_bytes=2**20),
        cost_estimate=pl.CostEstimate(flops=0, bytes_accessed=2 * 2**20, transcendentals=0),
        name="put",
    )(*operands)


def rings(blocks):
    ends = [sum(CHAINS[:i]) for i in range(len(CHAINS) + 1)]
    now = [blocks[i:j] for i, j in zip(ends, ends[1:])]
    held = token = None
    first = now
    for step in range(7):
        if held is not None:
            now[0], token = lax.optimization_barrier((now[0], token))
        passed = [lax.ppermute(piece, ("chan", "pair"), ROUND) for piece in now]
        if step == 1:
            held, token = put((0, 1), None, None, first + now)
        elif step > 1:
            held, token = put((step,), held, token, now)
        now = passed
    return held, now


def products(where, table, held, sources, k):
    def columns(block):
        slot = lax.rem((block // 2 - where[0]) * where[2] + 8, 8)
        lane = pl.ds(pl.multiple_of(block % 2 * BLOCK, BLOCK), BLOCK)
        return jnp.concatenate([held[slot, sources, i, :, lane].reshape(-1, BLOCK) for i in range(2)], axis=1)

    left, right = columns(table[0, k]), columns(table[1, k])
    out = lax.dot_general(left, right, (((0,), (0,)), ((), ())), preferred_element_type=jnp.float32)
    return out[:BLOCK, :BLOCK] + out[BLOCK:, BLOCK:], out[:BLOCK, BLOCK:] - out[BLOCK:, :BLOCK]


def most_kernel(where, table, *refs):
    last, (held, total, arrived) = refs[1:-3], refs[-3:]
    run(lay(7, last, held, arrived))
    sources = pl.ds(0, sum(CHAINS[:-1]))

    def tile(k, carry):
        total[k, 0], total[k, 1] = products(where, table, held, sources, k)
        return carry

    lax.fori_loop(0, table.shape[1], tile, 0, unroll=True)


def rest_kernel(where, table, _, total, last, held, keep, send, scale, whole, arrived):
    half = BLOCK // 2
    sources = pl.ds(sum(CHAINS[:-1]), CHAINS[-1])
    run([pltpu.make_async_copy(last, held.at[7, sources], arrived)])

    def tile(k, carry):
        real, imag = products(where, table, held, sources, k)
        whole[0] = (total[k, 0] + real) * (1.0 / TIME)
        whole[1] = (total[k, 1] + imag) * (1.0 / TIME)
        keep[k] = whole[:, pl.ds(pl.multiple_of(where[1] * half, half), half), :]
        other = whole[:, pl.ds(pl.multiple_of((1 - where[1]) * half, half), half), :]
        most = jnp.max(jnp.abs(other), axis=1, keepdims=True)
        scale[k] = (most * (1.0 / 32767.0))[:, 0]
        send[k] = jnp.round(other * jnp.where(most > 0, 32767.0 / most, 0.0)).astype(jnp.int32).astype(jnp.int16)
        return carry

    lax.fori_loop(0, table.shape[1], tile, 0, unroll=True)


def tiles(where, table, held, last):
    count = table.shape[1]
    smem, vmem, any_ = (pl.BlockSpec(memory_space=s) for s in (pltpu.SMEM, pltpu.VMEM, pl.ANY))
    blocks = jax.ShapeDtypeStruct(held.shape, held.dtype)
    options = dict(
        compiler_params=pltpu.CompilerParams(vmem_limit_bytes=4 * 2**20),
        cost_estimate=pl.CostEstimate(flops=count * 256 * 256 * 1024, bytes_accessed=10 * 2**20, transcendentals=0),
        input_output_aliases={2: 0},
    )
    held, total = pl.pallas_call(
        most_kernel,
        out_shape=(blocks, jax.ShapeDtypeStruct((count, 2, BLOCK, BLOCK), jnp.float32)),
        in_specs=[smem, smem, vmem] + [any_] * (len(last) - 1),
        out_specs=(vmem, vmem),
        scratch_shapes=[pltpu.SemaphoreType.DMA((len(last) - 1,))],
        name="most",
        **options,
    )(where, table, held, *last[:-1])
    part = jax.ShapeDtypeStruct((count, 2, BLOCK // 2, BLOCK), jnp.float32)
    return pl.pallas_call(
        rest_kernel,
        out_shape=(
            blocks,
            part,
            jax.ShapeDtypeStruct(part.shape, jnp.int16),
            jax.ShapeDtypeStruct((count, 2, BLOCK), jnp.float32),
        ),
        in_specs=[smem, smem, vmem, vmem, any_],
        out_specs=(vmem, vmem, vmem, vmem),
        scratch_shapes=[pltpu.VMEM((2, BLOCK, BLOCK), jnp.float32), pltpu.SemaphoreType.DMA],
        name="rest",
        **options,
    )(where, table, held, total, last[-1])


def body(spectra, pair_table):
    way = 2 * (lax.axis_index("chan") % 2) - 1
    where = jnp.stack([lax.axis_index("pair"), lax.axis_index("integ"), way]).astype(jnp.int32)
    ordered, where, table = lax.optimization_barrier((spectra.transpose(1, 0, 2, 3), where, pair_table.T))
    turned = lax.all_to_all(ordered, "chan", split_axis=0, concat_axis=0, tiled=True)
    _, keep, send, scale = tiles(where, table, *rings(turned))
    send, scale = (lax.ppermute(half, "integ", [(0, 1), (1, 0)]) for half in (send, scale))
    return (keep + send.astype(jnp.float32) * scale[:, :, None])[:, None]


def solution(mesh):
    in_specs = (P(None, None, ("chan", "integ"), "pair"), P("pair", None))
    out_specs = P("pair", "chan", None, "integ", None)
    return jax.shard_map(body, mesh=mesh, in_specs=in_specs, out_specs=out_specs, check_vma=False)
```

time: 152 us -> 149 us (0.980)
  waiting for transfers between devices: 29.9 us -> 13.8 us
  starting transfers between devices: 66.3 us -> 79.6 us
    ppermute x21, waiting for transfers between devices: 22.1 us -> 5.27 us  [rings(): passed = [lax.ppermute(piece, ('chan', 'pair'), ROUND) for piece in now]]
    ppermute x21, starting transfers between devices: 60.5 us -> 73.8 us  [rings(): passed = [lax.ppermute(piece, ('chan', 'pair'), ROUND) for piece in now]]
    pallas_call x9 -> x8, Pallas kernels: 8.36 us -> 8.82 us  [the longest x6 3.56 us: put(): pl.pallas_call(lambda *refs: put_kernel(steps, *refs), out_shape=(jax.Sha...]
  transfers between devices with their start and end apart: 23 -> 23, of which waited for: 17 -> 9; matrix products, arithmetic and copies ran while one was open for 1% -> 0% of each run, Pallas kernels for 2% -> 4%
where the time goes in v3:
time: 149 us; the launch traced here: 148 us
  starting transfers between devices  79.6 us (53%)
  blocking collectives  42.9 us (29%)
  waiting for transfers between devices  13.8 us (9%)
  Pallas kernels  8.82 us (6%)
    ppermute x21, starting transfers between devices, rings(): passed = [lax.ppermute(piece, ('chan', 'pair'), ROUND) for piece in now]  73.8 us
    all_to_all x1, blocking collectives, body(): lax.all_to_all(ordered, 'chan', split_axis=0, concat_axis=0, tiled=True)  42.9 us
    ppermute x2, waiting for transfers between devices, body(): lax.ppermute(half, 'integ', [(0, 1), (1, 0)])  8.52 us
    ppermute x2, starting transfers between devices, body(): lax.ppermute(half, 'integ', [(0, 1), (1, 0)])  5.84 us
    ppermute x21, waiting for transfers between devices, rings(): passed = [lax.ppermute(piece, ('chan', 'pair'), ROUND) for piece in now]  5.27 us
    pallas_call x6, Pallas kernels, put(): pl.pallas_call(lambda *refs: put_kernel(steps, *refs), out_shape=(jax.Sha...  3.56 us
    pallas_call x1, Pallas kernels, tiles(): pl.pallas_call(most_kernel, out_shape=(blocks, jax.ShapeDtypeStruct((coun...  3.02 us
  transfers between devices with their start and end apart: 23, of which 9 were waited for; matrix products, arithmetic and copies ran while one was open for 0% of the time, Pallas kernels for 4%

profile of v3, /device:TPU:64, one launch (start us, length us, event | category | flops | bytes accessed | tf_op | source)
XLA Modules:
  0.0 148.2 jit_solution(447029295469562462)
XLA Ops:
  0.0 1.3 copy.13
  1.3 0.1 pad_add_fusion.where
  1.4 42.9 %all_to_all.5 = bf16[32,2,32,256]{3,2,1,0:T(8,128)(2,1)S(1)} all-to-all(bf16[32,2,32,256]{3,2,1,0:T(8,128)(2,1)S(1)} %bitcast.13), channel_id=1, replica_groups=mesh['chan'=32,'pair'=8,'integ'=2] {'chan'}, dimensions={0} | all-to-all | bytes 2097152 | tf_op jit(solution)/shard_map/all_to_all | solution.py:157
  44.3 0.1 fusion
  44.3 3.5 %collective-permute-start = (bf16[11,2,32,256]{3,2,1,0:T(8,128)(2,1)S(1)}, bf16[11,2,32,256]{3,2,1,0:T(8,128)(2,1)S(1)}, u32[]{:S(2)}, u32[]{:S(2)}) collective-permute-start(bf16[11,2,32,256]{3,2,1,0:T(8,128)(2,1)S(1)} %get-tuple-element.64.refs_0_), channel_id=1, source_target_pairs={{0,2},{2,4},{4,6},{6,8},{8,10},{10,12},{12,14},{14,0},{16,30},{18,... | collective-permute-start | bytes 1081352 | tf_op jit(solution)/shard_map/ppermute | solution.py:67
  47.8 3.5 %collective-permute-start.1 = (bf16[11,2,32,256]{3,2,1,0:T(8,128)(2,1)S(1)}, bf16[11,2,32,256]{3,2,1,0:T(8,128)(2,1)S(1)}, u32[]{:S(2)}, u32[]{:S(2)}) collective-permute-start(bf16[11,2,32,256]{3,2,1,0:T(8,128)(2,1)S(1)} %get-tuple-element.63.refs_1_), channel_id=1, source_target_pairs={{0,2},{2,4},{4,6},{6,8},{8,10},{10,12},{12,14},{14,0},{16,30},{18,... | collective-permute-start | bytes 1081352 | tf_op jit(solution)/shard_map/ppermute | solution.py:67
  51.4 3.5 %collective-permute-start.2 = (bf16[10,2,32,256]{3,2,1,0:T(8,128)(2,1)S(1)}, bf16[10,2,32,256]{3,2,1,0:T(8,128)(2,1)S(1)}, u32[]{:S(2)}, u32[]{:S(2)}) collective-permute-start(bf16[10,2,32,256]{3,2,1,0:T(8,128)(2,1)S(1)} %slice.14.refs_2_), channel_id=1, source_target_pairs={{0,2},{2,4},{4,6},{6,8},{8,10},{10,12},{12,14},{14,0},{16,30},{18,... | collective-permute-start | bytes 983048 | tf_op jit(solution)/shard_map/ppermute | solution.py:67
  54.8 0.3 collective-permute-done.refs_3_
  55.1 4.4 %collective-permute-start.3 = (bf16[11,2,32,256]{3,2,1,0:T(8,128)(2,1)S(1)}, bf16[11,2,32,256]{3,2,1,0:T(8,128)(2,1)S(1)}, u32[]{:S(2)}, u32[]{:S(2)}) collective-permute-start(bf16[11,2,32,256]{3,2,1,0:T(8,128)(2,1)S(1)} %collective-permute-done.refs_3_), channel_id=1, source_target_pairs={{0,2},{2,4},{4,6},{6,8},{8,10},{10,12},{12,14},{14,0},{16,30},{18,... | collective-permute-start | bytes 1081352 | tf_op jit(solution)/shard_map/ppermute | solution.py:67
  59.6 0.0 collective-permute-done.1.refs_4_
  59.6 2.6 %collective-permute-start.4 = (bf16[11,2,32,256]{3,2,1,0:T(8,128)(2,1)S(1)}, bf16[11,2,32,256]{3,2,1,0:T(8,128)(2,1)S(1)}, u32[]{:S(2)}, u32[]{:S(2)}) collective-permute-start(bf16[11,2,32,256]{3,2,1,0:T(8,128)(2,1)S(1)} %collective-permute-done.1.refs_4_), channel_id=1, source_target_pairs={{0,2},{2,4},{4,6},{6,8},{8,10},{10,12},{12,14},{14,0},{16,30},{18,... | collective-permute-start | bytes 1081352 | tf_op jit(solution)/shard_map/ppermute | solution.py:67
  62.2 0.3 collective-permute-done.2.refs_5_
  62.5 2.3 %collective-permute-start.5 = (bf16[10,2,32,256]{3,2,1,0:T(8,128)(2,1)S(1)}, bf16[10,2,32,256]{3,2,1,0:T(8,128)(2,1)S(1)}, u32[]{:S(2)}, u32[]{:S(2)}) collective-permute-start(bf16[10,2,32,256]{3,2,1,0:T(8,128)(2,1)S(1)} %collective-permute-done.2.refs_5_), channel_id=1, source_target_pairs={{0,2},{2,4},{4,6},{6,8},{8,10},{10,12},{12,14},{14,0},{16,30},{18,... | collective-permute-start | bytes 983048 | tf_op jit(solution)/shard_map/ppermute | solution.py:67
  64.8 0.8 put.6
  65.6 0.7 collective-permute-done.3.refs_2_
  66.4 4.6 %collective-permute-start.6 = (bf16[11,2,32,256]{3,2,1,0:T(8,128)(2,1)S(1)}, bf16[11,2,32,256]{3,2,1,0:T(8,128)(2,1)S(1)}, u32[]{:S(2)}, u32[]{:S(2)}) collective-permute-start(bf16[11,2,32,256]{3,2,1,0:T(8,128)(2,1)S(1)} %collective-permute-done.3.refs_2_), channel_id=1, source_target_pairs={{0,2},{2,4},{4,6},{6,8},{8,10},{10,12},{12,14},{14,0},{16,30},{18,... | collective-permute-start | bytes 1081352 | tf_op jit(solution)/shard_map/ppermute | solution.py:67
  70.9 3.8 %collective-permute-start.7 = (bf16[11,2,32,256]{3,2,1,0:T(8,128)(2,1)S(1)}, bf16[11,2,32,256]{3,2,1,0:T(8,128)(2,1)S(1)}, u32[]{:S(2)}, u32[]{:S(2)}) collective-permute-start(bf16[11,2,32,256]{3,2,1,0:T(8,128)(2,1)S(1)} %collective-permute-done.4.refs_3_), channel_id=1, source_target_pairs={{0,2},{2,4},{4,6},{6,8},{8,10},{10,12},{12,14},{14,0},{16,30},{18,... | collective-permute-start | bytes 1081352 | tf_op jit(solution)/shard_map/ppermute | solution.py:67
  74.8 3.5 %collective-permute-start.8 = (bf16[10,2,32,256]{3,2,1,0:T(8,128)(2,1)S(1)}, bf16[10,2,32,256]{3,2,1,0:T(8,128)(2,1)S(1)}, u32[]{:S(2)}, u32[]{:S(2)}) collective-permute-start(bf16[10,2,32,256]{3,2,1,0:T(8,128)(2,1)S(1)} %collective-permute-done.5.refs_4_), channel_id=1, source_target_pairs={{0,2},{2,4},{4,6},{6,8},{8,10},{10,12},{12,14},{14,0},{16,30},{18,... | collective-permute-start | bytes 983048 | tf_op jit(solution)/shard_map/ppermute | solution.py:67
  78.3 0.4 put.7
  78.7 0.0 collective-permute-done.6.refs_2_
  78.7 3.0 %collective-permute-start.9 = (bf16[11,2,32,256]{3,2,1,0:T(8,128)(2,1)S(1)}, bf16[11,2,32,256]{3,2,1,0:T(8,128)(2,1)S(1)}, u32[]{:S(2)}, u32[]{:S(2)}) collective-permute-start(bf16[11,2,32,256]{3,2,1,0:T(8,128)(2,1)S(1)} %collective-permute-done.6.refs_2_), channel_id=1, source_target_pairs={{0,2},{2,4},{4,6},{6,8},{8,10},{10,12},{12,14},{14,0},{16,30},{18,... | collective-permute-start | bytes 1081352 | tf_op jit(solution)/shard_map/ppermute | solution.py:67
  81.8 3.8 %collective-permute-start.10 = (bf16[11,2,32,256]{3,2,1,0:T(8,128)(2,1)S(1)}, bf16[11,2,32,256]{3,2,1,0:T(8,128)(2,1)S(1)}, u32[]{:S(2)}, u32[]{:S(2)}) collective-permute-start(bf16[11,2,32,256]{3,2,1,0:T(8,128)(2,1)S(1)} %collective-permute-done.7.refs_3_), channel_id=1, source_target_pairs={{0,2},{2,4},{4,6},{6,8},{8,10},{10,12},{12,14},{14,0},{16,30},{18,... | collective-permute-start | bytes 1081352 | tf_op jit(solution)/shard_map/ppermute | solution.py:67
  85.6 3.5 %collective-permute-start.11 = (bf16[10,2,32,256]{3,2,1,0:T(8,128)(2,1)S(1)}, bf16[10,2,32,256]{3,2,1,0:T(8,128)(2,1)S(1)}, u32[]{:S(2)}, u32[]{:S(2)}) collective-permute-start(bf16[10,2,32,256]{3,2,1,0:T(8,128)(2,1)S(1)} %collective-permute-done.8.refs_4_), channel_id=1, source_target_pairs={{0,2},{2,4},{4,6},{6,8},{8,10},{10,12},{12,14},{14,0},{16,30},{18,... | collective-permute-start | bytes 983048 | tf_op jit(solution)/shard_map/ppermute | solution.py:67
  89.1 0.4 put.8
  89.6 3.4 %collective-permute-start.12 = (bf16[11,2,32,256]{3,2,1,0:T(8,128)(2,1)S(1)}, bf16[11,2,32,256]{3,2,1,0:T(8,128)(2,1)S(1)}, u32[]{:S(2)}, u32[]{:S(2)}) collective-permute-start(bf16[11,2,32,256]{3,2,1,0:T(8,128)(2,1)S(1)} %collective-permute-done.9.refs_2_), channel_id=1, source_target_pairs={{0,2},{2,4},{4,6},{6,8},{8,10},{10,12},{12,14},{14,0},{16,30},{18,... | collective-permute-start | bytes 1081352 | tf_op jit(solution)/shard_map/ppermute | solution.py:67
  93.0 0.2 collective-permute-done.10.refs_3_
  93.1 3.7 %collective-permute-start.13 = (bf16[11,2,32,256]{3,2,1,0:T(8,128)(2,1)S(1)}, bf16[11,2,32,256]{3,2,1,0:T(8,128)(2,1)S(1)}, u32[]{:S(2)}, u32[]{:S(2)}) collective-permute-start(bf16[11,2,32,256]{3,2,1,0:T(8,128)(2,1)S(1)} %collective-permute-done.10.refs_3_), channel_id=1, source_target_pairs={{0,2},{2,4},{4,6},{6,8},{8,10},{10,12},{12,14},{14,0},{16,30},{18,... | collective-permute-start | bytes 1081352 | tf_op jit(solution)/shard_map/ppermute | solution.py:67
  96.8 3.5 %collective-permute-start.14 = (bf16[10,2,32,256]{3,2,1,0:T(8,128)(2,1)S(1)}, bf16[10,2,32,256]{3,2,1,0:T(8,128)(2,1)S(1)}, u32[]{:S(2)}, u32[]{:S(2)}) collective-permute-start(bf16[10,2,32,256]{3,2,1,0:T(8,128)(2,1)S(1)} %collective-permute-done.11.refs_4_), channel_id=1, source_target_pairs={{0,2},{2,4},{4,6},{6,8},{8,10},{10,12},{12,14},{14,0},{16,30},{18,... | collective-permute-start | bytes 983048 | tf_op jit(solution)/shard_map/ppermute | solution.py:67
  100.3 0.4 put.9
  100.8 3.4 %collective-permute-start.15 = (bf16[11,2,32,256]{3,2,1,0:T(8,128)(2,1)S(1)}, bf16[11,2,32,256]{3,2,1,0:T(8,128)(2,1)S(1)}, u32[]{:S(2)}, u32[]{:S(2)}) collective-permute-start(bf16[11,2,32,256]{3,2,1,0:T(8,128)(2,1)S(1)} %collective-permute-done.12.refs_2_), channel_id=1, source_target_pairs={{0,2},{2,4},{4,6},{6,8},{8,10},{10,12},{12,14},{14,0},{16,30},{18,... | collective-permute-start | bytes 1081352 | tf_op jit(solution)/shard_map/ppermute | solution.py:67
  104.2 0.2 collective-permute-done.13.refs_3_
  104.4 3.7 %collective-permute-start.16 = (bf16[11,2,32,256]{3,2,1,0:T(8,128)(2,1)S(1)}, bf16[11,2,32,256]{3,2,1,0:T(8,128)(2,1)S(1)}, u32[]{:S(2)}, u32[]{:S(2)}) collective-permute-start(bf16[11,2,32,256]{3,2,1,0:T(8,128)(2,1)S(1)} %collective-permute-done.13.refs_3_), channel_id=1, source_target_pairs={{0,2},{2,4},{4,6},{6,8},{8,10},{10,12},{12,14},{14,0},{16,30},{18,... | collective-permute-start | bytes 1081352 | tf_op jit(solution)/shard_map/ppermute | solution.py:67
  108.1 3.5 %collective-permute-start.17 = (bf16[10,2,32,256]{3,2,1,0:T(8,128)(2,1)S(1)}, bf16[10,2,32,256]{3,2,1,0:T(8,128)(2,1)S(1)}, u32[]{:S(2)}, u32[]{:S(2)}) collective-permute-start(bf16[10,2,32,256]{3,2,1,0:T(8,128)(2,1)S(1)} %collective-permute-done.14.refs_4_), channel_id=1, source_target_pairs={{0,2},{2,4},{4,6},{6,8},{8,10},{10,12},{12,14},{14,0},{16,30},{18,... | collective-permute-start | bytes 983048 | tf_op jit(solution)/shard_map/ppermute | solution.py:67
  111.6 0.0 copy-start
  111.6 0.4 put.10
  112.0 3.4 %collective-permute-start.18 = (bf16[11,2,32,256]{3,2,1,0:T(8,128)(2,1)S(1)}, bf16[11,2,32,256]{3,2,1,0:T(8,128)(2,1)S(1)}, u32[]{:S(2)}, u32[]{:S(2)}) collective-permute-start(bf16[11,2,32,256]{3,2,1,0:T(8,128)(2,1)S(1)} %collective-permute-done.15.refs_2_), channel_id=1, source_target_pairs={{0,2},{2,4},{4,6},{6,8},{8,10},{10,12},{12,14},{14,0},{16,30},{18,... | collective-permute-start | bytes 1081352 | tf_op jit(solution)/shard_map/ppermute | solution.py:67
  115.5 0.1 collective-permute-done.16.refs_3_
  115.6 3.7 %collective-permute-start.19 = (bf16[11,2,32,256]{3,2,1,0:T(8,128)(2,1)S(1)}, bf16[11,2,32,256]{3,2,1,0:T(8,128)(2,1)S(1)}, u32[]{:S(2)}, u32[]{:S(2)}) collective-permute-start(bf16[11,2,32,256]{3,2,1,0:T(8,128)(2,1)S(1)} %collective-permute-done.16.refs_3_), channel_id=1, source_target_pairs={{0,2},{2,4},{4,6},{6,8},{8,10},{10,12},{12,14},{14,0},{16,30},{18,... | collective-permute-start | bytes 1081352 | tf_op jit(solution)/shard_map/ppermute | solution.py:67
  119.3 3.5 %collective-permute-start.20 = (bf16[10,2,32,256]{3,2,1,0:T(8,128)(2,1)S(1)}, bf16[10,2,32,256]{3,2,1,0:T(8,128)(2,1)S(1)}, u32[]{:S(2)}, u32[]{:S(2)}) collective-permute-start(bf16[10,2,32,256]{3,2,1,0:T(8,128)(2,1)S(1)} %collective-permute-done.17.refs_4_), channel_id=1, source_target_pairs={{0,2},{2,4},{4,6},{6,8},{8,10},{10,12},{12,14},{14,0},{16,30},{18,... | collective-permute-start | bytes 983048 | tf_op jit(solution)/shard_map/ppermute | solution.py:67
  122.8 1.0 put.11
  123.9 3.0 %collective-permute-done.19.refs_2_ = bf16[11,2,32,256]{3,2,1,0:T(8,128)(2,1)S(1)} collective-permute-done((bf16[11,2,32,256]{3,2,1,0:T(8,128)(2,1)S(1)}, bf16[11,2,32,256]{3,2,1,0:T(8,128)(2,1)S(1)}, u32[]{:S(2)}, u32[]{:S(2)}) %collective-permute-start.19) | collective-permute-done | bytes 360480 | tf_op jit(solution)/shard_map/ppermute | solution.py:67
  126.8 3.0 %most.1 = (bf16[8,32,2,32,256]{4,3,2,1,0:T(8,128)(2,1)S(1)}, f32[17,2,128,128]{3,2,1,0:T(8,128)S(1)}) custom-call(s32[3]{0:T(128)S(1)} %pad_add_fusion.where, s32[2,17]{1,0:T(2,128)S(1)} %bitcast.11, bf16[8,32,2,32,256]{4,3,2,1,0:T(8,128)(2,1)S(1)} %get-tuple-element.57.refs_0_, ...), custom_call_target="tpu_custom_call", output_to_operand_aliasing={{0}: (2, {})} | custom-call | flops 1140850688 | bytes 10485760 | tf_op jit(solution)/shard_map/most/pallas_call | solution.py:127
  129.9 0.5 collective-permute-done.20.last
  130.4 2.2 %rest.1 = (bf16[8,32,2,32,256]{4,3,2,1,0:T(8,128)(2,1)S(1)}, f32[17,2,64,128]{3,2,1,0:T(8,128)S(1)}, s16[17,2,64,128]{3,2,1,0:T(8,128)(2,1)S(1)}, f32[17,2,128]{2,1,0:T(2,128)S(1)}) custom-call(s32[3]{0:T(128)S(1)} %pad_add_fusion.where, s32[2,17]{1,0:T(2,128)S(1)} %bitcast.12, ...), custom_call_target="tpu_custom_call", output_to_operand_aliasing={{0}: (2, {})} | custom-call | flops 1140850688 | bytes 10485760 | tf_op jit(solution)/shard_map/rest/pallas_call | solution.py:137
  132.6 2.5 %collective-permute-start.21 = (s16[17,2,64,128]{3,2,1,0:T(8,128)(2,1)S(1)}, s16[17,2,64,128]{3,2,1,0:T(8,128)(2,1)S(1)}, u32[]{:S(2)}, u32[]{:S(2)}) collective-permute-start(s16[17,2,64,128]{3,2,1,0:T(8,128)(2,1)S(1)} %get-tuple-element.61), channel_id=1, source_target_pairs={{0,1},{1,0},{2,3},{3,2},{4,5},{5,4},{6,7},{7,6},{8,9},{9,8},{10,11... | collective-permute-start | bytes 1671176 | tf_op jit(solution)/shard_map/ppermute | solution.py:159
  135.1 3.3 %collective-permute-start.22 = (f32[17,2,128]{2,1,0:T(2,128)S(1)}, f32[17,2,128]{2,1,0:T(2,128)S(1)}, u32[]{:S(2)}, u32[]{:S(2)}) collective-permute-start(f32[17,2,128]{2,1,0:T(2,128)S(1)} %get-tuple-element.62), channel_id=1, source_target_pairs={{0,1},{1,0},{2,3},{3,2},{4,5},{5,4},{6,7},{7,6},{8,9},{9,8},{10,11... | collective-permute-start | bytes 52232 | tf_op jit(solution)/shard_map/ppermute | solution.py:159
  138.5 8.5 %collective-permute-done.22 = f32[17,2,128]{2,1,0:T(2,128)S(1)} collective-permute-done((f32[17,2,128]{2,1,0:T(2,128)S(1)}, f32[17,2,128]{2,1,0:T(2,128)S(1)}, u32[]{:S(2)}, u32[]{:S(2)}) %collective-permute-start.22) | collective-permute-done | bytes 17440 | tf_op jit(solution)/shard_map/ppermute | solution.py:159
  147.0 1.2 add_bitcast_fusion
  (14 shorter events, 0.1 us)
Async XLA Ops:
  44.3 10.8 %collective-permute-start = (bf16[11,2,32,256]{3,2,1,0:T(8,128)(2,1)S(1)}, bf16[11,2,32,256]{3,2,1,0:T(8,128)(2,1)S(1)}, u32[]{:S(2)}, u32[]{:S(2)}) collective-permute-start(bf16[11,2,32,256]{3,2,1,0:T(8,128)(2,1)S(1)} %get-tuple-element.64.refs_0_), channel_id=1, source_target_pairs={{0,2},{2,4},{4,6},{6,8},{8,10},{10,12},{12,14},{14,0},{16,30},{18,... | collective-permute-start | bytes 1081352 | tf_op jit(solution)/shard_map/ppermute | solution.py:67
  47.8 11.7 %collective-permute-start.1 = (bf16[11,2,32,256]{3,2,1,0:T(8,128)(2,1)S(1)}, bf16[11,2,32,256]{3,2,1,0:T(8,128)(2,1)S(1)}, u32[]{:S(2)}, u32[]{:S(2)}) collective-permute-start(bf16[11,2,32,256]{3,2,1,0:T(8,128)(2,1)S(1)} %get-tuple-element.63.refs_1_), channel_id=1, source_target_pairs={{0,2},{2,4},{4,6},{6,8},{8,10},{10,12},{12,14},{14,0},{16,30},{18,... | collective-permute-start | bytes 1081352 | tf_op jit(solution)/shard_map/ppermute | solution.py:67
  51.4 11.1 %collective-permute-start.2 = (bf16[10,2,32,256]{3,2,1,0:T(8,128)(2,1)S(1)}, bf16[10,2,32,256]{3,2,1,0:T(8,128)(2,1)S(1)}, u32[]{:S(2)}, u32[]{:S(2)}) collective-permute-start(bf16[10,2,32,256]{3,2,1,0:T(8,128)(2,1)S(1)} %slice.14.refs_2_), channel_id=1, source_target_pairs={{0,2},{2,4},{4,6},{6,8},{8,10},{10,12},{12,14},{14,0},{16,30},{18,... | collective-permute-start | bytes 983048 | tf_op jit(solution)/shard_map/ppermute | solution.py:67
  55.1 11.2 %collective-permute-start.3 = (bf16[11,2,32,256]{3,2,1,0:T(8,128)(2,1)S(1)}, bf16[11,2,32,256]{3,2,1,0:T(8,128)(2,1)S(1)}, u32[]{:S(2)}, u32[]{:S(2)}) collective-permute-start(bf16[11,2,32,256]{3,2,1,0:T(8,128)(2,1)S(1)} %collective-permute-done.refs_3_), channel_id=1, source_target_pairs={{0,2},{2,4},{4,6},{6,8},{8,10},{10,12},{12,14},{14,0},{16,30},{18,... | collective-permute-start | bytes 1081352 | tf_op jit(solution)/shard_map/ppermute | solution.py:67
  59.6 11.4 %collective-permute-start.4 = (bf16[11,2,32,256]{3,2,1,0:T(8,128)(2,1)S(1)}, bf16[11,2,32,256]{3,2,1,0:T(8,128)(2,1)S(1)}, u32[]{:S(2)}, u32[]{:S(2)}) collective-permute-start(bf16[11,2,32,256]{3,2,1,0:T(8,128)(2,1)S(1)} %collective-permute-done.1.refs_4_), channel_id=1, source_target_pairs={{0,2},{2,4},{4,6},{6,8},{8,10},{10,12},{12,14},{14,0},{16,30},{18,... | collective-permute-start | bytes 1081352 | tf_op jit(solution)/shard_map/ppermute | solution.py:67
  62.5 12.3 %collective-permute-start.5 = (bf16[10,2,32,256]{3,2,1,0:T(8,128)(2,1)S(1)}, bf16[10,2,32,256]{3,2,1,0:T(8,128)(2,1)S(1)}, u32[]{:S(2)}, u32[]{:S(2)}) collective-permute-start(bf16[10,2,32,256]{3,2,1,0:T(8,128)(2,1)S(1)} %collective-permute-done.2.refs_5_), channel_id=1, source_target_pairs={{0,2},{2,4},{4,6},{6,8},{8,10},{10,12},{12,14},{14,0},{16,30},{18,... | collective-permute-start | bytes 983048 | tf_op jit(solution)/shard_map/ppermute | solution.py:67
  66.4 12.4 %collective-permute-start.6 = (bf16[11,2,32,256]{3,2,1,0:T(8,128)(2,1)S(1)}, bf16[11,2,32,256]{3,2,1,0:T(8,128)(2,1)S(1)}, u32[]{:S(2)}, u32[]{:S(2)}) collective-permute-start(bf16[11,2,32,256]{3,2,1,0:T(8,128)(2,1)S(1)} %collective-permute-done.3.refs_2_), channel_id=1, source_target_pairs={{0,2},{2,4},{4,6},{6,8},{8,10},{10,12},{12,14},{14,0},{16,30},{18,... | collective-permute-start | bytes 1081352 | tf_op jit(solution)/shard_map/ppermute | solution.py:67
  70.9 10.8 %collective-permute-start.7 = (bf16[11,2,32,256]{3,2,1,0:T(8,128)(2,1)S(1)}, bf16[11,2,32,256]{3,2,1,0:T(8,128)(2,1)S(1)}, u32[]{:S(2)}, u32[]{:S(2)}) collective-permute-start(bf16[11,2,32,256]{3,2,1,0:T(8,128)(2,1)S(1)} %collective-permute-done.4.refs_3_), channel_id=1, source_target_pairs={{0,2},{2,4},{4,6},{6,8},{8,10},{10,12},{12,14},{14,0},{16,30},{18,... | collective-permute-start | bytes 1081352 | tf_op jit(solution)/shard_map/ppermute | solution.py:67
  74.8 10.8 %collective-permute-start.8 = (bf16[10,2,32,256]{3,2,1,0:T(8,128)(2,1)S(1)}, bf16[10,2,32,256]{3,2,1,0:T(8,128)(2,1)S(1)}, u32[]{:S(2)}, u32[]{:S(2)}) collective-permute-start(bf16[10,2,32,256]{3,2,1,0:T(8,128)(2,1)S(1)} %collective-permute-done.5.refs_4_), channel_id=1, source_target_pairs={{0,2},{2,4},{4,6},{6,8},{8,10},{10,12},{12,14},{14,0},{16,30},{18,... | collective-permute-start | bytes 983048 | tf_op jit(solution)/shard_map/ppermute | solution.py:67
  78.7 10.8 %collective-permute-start.9 = (bf16[11,2,32,256]{3,2,1,0:T(8,128)(2,1)S(1)}, bf16[11,2,32,256]{3,2,1,0:T(8,128)(2,1)S(1)}, u32[]{:S(2)}, u32[]{:S(2)}) collective-permute-start(bf16[11,2,32,256]{3,2,1,0:T(8,128)(2,1)S(1)} %collective-permute-done.6.refs_2_), channel_id=1, source_target_pairs={{0,2},{2,4},{4,6},{6,8},{8,10},{10,12},{12,14},{14,0},{16,30},{18,... | collective-permute-start | bytes 1081352 | tf_op jit(solution)/shard_map/ppermute | solution.py:67
  81.8 11.4 %collective-permute-start.10 = (bf16[11,2,32,256]{3,2,1,0:T(8,128)(2,1)S(1)}, bf16[11,2,32,256]{3,2,1,0:T(8,128)(2,1)S(1)}, u32[]{:S(2)}, u32[]{:S(2)}) collective-permute-start(bf16[11,2,32,256]{3,2,1,0:T(8,128)(2,1)S(1)} %collective-permute-done.7.refs_3_), channel_id=1, source_target_pairs={{0,2},{2,4},{4,6},{6,8},{8,10},{10,12},{12,14},{14,0},{16,30},{18,... | collective-permute-start | bytes 1081352 | tf_op jit(solution)/shard_map/ppermute | solution.py:67
  85.6 11.2 %collective-permute-start.11 = (bf16[10,2,32,256]{3,2,1,0:T(8,128)(2,1)S(1)}, bf16[10,2,32,256]{3,2,1,0:T(8,128)(2,1)S(1)}, u32[]{:S(2)}, u32[]{:S(2)}) collective-permute-start(bf16[10,2,32,256]{3,2,1,0:T(8,128)(2,1)S(1)} %collective-permute-done.8.refs_4_), channel_id=1, source_target_pairs={{0,2},{2,4},{4,6},{6,8},{8,10},{10,12},{12,14},{14,0},{16,30},{18,... | collective-permute-start | bytes 983048 | tf_op jit(solution)/shard_map/ppermute | solution.py:67
  89.6 11.2 %collective-permute-start.12 = (bf16[11,2,32,256]{3,2,1,0:T(8,128)(2,1)S(1)}, bf16[11,2,32,256]{3,2,1,0:T(8,128)(2,1)S(1)}, u32[]{:S(2)}, u32[]{:S(2)}) collective-permute-start(bf16[11,2,32,256]{3,2,1,0:T(8,128)(2,1)S(1)} %collective-permute-done.9.refs_2_), channel_id=1, source_target_pairs={{0,2},{2,4},{4,6},{6,8},{8,10},{10,12},{12,14},{14,0},{16,30},{18,... | collective-permute-start | bytes 1081352 | tf_op jit(solution)/shard_map/ppermute | solution.py:67
  93.1 11.2 %collective-permute-start.13 = (bf16[11,2,32,256]{3,2,1,0:T(8,128)(2,1)S(1)}, bf16[11,2,32,256]{3,2,1,0:T(8,128)(2,1)S(1)}, u32[]{:S(2)}, u32[]{:S(2)}) collective-permute-start(bf16[11,2,32,256]{3,2,1,0:T(8,128)(2,1)S(1)} %collective-permute-done.10.refs_3_), channel_id=1, source_target_pairs={{0,2},{2,4},{4,6},{6,8},{8,10},{10,12},{12,14},{14,0},{16,30},{18,... | collective-permute-start | bytes 1081352 | tf_op jit(solution)/shard_map/ppermute | solution.py:67
  96.8 11.2 %collective-permute-start.14 = (bf16[10,2,32,256]{3,2,1,0:T(8,128)(2,1)S(1)}, bf16[10,2,32,256]{3,2,1,0:T(8,128)(2,1)S(1)}, u32[]{:S(2)}, u32[]{:S(2)}) collective-permute-start(bf16[10,2,32,256]{3,2,1,0:T(8,128)(2,1)S(1)} %collective-permute-done.11.refs_4_), channel_id=1, source_target_pairs={{0,2},{2,4},{4,6},{6,8},{8,10},{10,12},{12,14},{14,0},{16,30},{18,... | collective-permute-start | bytes 983048 | tf_op jit(solution)/shard_map/ppermute | solution.py:67
  100.8 11.2 %collective-permute-start.15 = (bf16[11,2,32,256]{3,2,1,0:T(8,128)(2,1)S(1)}, bf16[11,2,32,256]{3,2,1,0:T(8,128)(2,1)S(1)}, u32[]{:S(2)}, u32[]{:S(2)}) collective-permute-start(bf16[11,2,32,256]{3,2,1,0:T(8,128)(2,1)S(1)} %collective-permute-done.12.refs_2_), channel_id=1, source_target_pairs={{0,2},{2,4},{4,6},{6,8},{8,10},{10,12},{12,14},{14,0},{16,30},{18,... | collective-permute-start | bytes 1081352 | tf_op jit(solution)/shard_map/ppermute | solution.py:67
  104.4 11.2 %collective-permute-start.16 = (bf16[11,2,32,256]{3,2,1,0:T(8,128)(2,1)S(1)}, bf16[11,2,32,256]{3,2,1,0:T(8,128)(2,1)S(1)}, u32[]{:S(2)}, u32[]{:S(2)}) collective-permute-start(bf16[11,2,32,256]{3,2,1,0:T(8,128)(2,1)S(1)} %collective-permute-done.13.refs_3_), channel_id=1, source_target_pairs={{0,2},{2,4},{4,6},{6,8},{8,10},{10,12},{12,14},{14,0},{16,30},{18,... | collective-permute-start | bytes 1081352 | tf_op jit(solution)/shard_map/ppermute | solution.py:67
  108.1 11.2 %collective-permute-start.17 = (bf16[10,2,32,256]{3,2,1,0:T(8,128)(2,1)S(1)}, bf16[10,2,32,256]{3,2,1,0:T(8,128)(2,1)S(1)}, u32[]{:S(2)}, u32[]{:S(2)}) collective-permute-start(bf16[10,2,32,256]{3,2,1,0:T(8,128)(2,1)S(1)} %collective-permute-done.14.refs_4_), channel_id=1, source_target_pairs={{0,2},{2,4},{4,6},{6,8},{8,10},{10,12},{12,14},{14,0},{16,30},{18,... | collective-permute-start | bytes 983048 | tf_op jit(solution)/shard_map/ppermute | solution.py:67
  111.6 15.3 %copy-start = (s32[17,2]{0,1:T(2,128)S(1)}, s32[17,2]{0,1:T(2,128)}, u32[]{:S(2)}) copy-start(s32[17,2]{0,1:T(2,128)} %param.3) | copy-start | bytes 412
  112.0 11.8 %collective-permute-start.18 = (bf16[11,2,32,256]{3,2,1,0:T(8,128)(2,1)S(1)}, bf16[11,2,32,256]{3,2,1,0:T(8,128)(2,1)S(1)}, u32[]{:S(2)}, u32[]{:S(2)}) collective-permute-start(bf16[11,2,32,256]{3,2,1,0:T(8,128)(2,1)S(1)} %collective-permute-done.15.refs_2_), channel_id=1, source_target_pairs={{0,2},{2,4},{4,6},{6,8},{8,10},{10,12},{12,14},{14,0},{16,30},{18,... | collective-permute-start | bytes 1081352 | tf_op jit(solution)/shard_map/ppermute | solution.py:67
  115.6 11.2 %collective-permute-start.19 = (bf16[11,2,32,256]{3,2,1,0:T(8,128)(2,1)S(1)}, bf16[11,2,32,256]{3,2,1,0:T(8,128)(2,1)S(1)}, u32[]{:S(2)}, u32[]{:S(2)}) collective-permute-start(bf16[11,2,32,256]{3,2,1,0:T(8,128)(2,1)S(1)} %collective-permute-done.16.refs_3_), channel_id=1, source_target_pairs={{0,2},{2,4},{4,6},{6,8},{8,10},{10,12},{12,14},{14,0},{16,30},{18,... | collective-permute-start | bytes 1081352 | tf_op jit(solution)/shard_map/ppermute | solution.py:67
  119.3 11.0 %collective-permute-start.20 = (bf16[10,2,32,256]{3,2,1,0:T(8,128)(2,1)S(1)}, bf16[10,2,32,256]{3,2,1,0:T(8,128)(2,1)S(1)}, u32[]{:S(2)}, u32[]{:S(2)}) collective-permute-start(bf16[10,2,32,256]{3,2,1,0:T(8,128)(2,1)S(1)} %collective-permute-done.17.refs_4_), channel_id=1, source_target_pairs={{0,2},{2,4},{4,6},{6,8},{8,10},{10,12},{12,14},{14,0},{16,30},{18,... | collective-permute-start | bytes 983048 | tf_op jit(solution)/shard_map/ppermute | solution.py:67
  132.6 14.4 %collective-permute-start.21 = (s16[17,2,64,128]{3,2,1,0:T(8,128)(2,1)S(1)}, s16[17,2,64,128]{3,2,1,0:T(8,128)(2,1)S(1)}, u32[]{:S(2)}, u32[]{:S(2)}) collective-permute-start(s16[17,2,64,128]{3,2,1,0:T(8,128)(2,1)S(1)} %get-tuple-element.61), channel_id=1, source_target_pairs={{0,1},{1,0},{2,3},{3,2},{4,5},{5,4},{6,7},{7,6},{8,9},{9,8},{10,11... | collective-permute-start | bytes 1671176 | tf_op jit(solution)/shard_map/ppermute | solution.py:159
  135.1 11.9 %collective-permute-start.22 = (f32[17,2,128]{2,1,0:T(2,128)S(1)}, f32[17,2,128]{2,1,0:T(2,128)S(1)}, u32[]{:S(2)}, u32[]{:S(2)}) collective-permute-start(f32[17,2,128]{2,1,0:T(2,128)S(1)} %get-tuple-element.62), channel_id=1, source_target_pairs={{0,1},{1,0},{2,3},{3,2},{4,5},{5,4},{6,7},{7,6},{8,9},{9,8},{10,11... | collective-permute-start | bytes 52232 | tf_op jit(solution)/shard_map/ppermute | solution.py:159

commit v4 on v3

--- a/solution.py
+++ b/solution.py
@@ -7,6 +7,7 @@
 
 BLOCK = 128
 TIME = 2048
+STEPS = 32767.0
 CHAINS = (11, 11, 10)
 ROUND = [(c * 8 + y, c * 8 + (y + 1 - 2 * (c % 2)) % 8) for c in range(32) for y in range(8)]
 
@@ -108,8 +109,8 @@
         keep[k] = whole[:, pl.ds(pl.multiple_of(where[1] * half, half), half), :]
         other = whole[:, pl.ds(pl.multiple_of((1 - where[1]) * half, half), half), :]
         most = jnp.max(jnp.abs(other), axis=1, keepdims=True)
-        scale[k] = (most * (1.0 / 32767.0))[:, 0]
-        send[k] = jnp.round(other * jnp.where(most > 0, 32767.0 / most, 0.0)).astype(jnp.int32).astype(jnp.int16)
+        scale[k] = most[:, 0]
+        send[k] = jnp.round(other * jnp.where(most > 0, 1.0 / most, 0.0) * STEPS).astype(jnp.int32).astype(jnp.int16)
         return carry
 
     lax.fori_loop(0, table.shape[1], tile, 0, unroll=True)
@@ -157,7 +158,7 @@
     turned = lax.all_to_all(ordered, "chan", split_axis=0, concat_axis=0, tiled=True)
     _, keep, send, scale = tiles(where, table, *rings(turned))
     send, scale = (lax.ppermute(half, "integ", [(0, 1), (1, 0)]) for half in (send, scale))
-    return (keep + send.astype(jnp.float32) * scale[:, :, None])[:, None]
+    return (keep + send.astype(jnp.float32) * (1.0 / STEPS) * scale[:, :, None])[:, None]
 
 
 def solution(mesh):

time: 149 us -> 149 us (level)
  no operation moved by 1% of the time
where the time goes in v4:
time: 149 us; the launch traced here: 148 us
  starting transfers between devices  79.6 us (53%)
  blocking collectives  42.9 us (29%)
  waiting for transfers between devices  13.8 us (9%)
  Pallas kernels  8.84 us (6%)
    ppermute x21, starting transfers between devices, rings(): passed = [lax.ppermute(piece, ('chan', 'pair'), ROUND) for piece in now]  73.8 us
    all_to_all x1, blocking collectives, body(): lax.all_to_all(ordered, 'chan', split_axis=0, concat_axis=0, tiled=True)  42.9 us
    ppermute x2, waiting for transfers between devices, body(): lax.ppermute(half, 'integ', [(0, 1), (1, 0)])  8.51 us
    ppermute x2, starting transfers between devices, body(): lax.ppermute(half, 'integ', [(0, 1), (1, 0)])  5.84 us
    ppermute x21, waiting for transfers between devices, rings(): passed = [lax.ppermute(piece, ('chan', 'pair'), ROUND) for piece in now]  5.27 us
    pallas_call x6, Pallas kernels, put(): pl.pallas_call(lambda *refs: put_kernel(steps, *refs), out_shape=(jax.Sha...  3.56 us
    pallas_call x1, Pallas kernels, tiles(): pl.pallas_call(most_kernel, out_shape=(blocks, jax.ShapeDtypeStruct((coun...  3.02 us
  transfers between devices with their start and end apart: 23, of which 9 were waited for; matrix products, arithmetic and copies ran while one was open for 0% of the time, Pallas kernels for 4%

profile of v4, /device:TPU:64, one launch (start us, length us, event | category | flops | bytes accessed | tf_op | source)
XLA Modules:
  0.0 148.3 jit_solution(8757656611974433727)
XLA Ops:
  0.0 1.3 copy.13
  1.3 0.1 pad_add_fusion.where
  1.4 42.9 %all_to_all.5 = bf16[32,2,32,256]{3,2,1,0:T(8,128)(2,1)S(1)} all-to-all(bf16[32,2,32,256]{3,2,1,0:T(8,128)(2,1)S(1)} %bitcast.13), channel_id=1, replica_groups=mesh['chan'=32,'pair'=8,'integ'=2] {'chan'}, dimensions={0} | all-to-all | bytes 2097152 | tf_op jit(solution)/shard_map/all_to_all | solution.py:158
  44.3 0.1 fusion
  44.3 3.5 %collective-permute-start = (bf16[11,2,32,256]{3,2,1,0:T(8,128)(2,1)S(1)}, bf16[11,2,32,256]{3,2,1,0:T(8,128)(2,1)S(1)}, u32[]{:S(2)}, u32[]{:S(2)}) collective-permute-start(bf16[11,2,32,256]{3,2,1,0:T(8,128)(2,1)S(1)} %get-tuple-element.64.refs_0_), channel_id=1, source_target_pairs={{0,2},{2,4},{4,6},{6,8},{8,10},{10,12},{12,14},{14,0},{16,30},{18,... | collective-permute-start | bytes 1081352 | tf_op jit(solution)/shard_map/ppermute | solution.py:68
  47.8 3.5 %collective-permute-start.1 = (bf16[11,2,32,256]{3,2,1,0:T(8,128)(2,1)S(1)}, bf16[11,2,32,256]{3,2,1,0:T(8,128)(2,1)S(1)}, u32[]{:S(2)}, u32[]{:S(2)}) collective-permute-start(bf16[11,2,32,256]{3,2,1,0:T(8,128)(2,1)S(1)} %get-tuple-element.63.refs_1_), channel_id=1, source_target_pairs={{0,2},{2,4},{4,6},{6,8},{8,10},{10,12},{12,14},{14,0},{16,30},{18,... | collective-permute-start | bytes 1081352 | tf_op jit(solution)/shard_map/ppermute | solution.py:68
  51.4 3.5 %collective-permute-start.2 = (bf16[10,2,32,256]{3,2,1,0:T(8,128)(2,1)S(1)}, bf16[10,2,32,256]{3,2,1,0:T(8,128)(2,1)S(1)}, u32[]{:S(2)}, u32[]{:S(2)}) collective-permute-start(bf16[10,2,32,256]{3,2,1,0:T(8,128)(2,1)S(1)} %slice.14.refs_2_), channel_id=1, source_target_pairs={{0,2},{2,4},{4,6},{6,8},{8,10},{10,12},{12,14},{14,0},{16,30},{18,... | collective-permute-start | bytes 983048 | tf_op jit(solution)/shard_map/ppermute | solution.py:68
  54.8 0.3 collective-permute-done.refs_3_
  55.1 4.4 %collective-permute-start.3 = (bf16[11,2,32,256]{3,2,1,0:T(8,128)(2,1)S(1)}, bf16[11,2,32,256]{3,2,1,0:T(8,128)(2,1)S(1)}, u32[]{:S(2)}, u32[]{:S(2)}) collective-permute-start(bf16[11,2,32,256]{3,2,1,0:T(8,128)(2,1)S(1)} %collective-permute-done.refs_3_), channel_id=1, source_target_pairs={{0,2},{2,4},{4,6},{6,8},{8,10},{10,12},{12,14},{14,0},{16,30},{18,... | collective-permute-start | bytes 1081352 | tf_op jit(solution)/shard_map/ppermute | solution.py:68
  59.6 0.0 collective-permute-done.1.refs_4_
  59.6 2.6 %collective-permute-start.4 = (bf16[11,2,32,256]{3,2,1,0:T(8,128)(2,1)S(1)}, bf16[11,2,32,256]{3,2,1,0:T(8,128)(2,1)S(1)}, u32[]{:S(2)}, u32[]{:S(2)}) collective-permute-start(bf16[11,2,32,256]{3,2,1,0:T(8,128)(2,1)S(1)} %collective-permute-done.1.refs_4_), channel_id=1, source_target_pairs={{0,2},{2,4},{4,6},{6,8},{8,10},{10,12},{12,14},{14,0},{16,30},{18,... | collective-permute-start | bytes 1081352 | tf_op jit(solution)/shard_map/ppermute | solution.py:68
  62.2 0.3 collective-permute-done.2.refs_5_
  62.5 2.3 %collective-permute-start.5 = (bf16[10,2,32,256]{3,2,1,0:T(8,128)(2,1)S(1)}, bf16[10,2,32,256]{3,2,1,0:T(8,128)(2,1)S(1)}, u32[]{:S(2)}, u32[]{:S(2)}) collective-permute-start(bf16[10,2,32,256]{3,2,1,0:T(8,128)(2,1)S(1)} %collective-permute-done.2.refs_5_), channel_id=1, source_target_pairs={{0,2},{2,4},{4,6},{6,8},{8,10},{10,12},{12,14},{14,0},{16,30},{18,... | collective-permute-start | bytes 983048 | tf_op jit(solution)/shard_map/ppermute | solution.py:68
  64.8 0.8 put.6
  65.6 0.7 collective-permute-done.3.refs_2_
  66.4 4.6 %collective-permute-start.6 = (bf16[11,2,32,256]{3,2,1,0:T(8,128)(2,1)S(1)}, bf16[11,2,32,256]{3,2,1,0:T(8,128)(2,1)S(1)}, u32[]{:S(2)}, u32[]{:S(2)}) collective-permute-start(bf16[11,2,32,256]{3,2,1,0:T(8,128)(2,1)S(1)} %collective-permute-done.3.refs_2_), channel_id=1, source_target_pairs={{0,2},{2,4},{4,6},{6,8},{8,10},{10,12},{12,14},{14,0},{16,30},{18,... | collective-permute-start | bytes 1081352 | tf_op jit(solution)/shard_map/ppermute | solution.py:68
  70.9 3.8 %collective-permute-start.7 = (bf16[11,2,32,256]{3,2,1,0:T(8,128)(2,1)S(1)}, bf16[11,2,32,256]{3,2,1,0:T(8,128)(2,1)S(1)}, u32[]{:S(2)}, u32[]{:S(2)}) collective-permute-start(bf16[11,2,32,256]{3,2,1,0:T(8,128)(2,1)S(1)} %collective-permute-done.4.refs_3_), channel_id=1, source_target_pairs={{0,2},{2,4},{4,6},{6,8},{8,10},{10,12},{12,14},{14,0},{16,30},{18,... | collective-permute-start | bytes 1081352 | tf_op jit(solution)/shard_map/ppermute | solution.py:68
  74.8 0.0 collective-permute-done.5.refs_4_
  74.8 3.5 %collective-permute-start.8 = (bf16[10,2,32,256]{3,2,1,0:T(8,128)(2,1)S(1)}, bf16[10,2,32,256]{3,2,1,0:T(8,128)(2,1)S(1)}, u32[]{:S(2)}, u32[]{:S(2)}) collective-permute-start(bf16[10,2,32,256]{3,2,1,0:T(8,128)(2,1)S(1)} %collective-permute-done.5.refs_4_), channel_id=1, source_target_pairs={{0,2},{2,4},{4,6},{6,8},{8,10},{10,12},{12,14},{14,0},{16,30},{18,... | collective-permute-start | bytes 983048 | tf_op jit(solution)/shard_map/ppermute | solution.py:68
  78.3 0.4 put.7
  78.7 3.0 %collective-permute-start.9 = (bf16[11,2,32,256]{3,2,1,0:T(8,128)(2,1)S(1)}, bf16[11,2,32,256]{3,2,1,0:T(8,128)(2,1)S(1)}, u32[]{:S(2)}, u32[]{:S(2)}) collective-permute-start(bf16[11,2,32,256]{3,2,1,0:T(8,128)(2,1)S(1)} %collective-permute-done.6.refs_2_), channel_id=1, source_target_pairs={{0,2},{2,4},{4,6},{6,8},{8,10},{10,12},{12,14},{14,0},{16,30},{18,... | collective-permute-start | bytes 1081352 | tf_op jit(solution)/shard_map/ppermute | solution.py:68
  81.8 3.8 %collective-permute-start.10 = (bf16[11,2,32,256]{3,2,1,0:T(8,128)(2,1)S(1)}, bf16[11,2,32,256]{3,2,1,0:T(8,128)(2,1)S(1)}, u32[]{:S(2)}, u32[]{:S(2)}) collective-permute-start(bf16[11,2,32,256]{3,2,1,0:T(8,128)(2,1)S(1)} %collective-permute-done.7.refs_3_), channel_id=1, source_target_pairs={{0,2},{2,4},{4,6},{6,8},{8,10},{10,12},{12,14},{14,0},{16,30},{18,... | collective-permute-start | bytes 1081352 | tf_op jit(solution)/shard_map/ppermute | solution.py:68
  85.6 3.5 %collective-permute-start.11 = (bf16[10,2,32,256]{3,2,1,0:T(8,128)(2,1)S(1)}, bf16[10,2,32,256]{3,2,1,0:T(8,128)(2,1)S(1)}, u32[]{:S(2)}, u32[]{:S(2)}) collective-permute-start(bf16[10,2,32,256]{3,2,1,0:T(8,128)(2,1)S(1)} %collective-permute-done.8.refs_4_), channel_id=1, source_target_pairs={{0,2},{2,4},{4,6},{6,8},{8,10},{10,12},{12,14},{14,0},{16,30},{18,... | collective-permute-start | bytes 983048 | tf_op jit(solution)/shard_map/ppermute | solution.py:68
  89.1 0.4 put.8
  89.6 3.4 %collective-permute-start.12 = (bf16[11,2,32,256]{3,2,1,0:T(8,128)(2,1)S(1)}, bf16[11,2,32,256]{3,2,1,0:T(8,128)(2,1)S(1)}, u32[]{:S(2)}, u32[]{:S(2)}) collective-permute-start(bf16[11,2,32,256]{3,2,1,0:T(8,128)(2,1)S(1)} %collective-permute-done.9.refs_2_), channel_id=1, source_target_pairs={{0,2},{2,4},{4,6},{6,8},{8,10},{10,12},{12,14},{14,0},{16,30},{18,... | collective-permute-start | bytes 1081352 | tf_op jit(solution)/shard_map/ppermute | solution.py:68
  93.0 0.2 collective-permute-done.10.refs_3_
  93.1 3.7 %collective-permute-start.13 = (bf16[11,2,32,256]{3,2,1,0:T(8,128)(2,1)S(1)}, bf16[11,2,32,256]{3,2,1,0:T(8,128)(2,1)S(1)}, u32[]{:S(2)}, u32[]{:S(2)}) collective-permute-start(bf16[11,2,32,256]{3,2,1,0:T(8,128)(2,1)S(1)} %collective-permute-done.10.refs_3_), channel_id=1, source_target_pairs={{0,2},{2,4},{4,6},{6,8},{8,10},{10,12},{12,14},{14,0},{16,30},{18,... | collective-permute-start | bytes 1081352 | tf_op jit(solution)/shard_map/ppermute | solution.py:68
  96.8 3.5 %collective-permute-start.14 = (bf16[10,2,32,256]{3,2,1,0:T(8,128)(2,1)S(1)}, bf16[10,2,32,256]{3,2,1,0:T(8,128)(2,1)S(1)}, u32[]{:S(2)}, u32[]{:S(2)}) collective-permute-start(bf16[10,2,32,256]{3,2,1,0:T(8,128)(2,1)S(1)} %collective-permute-done.11.refs_4_), channel_id=1, source_target_pairs={{0,2},{2,4},{4,6},{6,8},{8,10},{10,12},{12,14},{14,0},{16,30},{18,... | collective-permute-start | bytes 983048 | tf_op jit(solution)/shard_map/ppermute | solution.py:68
  100.3 0.4 put.9
  100.8 3.4 %collective-permute-start.15 = (bf16[11,2,32,256]{3,2,1,0:T(8,128)(2,1)S(1)}, bf16[11,2,32,256]{3,2,1,0:T(8,128)(2,1)S(1)}, u32[]{:S(2)}, u32[]{:S(2)}) collective-permute-start(bf16[11,2,32,256]{3,2,1,0:T(8,128)(2,1)S(1)} %collective-permute-done.12.refs_2_), channel_id=1, source_target_pairs={{0,2},{2,4},{4,6},{6,8},{8,10},{10,12},{12,14},{14,0},{16,30},{18,... | collective-permute-start | bytes 1081352 | tf_op jit(solution)/shard_map/ppermute | solution.py:68
  104.2 0.2 collective-permute-done.13.refs_3_
  104.4 3.7 %collective-permute-start.16 = (bf16[11,2,32,256]{3,2,1,0:T(8,128)(2,1)S(1)}, bf16[11,2,32,256]{3,2,1,0:T(8,128)(2,1)S(1)}, u32[]{:S(2)}, u32[]{:S(2)}) collective-permute-start(bf16[11,2,32,256]{3,2,1,0:T(8,128)(2,1)S(1)} %collective-permute-done.13.refs_3_), channel_id=1, source_target_pairs={{0,2},{2,4},{4,6},{6,8},{8,10},{10,12},{12,14},{14,0},{16,30},{18,... | collective-permute-start | bytes 1081352 | tf_op jit(solution)/shard_map/ppermute | solution.py:68
  108.1 3.5 %collective-permute-start.17 = (bf16[10,2,32,256]{3,2,1,0:T(8,128)(2,1)S(1)}, bf16[10,2,32,256]{3,2,1,0:T(8,128)(2,1)S(1)}, u32[]{:S(2)}, u32[]{:S(2)}) collective-permute-start(bf16[10,2,32,256]{3,2,1,0:T(8,128)(2,1)S(1)} %collective-permute-done.14.refs_4_), channel_id=1, source_target_pairs={{0,2},{2,4},{4,6},{6,8},{8,10},{10,12},{12,14},{14,0},{16,30},{18,... | collective-permute-start | bytes 983048 | tf_op jit(solution)/shard_map/ppermute | solution.py:68
  111.6 0.0 copy-start
  111.6 0.4 put.10
  112.0 3.4 %collective-permute-start.18 = (bf16[11,2,32,256]{3,2,1,0:T(8,128)(2,1)S(1)}, bf16[11,2,32,256]{3,2,1,0:T(8,128)(2,1)S(1)}, u32[]{:S(2)}, u32[]{:S(2)}) collective-permute-start(bf16[11,2,32,256]{3,2,1,0:T(8,128)(2,1)S(1)} %collective-permute-done.15.refs_2_), channel_id=1, source_target_pairs={{0,2},{2,4},{4,6},{6,8},{8,10},{10,12},{12,14},{14,0},{16,30},{18,... | collective-permute-start | bytes 1081352 | tf_op jit(solution)/shard_map/ppermute | solution.py:68
  115.5 0.1 collective-permute-done.16.refs_3_
  115.6 3.7 %collective-permute-start.19 = (bf16[11,2,32,256]{3,2,1,0:T(8,128)(2,1)S(1)}, bf16[11,2,32,256]{3,2,1,0:T(8,128)(2,1)S(1)}, u32[]{:S(2)}, u32[]{:S(2)}) collective-permute-start(bf16[11,2,32,256]{3,2,1,0:T(8,128)(2,1)S(1)} %collective-permute-done.16.refs_3_), channel_id=1, source_target_pairs={{0,2},{2,4},{4,6},{6,8},{8,10},{10,12},{12,14},{14,0},{16,30},{18,... | collective-permute-start | bytes 1081352 | tf_op jit(solution)/shard_map/ppermute | solution.py:68
  119.3 3.5 %collective-permute-start.20 = (bf16[10,2,32,256]{3,2,1,0:T(8,128)(2,1)S(1)}, bf16[10,2,32,256]{3,2,1,0:T(8,128)(2,1)S(1)}, u32[]{:S(2)}, u32[]{:S(2)}) collective-permute-start(bf16[10,2,32,256]{3,2,1,0:T(8,128)(2,1)S(1)} %collective-permute-done.17.refs_4_), channel_id=1, source_target_pairs={{0,2},{2,4},{4,6},{6,8},{8,10},{10,12},{12,14},{14,0},{16,30},{18,... | collective-permute-start | bytes 983048 | tf_op jit(solution)/shard_map/ppermute | solution.py:68
  122.8 1.0 put.11
  123.9 3.0 %collective-permute-done.19.refs_2_ = bf16[11,2,32,256]{3,2,1,0:T(8,128)(2,1)S(1)} collective-permute-done((bf16[11,2,32,256]{3,2,1,0:T(8,128)(2,1)S(1)}, bf16[11,2,32,256]{3,2,1,0:T(8,128)(2,1)S(1)}, u32[]{:S(2)}, u32[]{:S(2)}) %collective-permute-start.19) | collective-permute-done | bytes 360480 | tf_op jit(solution)/shard_map/ppermute | solution.py:68
  126.8 3.0 %most.1 = (bf16[8,32,2,32,256]{4,3,2,1,0:T(8,128)(2,1)S(1)}, f32[17,2,128,128]{3,2,1,0:T(8,128)S(1)}) custom-call(s32[3]{0:T(128)S(1)} %pad_add_fusion.where, s32[2,17]{1,0:T(2,128)S(1)} %bitcast.11, bf16[8,32,2,32,256]{4,3,2,1,0:T(8,128)(2,1)S(1)} %get-tuple-element.57.refs_0_, ...), custom_call_target="tpu_custom_call", output_to_operand_aliasing={{0}: (2, {})} | custom-call | flops 1140850688 | bytes 10485760 | tf_op jit(solution)/shard_map/most/pallas_call | solution.py:128
  129.9 0.5 collective-permute-done.20.last
  130.4 2.3 %rest.1 = (bf16[8,32,2,32,256]{4,3,2,1,0:T(8,128)(2,1)S(1)}, f32[17,2,64,128]{3,2,1,0:T(8,128)S(1)}, s16[17,2,64,128]{3,2,1,0:T(8,128)(2,1)S(1)}, f32[17,2,128]{2,1,0:T(2,128)S(1)}) custom-call(s32[3]{0:T(128)S(1)} %pad_add_fusion.where, s32[2,17]{1,0:T(2,128)S(1)} %bitcast.12, ...), custom_call_target="tpu_custom_call", output_to_operand_aliasing={{0}: (2, {})} | custom-call | flops 1140850688 | bytes 10485760 | tf_op jit(solution)/shard_map/rest/pallas_call | solution.py:138
  132.6 2.5 %collective-permute-start.21 = (s16[17,2,64,128]{3,2,1,0:T(8,128)(2,1)S(1)}, s16[17,2,64,128]{3,2,1,0:T(8,128)(2,1)S(1)}, u32[]{:S(2)}, u32[]{:S(2)}) collective-permute-start(s16[17,2,64,128]{3,2,1,0:T(8,128)(2,1)S(1)} %get-tuple-element.61), channel_id=1, source_target_pairs={{0,1},{1,0},{2,3},{3,2},{4,5},{5,4},{6,7},{7,6},{8,9},{9,8},{10,11... | collective-permute-start | bytes 1671176 | tf_op jit(solution)/shard_map/ppermute | solution.py:160
  135.1 3.3 %collective-permute-start.22 = (f32[17,2,128]{2,1,0:T(2,128)S(1)}, f32[17,2,128]{2,1,0:T(2,128)S(1)}, u32[]{:S(2)}, u32[]{:S(2)}) collective-permute-start(f32[17,2,128]{2,1,0:T(2,128)S(1)} %get-tuple-element.62), channel_id=1, source_target_pairs={{0,1},{1,0},{2,3},{3,2},{4,5},{5,4},{6,7},{7,6},{8,9},{9,8},{10,11... | collective-permute-start | bytes 52232 | tf_op jit(solution)/shard_map/ppermute | solution.py:160
  138.5 8.5 %collective-permute-done.22 = f32[17,2,128]{2,1,0:T(2,128)S(1)} collective-permute-done((f32[17,2,128]{2,1,0:T(2,128)S(1)}, f32[17,2,128]{2,1,0:T(2,128)S(1)}, u32[]{:S(2)}, u32[]{:S(2)}) %collective-permute-start.22) | collective-permute-done | bytes 17440 | tf_op jit(solution)/shard_map/ppermute | solution.py:160
  147.0 1.2 add_bitcast_fusion
  (15 shorter events, 0.1 us)
Async XLA Ops:
  44.3 10.8 %collective-permute-start = (bf16[11,2,32,256]{3,2,1,0:T(8,128)(2,1)S(1)}, bf16[11,2,32,256]{3,2,1,0:T(8,128)(2,1)S(1)}, u32[]{:S(2)}, u32[]{:S(2)}) collective-permute-start(bf16[11,2,32,256]{3,2,1,0:T(8,128)(2,1)S(1)} %get-tuple-element.64.refs_0_), channel_id=1, source_target_pairs={{0,2},{2,4},{4,6},{6,8},{8,10},{10,12},{12,14},{14,0},{16,30},{18,... | collective-permute-start | bytes 1081352 | tf_op jit(solution)/shard_map/ppermute | solution.py:68
  47.8 11.7 %collective-permute-start.1 = (bf16[11,2,32,256]{3,2,1,0:T(8,128)(2,1)S(1)}, bf16[11,2,32,256]{3,2,1,0:T(8,128)(2,1)S(1)}, u32[]{:S(2)}, u32[]{:S(2)}) collective-permute-start(bf16[11,2,32,256]{3,2,1,0:T(8,128)(2,1)S(1)} %get-tuple-element.63.refs_1_), channel_id=1, source_target_pairs={{0,2},{2,4},{4,6},{6,8},{8,10},{10,12},{12,14},{14,0},{16,30},{18,... | collective-permute-start | bytes 1081352 | tf_op jit(solution)/shard_map/ppermute | solution.py:68
  51.4 11.1 %collective-permute-start.2 = (bf16[10,2,32,256]{3,2,1,0:T(8,128)(2,1)S(1)}, bf16[10,2,32,256]{3,2,1,0:T(8,128)(2,1)S(1)}, u32[]{:S(2)}, u32[]{:S(2)}) collective-permute-start(bf16[10,2,32,256]{3,2,1,0:T(8,128)(2,1)S(1)} %slice.14.refs_2_), channel_id=1, source_target_pairs={{0,2},{2,4},{4,6},{6,8},{8,10},{10,12},{12,14},{14,0},{16,30},{18,... | collective-permute-start | bytes 983048 | tf_op jit(solution)/shard_map/ppermute | solution.py:68
  55.1 11.2 %collective-permute-start.3 = (bf16[11,2,32,256]{3,2,1,0:T(8,128)(2,1)S(1)}, bf16[11,2,32,256]{3,2,1,0:T(8,128)(2,1)S(1)}, u32[]{:S(2)}, u32[]{:S(2)}) collective-permute-start(bf16[11,2,32,256]{3,2,1,0:T(8,128)(2,1)S(1)} %collective-permute-done.refs_3_), channel_id=1, source_target_pairs={{0,2},{2,4},{4,6},{6,8},{8,10},{10,12},{12,14},{14,0},{16,30},{18,... | collective-permute-start | bytes 1081352 | tf_op jit(solution)/shard_map/ppermute | solution.py:68
  59.6 11.4 %collective-permute-start.4 = (bf16[11,2,32,256]{3,2,1,0:T(8,128)(2,1)S(1)}, bf16[11,2,32,256]{3,2,1,0:T(8,128)(2,1)S(1)}, u32[]{:S(2)}, u32[]{:S(2)}) collective-permute-start(bf16[11,2,32,256]{3,2,1,0:T(8,128)(2,1)S(1)} %collective-permute-done.1.refs_4_), channel_id=1, source_target_pairs={{0,2},{2,4},{4,6},{6,8},{8,10},{10,12},{12,14},{14,0},{16,30},{18,... | collective-permute-start | bytes 1081352 | tf_op jit(solution)/shard_map/ppermute | solution.py:68
  62.5 12.3 %collective-permute-start.5 = (bf16[10,2,32,256]{3,2,1,0:T(8,128)(2,1)S(1)}, bf16[10,2,32,256]{3,2,1,0:T(8,128)(2,1)S(1)}, u32[]{:S(2)}, u32[]{:S(2)}) collective-permute-start(bf16[10,2,32,256]{3,2,1,0:T(8,128)(2,1)S(1)} %collective-permute-done.2.refs_5_), channel_id=1, source_target_pairs={{0,2},{2,4},{4,6},{6,8},{8,10},{10,12},{12,14},{14,0},{16,30},{18,... | collective-permute-start | bytes 983048 | tf_op jit(solution)/shard_map/ppermute | solution.py:68
  66.4 12.4 %collective-permute-start.6 = (bf16[11,2,32,256]{3,2,1,0:T(8,128)(2,1)S(1)}, bf16[11,2,32,256]{3,2,1,0:T(8,128)(2,1)S(1)}, u32[]{:S(2)}, u32[]{:S(2)}) collective-permute-start(bf16[11,2,32,256]{3,2,1,0:T(8,128)(2,1)S(1)} %collective-permute-done.3.refs_2_), channel_id=1, source_target_pairs={{0,2},{2,4},{4,6},{6,8},{8,10},{10,12},{12,14},{14,0},{16,30},{18,... | collective-permute-start | bytes 1081352 | tf_op jit(solution)/shard_map/ppermute | solution.py:68
  70.9 10.8 %collective-permute-start.7 = (bf16[11,2,32,256]{3,2,1,0:T(8,128)(2,1)S(1)}, bf16[11,2,32,256]{3,2,1,0:T(8,128)(2,1)S(1)}, u32[]{:S(2)}, u32[]{:S(2)}) collective-permute-start(bf16[11,2,32,256]{3,2,1,0:T(8,128)(2,1)S(1)} %collective-permute-done.4.refs_3_), channel_id=1, source_target_pairs={{0,2},{2,4},{4,6},{6,8},{8,10},{10,12},{12,14},{14,0},{16,30},{18,... | collective-permute-start | bytes 1081352 | tf_op jit(solution)/shard_map/ppermute | solution.py:68
  74.8 10.8 %collective-permute-start.8 = (bf16[10,2,32,256]{3,2,1,0:T(8,128)(2,1)S(1)}, bf16[10,2,32,256]{3,2,1,0:T(8,128)(2,1)S(1)}, u32[]{:S(2)}, u32[]{:S(2)}) collective-permute-start(bf16[10,2,32,256]{3,2,1,0:T(8,128)(2,1)S(1)} %collective-permute-done.5.refs_4_), channel_id=1, source_target_pairs={{0,2},{2,4},{4,6},{6,8},{8,10},{10,12},{12,14},{14,0},{16,30},{18,... | collective-permute-start | bytes 983048 | tf_op jit(solution)/shard_map/ppermute | solution.py:68
  78.7 10.8 %collective-permute-start.9 = (bf16[11,2,32,256]{3,2,1,0:T(8,128)(2,1)S(1)}, bf16[11,2,32,256]{3,2,1,0:T(8,128)(2,1)S(1)}, u32[]{:S(2)}, u32[]{:S(2)}) collective-permute-start(bf16[11,2,32,256]{3,2,1,0:T(8,128)(2,1)S(1)} %collective-permute-done.6.refs_2_), channel_id=1, source_target_pairs={{0,2},{2,4},{4,6},{6,8},{8,10},{10,12},{12,14},{14,0},{16,30},{18,... | collective-permute-start | bytes 1081352 | tf_op jit(solution)/shard_map/ppermute | solution.py:68
  81.8 11.4 %collective-permute-start.10 = (bf16[11,2,32,256]{3,2,1,0:T(8,128)(2,1)S(1)}, bf16[11,2,32,256]{3,2,1,0:T(8,128)(2,1)S(1)}, u32[]{:S(2)}, u32[]{:S(2)}) collective-permute-start(bf16[11,2,32,256]{3,2,1,0:T(8,128)(2,1)S(1)} %collective-permute-done.7.refs_3_), channel_id=1, source_target_pairs={{0,2},{2,4},{4,6},{6,8},{8,10},{10,12},{12,14},{14,0},{16,30},{18,... | collective-permute-start | bytes 1081352 | tf_op jit(solution)/shard_map/ppermute | solution.py:68
  85.6 11.2 %collective-permute-start.11 = (bf16[10,2,32,256]{3,2,1,0:T(8,128)(2,1)S(1)}, bf16[10,2,32,256]{3,2,1,0:T(8,128)(2,1)S(1)}, u32[]{:S(2)}, u32[]{:S(2)}) collective-permute-start(bf16[10,2,32,256]{3,2,1,0:T(8,128)(2,1)S(1)} %collective-permute-done.8.refs_4_), channel_id=1, source_target_pairs={{0,2},{2,4},{4,6},{6,8},{8,10},{10,12},{12,14},{14,0},{16,30},{18,... | collective-permute-start | bytes 983048 | tf_op jit(solution)/shard_map/ppermute | solution.py:68
  89.6 11.2 %collective-permute-start.12 = (bf16[11,2,32,256]{3,2,1,0:T(8,128)(2,1)S(1)}, bf16[11,2,32,256]{3,2,1,0:T(8,128)(2,1)S(1)}, u32[]{:S(2)}, u32[]{:S(2)}) collective-permute-start(bf16[11,2,32,256]{3,2,1,0:T(8,128)(2,1)S(1)} %collective-permute-done.9.refs_2_), channel_id=1, source_target_pairs={{0,2},{2,4},{4,6},{6,8},{8,10},{10,12},{12,14},{14,0},{16,30},{18,... | collective-permute-start | bytes 1081352 | tf_op jit(solution)/shard_map/ppermute | solution.py:68
  93.1 11.2 %collective-permute-start.13 = (bf16[11,2,32,256]{3,2,1,0:T(8,128)(2,1)S(1)}, bf16[11,2,32,256]{3,2,1,0:T(8,128)(2,1)S(1)}, u32[]{:S(2)}, u32[]{:S(2)}) collective-permute-start(bf16[11,2,32,256]{3,2,1,0:T(8,128)(2,1)S(1)} %collective-permute-done.10.refs_3_), channel_id=1, source_target_pairs={{0,2},{2,4},{4,6},{6,8},{8,10},{10,12},{12,14},{14,0},{16,30},{18,... | collective-permute-start | bytes 1081352 | tf_op jit(solution)/shard_map/ppermute | solution.py:68
  96.8 11.2 %collective-permute-start.14 = (bf16[10,2,32,256]{3,2,1,0:T(8,128)(2,1)S(1)}, bf16[10,2,32,256]{3,2,1,0:T(8,128)(2,1)S(1)}, u32[]{:S(2)}, u32[]{:S(2)}) collective-permute-start(bf16[10,2,32,256]{3,2,1,0:T(8,128)(2,1)S(1)} %collective-permute-done.11.refs_4_), channel_id=1, source_target_pairs={{0,2},{2,4},{4,6},{6,8},{8,10},{10,12},{12,14},{14,0},{16,30},{18,... | collective-permute-start | bytes 983048 | tf_op jit(solution)/shard_map/ppermute | solution.py:68
  100.8 11.2 %collective-permute-start.15 = (bf16[11,2,32,256]{3,2,1,0:T(8,128)(2,1)S(1)}, bf16[11,2,32,256]{3,2,1,0:T(8,128)(2,1)S(1)}, u32[]{:S(2)}, u32[]{:S(2)}) collective-permute-start(bf16[11,2,32,256]{3,2,1,0:T(8,128)(2,1)S(1)} %collective-permute-done.12.refs_2_), channel_id=1, source_target_pairs={{0,2},{2,4},{4,6},{6,8},{8,10},{10,12},{12,14},{14,0},{16,30},{18,... | collective-permute-start | bytes 1081352 | tf_op jit(solution)/shard_map/ppermute | solution.py:68
  104.4 11.2 %collective-permute-start.16 = (bf16[11,2,32,256]{3,2,1,0:T(8,128)(2,1)S(1)}, bf16[11,2,32,256]{3,2,1,0:T(8,128)(2,1)S(1)}, u32[]{:S(2)}, u32[]{:S(2)}) collective-permute-start(bf16[11,2,32,256]{3,2,1,0:T(8,128)(2,1)S(1)} %collective-permute-done.13.refs_3_), channel_id=1, source_target_pairs={{0,2},{2,4},{4,6},{6,8},{8,10},{10,12},{12,14},{14,0},{16,30},{18,... | collective-permute-start | bytes 1081352 | tf_op jit(solution)/shard_map/ppermute | solution.py:68
  108.1 11.2 %collective-permute-start.17 = (bf16[10,2,32,256]{3,2,1,0:T(8,128)(2,1)S(1)}, bf16[10,2,32,256]{3,2,1,0:T(8,128)(2,1)S(1)}, u32[]{:S(2)}, u32[]{:S(2)}) collective-permute-start(bf16[10,2,32,256]{3,2,1,0:T(8,128)(2,1)S(1)} %collective-permute-done.14.refs_4_), channel_id=1, source_target_pairs={{0,2},{2,4},{4,6},{6,8},{8,10},{10,12},{12,14},{14,0},{16,30},{18,... | collective-permute-start | bytes 983048 | tf_op jit(solution)/shard_map/ppermute | solution.py:68
  111.6 15.3 %copy-start = (s32[17,2]{0,1:T(2,128)S(1)}, s32[17,2]{0,1:T(2,128)}, u32[]{:S(2)}) copy-start(s32[17,2]{0,1:T(2,128)} %param.3) | copy-start | bytes 412
  112.0 11.8 %collective-permute-start.18 = (bf16[11,2,32,256]{3,2,1,0:T(8,128)(2,1)S(1)}, bf16[11,2,32,256]{3,2,1,0:T(8,128)(2,1)S(1)}, u32[]{:S(2)}, u32[]{:S(2)}) collective-permute-start(bf16[11,2,32,256]{3,2,1,0:T(8,128)(2,1)S(1)} %collective-permute-done.15.refs_2_), channel_id=1, source_target_pairs={{0,2},{2,4},{4,6},{6,8},{8,10},{10,12},{12,14},{14,0},{16,30},{18,... | collective-permute-start | bytes 1081352 | tf_op jit(solution)/shard_map/ppermute | solution.py:68
  115.6 11.2 %collective-permute-start.19 = (bf16[11,2,32,256]{3,2,1,0:T(8,128)(2,1)S(1)}, bf16[11,2,32,256]{3,2,1,0:T(8,128)(2,1)S(1)}, u32[]{:S(2)}, u32[]{:S(2)}) collective-permute-start(bf16[11,2,32,256]{3,2,1,0:T(8,128)(2,1)S(1)} %collective-permute-done.16.refs_3_), channel_id=1, source_target_pairs={{0,2},{2,4},{4,6},{6,8},{8,10},{10,12},{12,14},{14,0},{16,30},{18,... | collective-permute-start | bytes 1081352 | tf_op jit(solution)/shard_map/ppermute | solution.py:68
  119.3 11.0 %collective-permute-start.20 = (bf16[10,2,32,256]{3,2,1,0:T(8,128)(2,1)S(1)}, bf16[10,2,32,256]{3,2,1,0:T(8,128)(2,1)S(1)}, u32[]{:S(2)}, u32[]{:S(2)}) collective-permute-start(bf16[10,2,32,256]{3,2,1,0:T(8,128)(2,1)S(1)} %collective-permute-done.17.refs_4_), channel_id=1, source_target_pairs={{0,2},{2,4},{4,6},{6,8},{8,10},{10,12},{12,14},{14,0},{16,30},{18,... | collective-permute-start | bytes 983048 | tf_op jit(solution)/shard_map/ppermute | solution.py:68
  132.6 14.4 %collective-permute-start.21 = (s16[17,2,64,128]{3,2,1,0:T(8,128)(2,1)S(1)}, s16[17,2,64,128]{3,2,1,0:T(8,128)(2,1)S(1)}, u32[]{:S(2)}, u32[]{:S(2)}) collective-permute-start(s16[17,2,64,128]{3,2,1,0:T(8,128)(2,1)S(1)} %get-tuple-element.61), channel_id=1, source_target_pairs={{0,1},{1,0},{2,3},{3,2},{4,5},{5,4},{6,7},{7,6},{8,9},{9,8},{10,11... | collective-permute-start | bytes 1671176 | tf_op jit(solution)/shard_map/ppermute | solution.py:160
  135.1 11.9 %collective-permute-start.22 = (f32[17,2,128]{2,1,0:T(2,128)S(1)}, f32[17,2,128]{2,1,0:T(2,128)S(1)}, u32[]{:S(2)}, u32[]{:S(2)}) collective-permute-start(f32[17,2,128]{2,1,0:T(2,128)S(1)} %get-tuple-element.62), channel_id=1, source_target_pairs={{0,1},{1,0},{2,3},{3,2},{4,5},{5,4},{6,7},{7,6},{8,9},{9,8},{10,11... | collective-permute-start | bytes 52232 | tf_op jit(solution)/shard_map/ppermute | solution.py:160

commit v5 on v4

--- a/solution.py
+++ b/solution.py
@@ -97,17 +97,19 @@
     lax.fori_loop(0, table.shape[1], tile, 0, unroll=True)
 
 
-def rest_kernel(where, table, _, total, last, held, keep, send, scale, whole, arrived):
+def rest_kernel(where, table, _, total, last, held, keep, send, scale):
     half = BLOCK // 2
     sources = pl.ds(sum(CHAINS[:-1]), CHAINS[-1])
-    run([pltpu.make_async_copy(last, held.at[7, sources], arrived)])
+    held[7, sources] = last[...]
 
     def tile(k, carry):
         real, imag = products(where, table, held, sources, k)
-        whole[0] = (total[k, 0] + real) * (1.0 / TIME)
-        whole[1] = (total[k, 1] + imag) * (1.0 / TIME)
-        keep[k] = whole[:, pl.ds(pl.multiple_of(where[1] * half, half), half), :]
-        other = whole[:, pl.ds(pl.multiple_of((1 - where[1]) * half, half), half), :]
+        parts = [(total[k, i] + part) * (1.0 / TIME) for i, part in enumerate((real, imag))]
+        top = jnp.stack([part[:half] for part in parts])
+        bottom = jnp.stack([part[half:] for part in parts])
+        mine_is_top = where[1] == 0
+        keep[k] = jnp.where(mine_is_top, top, bottom)
+        other = jnp.where(mine_is_top, bottom, top)
         most = jnp.max(jnp.abs(other), axis=1, keepdims=True)
         scale[k] = most[:, 0]
         send[k] = jnp.round(other * jnp.where(most > 0, 1.0 / most, 0.0) * STEPS).astype(jnp.int32).astype(jnp.int16)
@@ -143,9 +145,8 @@
             jax.ShapeDtypeStruct(part.shape, jnp.int16),
             jax.ShapeDtypeStruct((count, 2, BLOCK), jnp.float32),
         ),
-        in_specs=[smem, smem, vmem, vmem, any_],
+        in_specs=[smem, smem, vmem, vmem, vmem],
         out_specs=(vmem, vmem, vmem, vmem),
-        scratch_shapes=[pltpu.VMEM((2, BLOCK, BLOCK), jnp.float32), pltpu.SemaphoreType.DMA],
         name="rest",
         **options,
     )(where, table, held, total, last[-1])

time: 149 us -> 149 us (level)
  no operation moved by 1% of the time
where the time goes in v5:
time: 149 us; the launch traced here: 148 us
  starting transfers between devices  79.6 us (53%)
  blocking collectives  42.9 us (29%)
  waiting for transfers between devices  13.8 us (9%)
  Pallas kernels  8.69 us (6%)
    ppermute x21, starting transfers between devices, rings(): passed = [lax.ppermute(piece, ('chan', 'pair'), ROUND) for piece in now]  73.8 us
    all_to_all x1, blocking collectives, body(): lax.all_to_all(ordered, 'chan', split_axis=0, concat_axis=0, tiled=True)  42.9 us
    ppermute x2, waiting for transfers between devices, body(): lax.ppermute(half, 'integ', [(0, 1), (1, 0)])  8.52 us
    ppermute x2, starting transfers between devices, body(): lax.ppermute(half, 'integ', [(0, 1), (1, 0)])  5.84 us
    ppermute x21, waiting for transfers between devices, rings(): passed = [lax.ppermute(piece, ('chan', 'pair'), ROUND) for piece in now]  5.27 us
    pallas_call x6, Pallas kernels, put(): pl.pallas_call(lambda *refs: put_kernel(steps, *refs), out_shape=(jax.Sha...  3.56 us
    pallas_call x1, Pallas kernels, tiles(): pl.pallas_call(most_kernel, out_shape=(blocks, jax.ShapeDtypeStruct((coun...  3.02 us
  transfers between devices with their start and end apart: 23, of which 9 were waited for; matrix products, arithmetic and copies ran while one was open for 0% of the time, Pallas kernels for 4%

profile of v5, /device:TPU:64, one launch (start us, length us, event | category | flops | bytes accessed | tf_op | source)
XLA Modules:
  0.0 148.1 jit_solution(14782325252996919376)
XLA Ops:
  0.0 1.3 copy.13
  1.3 0.1 pad_add_fusion.where
  1.4 42.9 %all_to_all.5 = bf16[32,2,32,256]{3,2,1,0:T(8,128)(2,1)S(1)} all-to-all(bf16[32,2,32,256]{3,2,1,0:T(8,128)(2,1)S(1)} %bitcast.13), channel_id=1, replica_groups=mesh['chan'=32,'pair'=8,'integ'=2] {'chan'}, dimensions={0} | all-to-all | bytes 2097152 | tf_op jit(solution)/shard_map/all_to_all | solution.py:159
  44.3 0.1 fusion
  44.3 3.5 %collective-permute-start = (bf16[11,2,32,256]{3,2,1,0:T(8,128)(2,1)S(1)}, bf16[11,2,32,256]{3,2,1,0:T(8,128)(2,1)S(1)}, u32[]{:S(2)}, u32[]{:S(2)}) collective-permute-start(bf16[11,2,32,256]{3,2,1,0:T(8,128)(2,1)S(1)} %get-tuple-element.64.refs_0_), channel_id=1, source_target_pairs={{0,2},{2,4},{4,6},{6,8},{8,10},{10,12},{12,14},{14,0},{16,30},{18,... | collective-permute-start | bytes 1081352 | tf_op jit(solution)/shard_map/ppermute | solution.py:68
  47.8 3.5 %collective-permute-start.1 = (bf16[11,2,32,256]{3,2,1,0:T(8,128)(2,1)S(1)}, bf16[11,2,32,256]{3,2,1,0:T(8,128)(2,1)S(1)}, u32[]{:S(2)}, u32[]{:S(2)}) collective-permute-start(bf16[11,2,32,256]{3,2,1,0:T(8,128)(2,1)S(1)} %get-tuple-element.63.refs_1_), channel_id=1, source_target_pairs={{0,2},{2,4},{4,6},{6,8},{8,10},{10,12},{12,14},{14,0},{16,30},{18,... | collective-permute-start | bytes 1081352 | tf_op jit(solution)/shard_map/ppermute | solution.py:68
  51.4 3.5 %collective-permute-start.2 = (bf16[10,2,32,256]{3,2,1,0:T(8,128)(2,1)S(1)}, bf16[10,2,32,256]{3,2,1,0:T(8,128)(2,1)S(1)}, u32[]{:S(2)}, u32[]{:S(2)}) collective-permute-start(bf16[10,2,32,256]{3,2,1,0:T(8,128)(2,1)S(1)} %slice.14.refs_2_), channel_id=1, source_target_pairs={{0,2},{2,4},{4,6},{6,8},{8,10},{10,12},{12,14},{14,0},{16,30},{18,... | collective-permute-start | bytes 983048 | tf_op jit(solution)/shard_map/ppermute | solution.py:68
  54.8 0.3 collective-permute-done.refs_3_
  55.1 4.4 %collective-permute-start.3 = (bf16[11,2,32,256]{3,2,1,0:T(8,128)(2,1)S(1)}, bf16[11,2,32,256]{3,2,1,0:T(8,128)(2,1)S(1)}, u32[]{:S(2)}, u32[]{:S(2)}) collective-permute-start(bf16[11,2,32,256]{3,2,1,0:T(8,128)(2,1)S(1)} %collective-permute-done.refs_3_), channel_id=1, source_target_pairs={{0,2},{2,4},{4,6},{6,8},{8,10},{10,12},{12,14},{14,0},{16,30},{18,... | collective-permute-start | bytes 1081352 | tf_op jit(solution)/shard_map/ppermute | solution.py:68
  59.6 0.0 collective-permute-done.1.refs_4_
  59.6 2.6 %collective-permute-start.4 = (bf16[11,2,32,256]{3,2,1,0:T(8,128)(2,1)S(1)}, bf16[11,2,32,256]{3,2,1,0:T(8,128)(2,1)S(1)}, u32[]{:S(2)}, u32[]{:S(2)}) collective-permute-start(bf16[11,2,32,256]{3,2,1,0:T(8,128)(2,1)S(1)} %collective-permute-done.1.refs_4_), channel_id=1, source_target_pairs={{0,2},{2,4},{4,6},{6,8},{8,10},{10,12},{12,14},{14,0},{16,30},{18,... | collective-permute-start | bytes 1081352 | tf_op jit(solution)/shard_map/ppermute | solution.py:68
  62.2 0.3 collective-permute-done.2.refs_5_
  62.5 2.3 %collective-permute-start.5 = (bf16[10,2,32,256]{3,2,1,0:T(8,128)(2,1)S(1)}, bf16[10,2,32,256]{3,2,1,0:T(8,128)(2,1)S(1)}, u32[]{:S(2)}, u32[]{:S(2)}) collective-permute-start(bf16[10,2,32,256]{3,2,1,0:T(8,128)(2,1)S(1)} %collective-permute-done.2.refs_5_), channel_id=1, source_target_pairs={{0,2},{2,4},{4,6},{6,8},{8,10},{10,12},{12,14},{14,0},{16,30},{18,... | collective-permute-start | bytes 983048 | tf_op jit(solution)/shard_map/ppermute | solution.py:68
  64.8 0.8 put.6
  65.6 0.7 collective-permute-done.3.refs_2_
  66.4 4.6 %collective-permute-start.6 = (bf16[11,2,32,256]{3,2,1,0:T(8,128)(2,1)S(1)}, bf16[11,2,32,256]{3,2,1,0:T(8,128)(2,1)S(1)}, u32[]{:S(2)}, u32[]{:S(2)}) collective-permute-start(bf16[11,2,32,256]{3,2,1,0:T(8,128)(2,1)S(1)} %collective-permute-done.3.refs_2_), channel_id=1, source_target_pairs={{0,2},{2,4},{4,6},{6,8},{8,10},{10,12},{12,14},{14,0},{16,30},{18,... | collective-permute-start | bytes 1081352 | tf_op jit(solution)/shard_map/ppermute | solution.py:68
  70.9 3.8 %collective-permute-start.7 = (bf16[11,2,32,256]{3,2,1,0:T(8,128)(2,1)S(1)}, bf16[11,2,32,256]{3,2,1,0:T(8,128)(2,1)S(1)}, u32[]{:S(2)}, u32[]{:S(2)}) collective-permute-start(bf16[11,2,32,256]{3,2,1,0:T(8,128)(2,1)S(1)} %collective-permute-done.4.refs_3_), channel_id=1, source_target_pairs={{0,2},{2,4},{4,6},{6,8},{8,10},{10,12},{12,14},{14,0},{16,30},{18,... | collective-permute-start | bytes 1081352 | tf_op jit(solution)/shard_map/ppermute | solution.py:68
  74.8 3.5 %collective-permute-start.8 = (bf16[10,2,32,256]{3,2,1,0:T(8,128)(2,1)S(1)}, bf16[10,2,32,256]{3,2,1,0:T(8,128)(2,1)S(1)}, u32[]{:S(2)}, u32[]{:S(2)}) collective-permute-start(bf16[10,2,32,256]{3,2,1,0:T(8,128)(2,1)S(1)} %collective-permute-done.5.refs_4_), channel_id=1, source_target_pairs={{0,2},{2,4},{4,6},{6,8},{8,10},{10,12},{12,14},{14,0},{16,30},{18,... | collective-permute-start | bytes 983048 | tf_op jit(solution)/shard_map/ppermute | solution.py:68
  78.3 0.4 put.7
  78.7 0.0 collective-permute-done.6.refs_2_
  78.7 3.0 %collective-permute-start.9 = (bf16[11,2,32,256]{3,2,1,0:T(8,128)(2,1)S(1)}, bf16[11,2,32,256]{3,2,1,0:T(8,128)(2,1)S(1)}, u32[]{:S(2)}, u32[]{:S(2)}) collective-permute-start(bf16[11,2,32,256]{3,2,1,0:T(8,128)(2,1)S(1)} %collective-permute-done.6.refs_2_), channel_id=1, source_target_pairs={{0,2},{2,4},{4,6},{6,8},{8,10},{10,12},{12,14},{14,0},{16,30},{18,... | collective-permute-start | bytes 1081352 | tf_op jit(solution)/shard_map/ppermute | solution.py:68
  81.8 3.8 %collective-permute-start.10 = (bf16[11,2,32,256]{3,2,1,0:T(8,128)(2,1)S(1)}, bf16[11,2,32,256]{3,2,1,0:T(8,128)(2,1)S(1)}, u32[]{:S(2)}, u32[]{:S(2)}) collective-permute-start(bf16[11,2,32,256]{3,2,1,0:T(8,128)(2,1)S(1)} %collective-permute-done.7.refs_3_), channel_id=1, source_target_pairs={{0,2},{2,4},{4,6},{6,8},{8,10},{10,12},{12,14},{14,0},{16,30},{18,... | collective-permute-start | bytes 1081352 | tf_op jit(solution)/shard_map/ppermute | solution.py:68
  85.6 3.5 %collective-permute-start.11 = (bf16[10,2,32,256]{3,2,1,0:T(8,128)(2,1)S(1)}, bf16[10,2,32,256]{3,2,1,0:T(8,128)(2,1)S(1)}, u32[]{:S(2)}, u32[]{:S(2)}) collective-permute-start(bf16[10,2,32,256]{3,2,1,0:T(8,128)(2,1)S(1)} %collective-permute-done.8.refs_4_), channel_id=1, source_target_pairs={{0,2},{2,4},{4,6},{6,8},{8,10},{10,12},{12,14},{14,0},{16,30},{18,... | collective-permute-start | bytes 983048 | tf_op jit(solution)/shard_map/ppermute | solution.py:68
  89.1 0.4 put.8
  89.6 3.4 %collective-permute-start.12 = (bf16[11,2,32,256]{3,2,1,0:T(8,128)(2,1)S(1)}, bf16[11,2,32,256]{3,2,1,0:T(8,128)(2,1)S(1)}, u32[]{:S(2)}, u32[]{:S(2)}) collective-permute-start(bf16[11,2,32,256]{3,2,1,0:T(8,128)(2,1)S(1)} %collective-permute-done.9.refs_2_), channel_id=1, source_target_pairs={{0,2},{2,4},{4,6},{6,8},{8,10},{10,12},{12,14},{14,0},{16,30},{18,... | collective-permute-start | bytes 1081352 | tf_op jit(solution)/shard_map/ppermute | solution.py:68
  93.0 0.2 collective-permute-done.10.refs_3_
  93.1 3.7 %collective-permute-start.13 = (bf16[11,2,32,256]{3,2,1,0:T(8,128)(2,1)S(1)}, bf16[11,2,32,256]{3,2,1,0:T(8,128)(2,1)S(1)}, u32[]{:S(2)}, u32[]{:S(2)}) collective-permute-start(bf16[11,2,32,256]{3,2,1,0:T(8,128)(2,1)S(1)} %collective-permute-done.10.refs_3_), channel_id=1, source_target_pairs={{0,2},{2,4},{4,6},{6,8},{8,10},{10,12},{12,14},{14,0},{16,30},{18,... | collective-permute-start | bytes 1081352 | tf_op jit(solution)/shard_map/ppermute | solution.py:68
  96.8 3.5 %collective-permute-start.14 = (bf16[10,2,32,256]{3,2,1,0:T(8,128)(2,1)S(1)}, bf16[10,2,32,256]{3,2,1,0:T(8,128)(2,1)S(1)}, u32[]{:S(2)}, u32[]{:S(2)}) collective-permute-start(bf16[10,2,32,256]{3,2,1,0:T(8,128)(2,1)S(1)} %collective-permute-done.11.refs_4_), channel_id=1, source_target_pairs={{0,2},{2,4},{4,6},{6,8},{8,10},{10,12},{12,14},{14,0},{16,30},{18,... | collective-permute-start | bytes 983048 | tf_op jit(solution)/shard_map/ppermute | solution.py:68
  100.3 0.4 put.9
  100.8 3.4 %collective-permute-start.15 = (bf16[11,2,32,256]{3,2,1,0:T(8,128)(2,1)S(1)}, bf16[11,2,32,256]{3,2,1,0:T(8,128)(2,1)S(1)}, u32[]{:S(2)}, u32[]{:S(2)}) collective-permute-start(bf16[11,2,32,256]{3,2,1,0:T(8,128)(2,1)S(1)} %collective-permute-done.12.refs_2_), channel_id=1, source_target_pairs={{0,2},{2,4},{4,6},{6,8},{8,10},{10,12},{12,14},{14,0},{16,30},{18,... | collective-permute-start | bytes 1081352 | tf_op jit(solution)/shard_map/ppermute | solution.py:68
  104.2 0.2 collective-permute-done.13.refs_3_
  104.4 3.7 %collective-permute-start.16 = (bf16[11,2,32,256]{3,2,1,0:T(8,128)(2,1)S(1)}, bf16[11,2,32,256]{3,2,1,0:T(8,128)(2,1)S(1)}, u32[]{:S(2)}, u32[]{:S(2)}) collective-permute-start(bf16[11,2,32,256]{3,2,1,0:T(8,128)(2,1)S(1)} %collective-permute-done.13.refs_3_), channel_id=1, source_target_pairs={{0,2},{2,4},{4,6},{6,8},{8,10},{10,12},{12,14},{14,0},{16,30},{18,... | collective-permute-start | bytes 1081352 | tf_op jit(solution)/shard_map/ppermute | solution.py:68
  108.1 3.5 %collective-permute-start.17 = (bf16[10,2,32,256]{3,2,1,0:T(8,128)(2,1)S(1)}, bf16[10,2,32,256]{3,2,1,0:T(8,128)(2,1)S(1)}, u32[]{:S(2)}, u32[]{:S(2)}) collective-permute-start(bf16[10,2,32,256]{3,2,1,0:T(8,128)(2,1)S(1)} %collective-permute-done.14.refs_4_), channel_id=1, source_target_pairs={{0,2},{2,4},{4,6},{6,8},{8,10},{10,12},{12,14},{14,0},{16,30},{18,... | collective-permute-start | bytes 983048 | tf_op jit(solution)/shard_map/ppermute | solution.py:68
  111.6 0.0 copy-start
  111.6 0.4 put.10
  112.0 3.4 %collective-permute-start.18 = (bf16[11,2,32,256]{3,2,1,0:T(8,128)(2,1)S(1)}, bf16[11,2,32,256]{3,2,1,0:T(8,128)(2,1)S(1)}, u32[]{:S(2)}, u32[]{:S(2)}) collective-permute-start(bf16[11,2,32,256]{3,2,1,0:T(8,128)(2,1)S(1)} %collective-permute-done.15.refs_2_), channel_id=1, source_target_pairs={{0,2},{2,4},{4,6},{6,8},{8,10},{10,12},{12,14},{14,0},{16,30},{18,... | collective-permute-start | bytes 1081352 | tf_op jit(solution)/shard_map/ppermute | solution.py:68
  115.5 0.1 collective-permute-done.16.refs_3_
  115.6 3.7 %collective-permute-start.19 = (bf16[11,2,32,256]{3,2,1,0:T(8,128)(2,1)S(1)}, bf16[11,2,32,256]{3,2,1,0:T(8,128)(2,1)S(1)}, u32[]{:S(2)}, u32[]{:S(2)}) collective-permute-start(bf16[11,2,32,256]{3,2,1,0:T(8,128)(2,1)S(1)} %collective-permute-done.16.refs_3_), channel_id=1, source_target_pairs={{0,2},{2,4},{4,6},{6,8},{8,10},{10,12},{12,14},{14,0},{16,30},{18,... | collective-permute-start | bytes 1081352 | tf_op jit(solution)/shard_map/ppermute | solution.py:68
  119.3 3.5 %collective-permute-start.20 = (bf16[10,2,32,256]{3,2,1,0:T(8,128)(2,1)S(1)}, bf16[10,2,32,256]{3,2,1,0:T(8,128)(2,1)S(1)}, u32[]{:S(2)}, u32[]{:S(2)}) collective-permute-start(bf16[10,2,32,256]{3,2,1,0:T(8,128)(2,1)S(1)} %collective-permute-done.17.refs_4_), channel_id=1, source_target_pairs={{0,2},{2,4},{4,6},{6,8},{8,10},{10,12},{12,14},{14,0},{16,30},{18,... | collective-permute-start | bytes 983048 | tf_op jit(solution)/shard_map/ppermute | solution.py:68
  122.8 1.0 put.11
  123.9 3.0 %collective-permute-done.19.refs_2_ = bf16[11,2,32,256]{3,2,1,0:T(8,128)(2,1)S(1)} collective-permute-done((bf16[11,2,32,256]{3,2,1,0:T(8,128)(2,1)S(1)}, bf16[11,2,32,256]{3,2,1,0:T(8,128)(2,1)S(1)}, u32[]{:S(2)}, u32[]{:S(2)}) %collective-permute-start.19) | collective-permute-done | bytes 360480 | tf_op jit(solution)/shard_map/ppermute | solution.py:68
  126.8 3.0 %most.1 = (bf16[8,32,2,32,256]{4,3,2,1,0:T(8,128)(2,1)S(1)}, f32[17,2,128,128]{3,2,1,0:T(8,128)S(1)}) custom-call(s32[3]{0:T(128)S(1)} %pad_add_fusion.where, s32[2,17]{1,0:T(2,128)S(1)} %bitcast.11, bf16[8,32,2,32,256]{4,3,2,1,0:T(8,128)(2,1)S(1)} %get-tuple-element.57.refs_0_, ...), custom_call_target="tpu_custom_call", output_to_operand_aliasing={{0}: (2, {})} | custom-call | flops 1140850688 | bytes 10485760 | tf_op jit(solution)/shard_map/most/pallas_call | solution.py:130
  129.9 0.5 collective-permute-done.20.last
  130.4 2.1 %rest.1 = (bf16[8,32,2,32,256]{4,3,2,1,0:T(8,128)(2,1)S(1)}, f32[17,2,64,128]{3,2,1,0:T(8,128)S(1)}, s16[17,2,64,128]{3,2,1,0:T(8,128)(2,1)S(1)}, f32[17,2,128]{2,1,0:T(2,128)S(1)}) custom-call(s32[3]{0:T(128)S(1)} %pad_add_fusion.where, s32[2,17]{1,0:T(2,128)S(1)} %bitcast.12, ...), custom_call_target="tpu_custom_call", output_to_operand_aliasing={{0}: (2, {})} | custom-call | flops 1140850688 | bytes 10485760 | tf_op jit(solution)/shard_map/rest/pallas_call | solution.py:140
  132.5 2.5 %collective-permute-start.21 = (s16[17,2,64,128]{3,2,1,0:T(8,128)(2,1)S(1)}, s16[17,2,64,128]{3,2,1,0:T(8,128)(2,1)S(1)}, u32[]{:S(2)}, u32[]{:S(2)}) collective-permute-start(s16[17,2,64,128]{3,2,1,0:T(8,128)(2,1)S(1)} %get-tuple-element.61), channel_id=1, source_target_pairs={{0,1},{1,0},{2,3},{3,2},{4,5},{5,4},{6,7},{7,6},{8,9},{9,8},{10,11... | collective-permute-start | bytes 1671176 | tf_op jit(solution)/shard_map/ppermute | solution.py:161
  135.0 3.3 %collective-permute-start.22 = (f32[17,2,128]{2,1,0:T(2,128)S(1)}, f32[17,2,128]{2,1,0:T(2,128)S(1)}, u32[]{:S(2)}, u32[]{:S(2)}) collective-permute-start(f32[17,2,128]{2,1,0:T(2,128)S(1)} %get-tuple-element.62), channel_id=1, source_target_pairs={{0,1},{1,0},{2,3},{3,2},{4,5},{5,4},{6,7},{7,6},{8,9},{9,8},{10,11... | collective-permute-start | bytes 52232 | tf_op jit(solution)/shard_map/ppermute | solution.py:161
  138.3 8.5 %collective-permute-done.22 = f32[17,2,128]{2,1,0:T(2,128)S(1)} collective-permute-done((f32[17,2,128]{2,1,0:T(2,128)S(1)}, f32[17,2,128]{2,1,0:T(2,128)S(1)}, u32[]{:S(2)}, u32[]{:S(2)}) %collective-permute-start.22) | collective-permute-done | bytes 17440 | tf_op jit(solution)/shard_map/ppermute | solution.py:161
  146.9 1.2 add_bitcast_fusion
  (15 shorter events, 0.1 us)
Async XLA Ops:
  44.3 10.8 %collective-permute-start = (bf16[11,2,32,256]{3,2,1,0:T(8,128)(2,1)S(1)}, bf16[11,2,32,256]{3,2,1,0:T(8,128)(2,1)S(1)}, u32[]{:S(2)}, u32[]{:S(2)}) collective-permute-start(bf16[11,2,32,256]{3,2,1,0:T(8,128)(2,1)S(1)} %get-tuple-element.64.refs_0_), channel_id=1, source_target_pairs={{0,2},{2,4},{4,6},{6,8},{8,10},{10,12},{12,14},{14,0},{16,30},{18,... | collective-permute-start | bytes 1081352 | tf_op jit(solution)/shard_map/ppermute | solution.py:68
  47.8 11.7 %collective-permute-start.1 = (bf16[11,2,32,256]{3,2,1,0:T(8,128)(2,1)S(1)}, bf16[11,2,32,256]{3,2,1,0:T(8,128)(2,1)S(1)}, u32[]{:S(2)}, u32[]{:S(2)}) collective-permute-start(bf16[11,2,32,256]{3,2,1,0:T(8,128)(2,1)S(1)} %get-tuple-element.63.refs_1_), channel_id=1, source_target_pairs={{0,2},{2,4},{4,6},{6,8},{8,10},{10,12},{12,14},{14,0},{16,30},{18,... | collective-permute-start | bytes 1081352 | tf_op jit(solution)/shard_map/ppermute | solution.py:68
  51.4 11.1 %collective-permute-start.2 = (bf16[10,2,32,256]{3,2,1,0:T(8,128)(2,1)S(1)}, bf16[10,2,32,256]{3,2,1,0:T(8,128)(2,1)S(1)}, u32[]{:S(2)}, u32[]{:S(2)}) collective-permute-start(bf16[10,2,32,256]{3,2,1,0:T(8,128)(2,1)S(1)} %slice.14.refs_2_), channel_id=1, source_target_pairs={{0,2},{2,4},{4,6},{6,8},{8,10},{10,12},{12,14},{14,0},{16,30},{18,... | collective-permute-start | bytes 983048 | tf_op jit(solution)/shard_map/ppermute | solution.py:68
  55.1 11.2 %collective-permute-start.3 = (bf16[11,2,32,256]{3,2,1,0:T(8,128)(2,1)S(1)}, bf16[11,2,32,256]{3,2,1,0:T(8,128)(2,1)S(1)}, u32[]{:S(2)}, u32[]{:S(2)}) collective-permute-start(bf16[11,2,32,256]{3,2,1,0:T(8,128)(2,1)S(1)} %collective-permute-done.refs_3_), channel_id=1, source_target_pairs={{0,2},{2,4},{4,6},{6,8},{8,10},{10,12},{12,14},{14,0},{16,30},{18,... | collective-permute-start | bytes 1081352 | tf_op jit(solution)/shard_map/ppermute | solution.py:68
  59.6 11.4 %collective-permute-start.4 = (bf16[11,2,32,256]{3,2,1,0:T(8,128)(2,1)S(1)}, bf16[11,2,32,256]{3,2,1,0:T(8,128)(2,1)S(1)}, u32[]{:S(2)}, u32[]{:S(2)}) collective-permute-start(bf16[11,2,32,256]{3,2,1,0:T(8,128)(2,1)S(1)} %collective-permute-done.1.refs_4_), channel_id=1, source_target_pairs={{0,2},{2,4},{4,6},{6,8},{8,10},{10,12},{12,14},{14,0},{16,30},{18,... | collective-permute-start | bytes 1081352 | tf_op jit(solution)/shard_map/ppermute | solution.py:68
  62.5 12.3 %collective-permute-start.5 = (bf16[10,2,32,256]{3,2,1,0:T(8,128)(2,1)S(1)}, bf16[10,2,32,256]{3,2,1,0:T(8,128)(2,1)S(1)}, u32[]{:S(2)}, u32[]{:S(2)}) collective-permute-start(bf16[10,2,32,256]{3,2,1,0:T(8,128)(2,1)S(1)} %collective-permute-done.2.refs_5_), channel_id=1, source_target_pairs={{0,2},{2,4},{4,6},{6,8},{8,10},{10,12},{12,14},{14,0},{16,30},{18,... | collective-permute-start | bytes 983048 | tf_op jit(solution)/shard_map/ppermute | solution.py:68
  66.4 12.4 %collective-permute-start.6 = (bf16[11,2,32,256]{3,2,1,0:T(8,128)(2,1)S(1)}, bf16[11,2,32,256]{3,2,1,0:T(8,128)(2,1)S(1)}, u32[]{:S(2)}, u32[]{:S(2)}) collective-permute-start(bf16[11,2,32,256]{3,2,1,0:T(8,128)(2,1)S(1)} %collective-permute-done.3.refs_2_), channel_id=1, source_target_pairs={{0,2},{2,4},{4,6},{6,8},{8,10},{10,12},{12,14},{14,0},{16,30},{18,... | collective-permute-start | bytes 1081352 | tf_op jit(solution)/shard_map/ppermute | solution.py:68
  70.9 10.8 %collective-permute-start.7 = (bf16[11,2,32,256]{3,2,1,0:T(8,128)(2,1)S(1)}, bf16[11,2,32,256]{3,2,1,0:T(8,128)(2,1)S(1)}, u32[]{:S(2)}, u32[]{:S(2)}) collective-permute-start(bf16[11,2,32,256]{3,2,1,0:T(8,128)(2,1)S(1)} %collective-permute-done.4.refs_3_), channel_id=1, source_target_pairs={{0,2},{2,4},{4,6},{6,8},{8,10},{10,12},{12,14},{14,0},{16,30},{18,... | collective-permute-start | bytes 1081352 | tf_op jit(solution)/shard_map/ppermute | solution.py:68
  74.8 10.8 %collective-permute-start.8 = (bf16[10,2,32,256]{3,2,1,0:T(8,128)(2,1)S(1)}, bf16[10,2,32,256]{3,2,1,0:T(8,128)(2,1)S(1)}, u32[]{:S(2)}, u32[]{:S(2)}) collective-permute-start(bf16[10,2,32,256]{3,2,1,0:T(8,128)(2,1)S(1)} %collective-permute-done.5.refs_4_), channel_id=1, source_target_pairs={{0,2},{2,4},{4,6},{6,8},{8,10},{10,12},{12,14},{14,0},{16,30},{18,... | collective-permute-start | bytes 983048 | tf_op jit(solution)/shard_map/ppermute | solution.py:68
  78.7 10.8 %collective-permute-start.9 = (bf16[11,2,32,256]{3,2,1,0:T(8,128)(2,1)S(1)}, bf16[11,2,32,256]{3,2,1,0:T(8,128)(2,1)S(1)}, u32[]{:S(2)}, u32[]{:S(2)}) collective-permute-start(bf16[11,2,32,256]{3,2,1,0:T(8,128)(2,1)S(1)} %collective-permute-done.6.refs_2_), channel_id=1, source_target_pairs={{0,2},{2,4},{4,6},{6,8},{8,10},{10,12},{12,14},{14,0},{16,30},{18,... | collective-permute-start | bytes 1081352 | tf_op jit(solution)/shard_map/ppermute | solution.py:68
  81.8 11.4 %collective-permute-start.10 = (bf16[11,2,32,256]{3,2,1,0:T(8,128)(2,1)S(1)}, bf16[11,2,32,256]{3,2,1,0:T(8,128)(2,1)S(1)}, u32[]{:S(2)}, u32[]{:S(2)}) collective-permute-start(bf16[11,2,32,256]{3,2,1,0:T(8,128)(2,1)S(1)} %collective-permute-done.7.refs_3_), channel_id=1, source_target_pairs={{0,2},{2,4},{4,6},{6,8},{8,10},{10,12},{12,14},{14,0},{16,30},{18,... | collective-permute-start | bytes 1081352 | tf_op jit(solution)/shard_map/ppermute | solution.py:68
  85.6 11.2 %collective-permute-start.11 = (bf16[10,2,32,256]{3,2,1,0:T(8,128)(2,1)S(1)}, bf16[10,2,32,256]{3,2,1,0:T(8,128)(2,1)S(1)}, u32[]{:S(2)}, u32[]{:S(2)}) collective-permute-start(bf16[10,2,32,256]{3,2,1,0:T(8,128)(2,1)S(1)} %collective-permute-done.8.refs_4_), channel_id=1, source_target_pairs={{0,2},{2,4},{4,6},{6,8},{8,10},{10,12},{12,14},{14,0},{16,30},{18,... | collective-permute-start | bytes 983048 | tf_op jit(solution)/shard_map/ppermute | solution.py:68
  89.6 11.2 %collective-permute-start.12 = (bf16[11,2,32,256]{3,2,1,0:T(8,128)(2,1)S(1)}, bf16[11,2,32,256]{3,2,1,0:T(8,128)(2,1)S(1)}, u32[]{:S(2)}, u32[]{:S(2)}) collective-permute-start(bf16[11,2,32,256]{3,2,1,0:T(8,128)(2,1)S(1)} %collective-permute-done.9.refs_2_), channel_id=1, source_target_pairs={{0,2},{2,4},{4,6},{6,8},{8,10},{10,12},{12,14},{14,0},{16,30},{18,... | collective-permute-start | bytes 1081352 | tf_op jit(solution)/shard_map/ppermute | solution.py:68
  93.1 11.2 %collective-permute-start.13 = (bf16[11,2,32,256]{3,2,1,0:T(8,128)(2,1)S(1)}, bf16[11,2,32,256]{3,2,1,0:T(8,128)(2,1)S(1)}, u32[]{:S(2)}, u32[]{:S(2)}) collective-permute-start(bf16[11,2,32,256]{3,2,1,0:T(8,128)(2,1)S(1)} %collective-permute-done.10.refs_3_), channel_id=1, source_target_pairs={{0,2},{2,4},{4,6},{6,8},{8,10},{10,12},{12,14},{14,0},{16,30},{18,... | collective-permute-start | bytes 1081352 | tf_op jit(solution)/shard_map/ppermute | solution.py:68
  96.8 11.2 %collective-permute-start.14 = (bf16[10,2,32,256]{3,2,1,0:T(8,128)(2,1)S(1)}, bf16[10,2,32,256]{3,2,1,0:T(8,128)(2,1)S(1)}, u32[]{:S(2)}, u32[]{:S(2)}) collective-permute-start(bf16[10,2,32,256]{3,2,1,0:T(8,128)(2,1)S(1)} %collective-permute-done.11.refs_4_), channel_id=1, source_target_pairs={{0,2},{2,4},{4,6},{6,8},{8,10},{10,12},{12,14},{14,0},{16,30},{18,... | collective-permute-start | bytes 983048 | tf_op jit(solution)/shard_map/ppermute | solution.py:68
  100.8 11.2 %collective-permute-start.15 = (bf16[11,2,32,256]{3,2,1,0:T(8,128)(2,1)S(1)}, bf16[11,2,32,256]{3,2,1,0:T(8,128)(2,1)S(1)}, u32[]{:S(2)}, u32[]{:S(2)}) collective-permute-start(bf16[11,2,32,256]{3,2,1,0:T(8,128)(2,1)S(1)} %collective-permute-done.12.refs_2_), channel_id=1, source_target_pairs={{0,2},{2,4},{4,6},{6,8},{8,10},{10,12},{12,14},{14,0},{16,30},{18,... | collective-permute-start | bytes 1081352 | tf_op jit(solution)/shard_map/ppermute | solution.py:68
  104.4 11.2 %collective-permute-start.16 = (bf16[11,2,32,256]{3,2,1,0:T(8,128)(2,1)S(1)}, bf16[11,2,32,256]{3,2,1,0:T(8,128)(2,1)S(1)}, u32[]{:S(2)}, u32[]{:S(2)}) collective-permute-start(bf16[11,2,32,256]{3,2,1,0:T(8,128)(2,1)S(1)} %collective-permute-done.13.refs_3_), channel_id=1, source_target_pairs={{0,2},{2,4},{4,6},{6,8},{8,10},{10,12},{12,14},{14,0},{16,30},{18,... | collective-permute-start | bytes 1081352 | tf_op jit(solution)/shard_map/ppermute | solution.py:68
  108.1 11.2 %collective-permute-start.17 = (bf16[10,2,32,256]{3,2,1,0:T(8,128)(2,1)S(1)}, bf16[10,2,32,256]{3,2,1,0:T(8,128)(2,1)S(1)}, u32[]{:S(2)}, u32[]{:S(2)}) collective-permute-start(bf16[10,2,32,256]{3,2,1,0:T(8,128)(2,1)S(1)} %collective-permute-done.14.refs_4_), channel_id=1, source_target_pairs={{0,2},{2,4},{4,6},{6,8},{8,10},{10,12},{12,14},{14,0},{16,30},{18,... | collective-permute-start | bytes 983048 | tf_op jit(solution)/shard_map/ppermute | solution.py:68
  111.6 15.3 %copy-start = (s32[17,2]{0,1:T(2,128)S(1)}, s32[17,2]{0,1:T(2,128)}, u32[]{:S(2)}) copy-start(s32[17,2]{0,1:T(2,128)} %param.3) | copy-start | bytes 412
  112.0 11.8 %collective-permute-start.18 = (bf16[11,2,32,256]{3,2,1,0:T(8,128)(2,1)S(1)}, bf16[11,2,32,256]{3,2,1,0:T(8,128)(2,1)S(1)}, u32[]{:S(2)}, u32[]{:S(2)}) collective-permute-start(bf16[11,2,32,256]{3,2,1,0:T(8,128)(2,1)S(1)} %collective-permute-done.15.refs_2_), channel_id=1, source_target_pairs={{0,2},{2,4},{4,6},{6,8},{8,10},{10,12},{12,14},{14,0},{16,30},{18,... | collective-permute-start | bytes 1081352 | tf_op jit(solution)/shard_map/ppermute | solution.py:68
  115.6 11.2 %collective-permute-start.19 = (bf16[11,2,32,256]{3,2,1,0:T(8,128)(2,1)S(1)}, bf16[11,2,32,256]{3,2,1,0:T(8,128)(2,1)S(1)}, u32[]{:S(2)}, u32[]{:S(2)}) collective-permute-start(bf16[11,2,32,256]{3,2,1,0:T(8,128)(2,1)S(1)} %collective-permute-done.16.refs_3_), channel_id=1, source_target_pairs={{0,2},{2,4},{4,6},{6,8},{8,10},{10,12},{12,14},{14,0},{16,30},{18,... | collective-permute-start | bytes 1081352 | tf_op jit(solution)/shard_map/ppermute | solution.py:68
  119.3 11.0 %collective-permute-start.20 = (bf16[10,2,32,256]{3,2,1,0:T(8,128)(2,1)S(1)}, bf16[10,2,32,256]{3,2,1,0:T(8,128)(2,1)S(1)}, u32[]{:S(2)}, u32[]{:S(2)}) collective-permute-start(bf16[10,2,32,256]{3,2,1,0:T(8,128)(2,1)S(1)} %collective-permute-done.17.refs_4_), channel_id=1, source_target_pairs={{0,2},{2,4},{4,6},{6,8},{8,10},{10,12},{12,14},{14,0},{16,30},{18,... | collective-permute-start | bytes 983048 | tf_op jit(solution)/shard_map/ppermute | solution.py:68
  132.5 14.4 %collective-permute-start.21 = (s16[17,2,64,128]{3,2,1,0:T(8,128)(2,1)S(1)}, s16[17,2,64,128]{3,2,1,0:T(8,128)(2,1)S(1)}, u32[]{:S(2)}, u32[]{:S(2)}) collective-permute-start(s16[17,2,64,128]{3,2,1,0:T(8,128)(2,1)S(1)} %get-tuple-element.61), channel_id=1, source_target_pairs={{0,1},{1,0},{2,3},{3,2},{4,5},{5,4},{6,7},{7,6},{8,9},{9,8},{10,11... | collective-permute-start | bytes 1671176 | tf_op jit(solution)/shard_map/ppermute | solution.py:161
  135.0 11.9 %collective-permute-start.22 = (f32[17,2,128]{2,1,0:T(2,128)S(1)}, f32[17,2,128]{2,1,0:T(2,128)S(1)}, u32[]{:S(2)}, u32[]{:S(2)}) collective-permute-start(f32[17,2,128]{2,1,0:T(2,128)S(1)} %get-tuple-element.62), channel_id=1, source_target_pairs={{0,1},{1,0},{2,3},{3,2},{4,5},{5,4},{6,7},{7,6},{8,9},{9,8},{10,11... | collective-permute-start | bytes 52232 | tf_op jit(solution)/shard_map/ppermute | solution.py:161

commit v6 on v4

--- a/solution.py
+++ b/solution.py
@@ -104,8 +104,8 @@
 
     def tile(k, carry):
         real, imag = products(where, table, held, sources, k)
-        whole[0] = (total[k, 0] + real) * (1.0 / TIME)
-        whole[1] = (total[k, 1] + imag) * (1.0 / TIME)
+        whole[0] = total[k, 0] + real
+        whole[1] = total[k, 1] + imag
         keep[k] = whole[:, pl.ds(pl.multiple_of(where[1] * half, half), half), :]
         other = whole[:, pl.ds(pl.multiple_of((1 - where[1]) * half, half), half), :]
         most = jnp.max(jnp.abs(other), axis=1, keepdims=True)
@@ -158,7 +158,7 @@
     turned = lax.all_to_all(ordered, "chan", split_axis=0, concat_axis=0, tiled=True)
     _, keep, send, scale = tiles(where, table, *rings(turned))
     send, scale = (lax.ppermute(half, "integ", [(0, 1), (1, 0)]) for half in (send, scale))
-    return (keep + send.astype(jnp.float32) * (1.0 / STEPS) * scale[:, :, None])[:, None]
+    return ((keep + send.astype(jnp.float32) * (1.0 / STEPS) * scale[:, :, None]) * (1.0 / TIME))[:, None]
 
 
 def solution(mesh):

time: 149 us -> 149 us (level)
  no operation moved by 1% of the time
where the time goes in v6:
time: 149 us; the launch traced here: 148 us
  starting transfers between devices  79.6 us (53%)
  blocking collectives  42.9 us (29%)
  waiting for transfers between devices  13.8 us (9%)
  Pallas kernels  8.85 us (6%)
    ppermute x21, starting transfers between devices, rings(): passed = [lax.ppermute(piece, ('chan', 'pair'), ROUND) for piece in now]  73.8 us
    all_to_all x1, blocking collectives, body(): lax.all_to_all(ordered, 'chan', split_axis=0, concat_axis=0, tiled=True)  42.9 us
    ppermute x2, waiting for transfers between devices, body(): lax.ppermute(half, 'integ', [(0, 1), (1, 0)])  8.52 us
    ppermute x2, starting transfers between devices, body(): lax.ppermute(half, 'integ', [(0, 1), (1, 0)])  5.84 us
    ppermute x21, waiting for transfers between devices, rings(): passed = [lax.ppermute(piece, ('chan', 'pair'), ROUND) for piece in now]  5.28 us
    pallas_call x6, Pallas kernels, put(): pl.pallas_call(lambda *refs: put_kernel(steps, *refs), out_shape=(jax.Sha...  3.56 us
    pallas_call x1, Pallas kernels, tiles(): pl.pallas_call(most_kernel, out_shape=(blocks, jax.ShapeDtypeStruct((coun...  3.02 us
  transfers between devices with their start and end apart: 23, of which 9 were waited for; matrix products, arithmetic and copies ran while one was open for 0% of the time, Pallas kernels for 4%

profile of v6, /device:TPU:64, one launch (start us, length us, event | category | flops | bytes accessed | tf_op | source)
XLA Modules:
  0.0 148.3 jit_solution(14588266099378491468)
XLA Ops:
  0.0 1.3 copy.13
  1.3 0.1 pad_add_fusion.where
  1.4 42.9 %all_to_all.5 = bf16[32,2,32,256]{3,2,1,0:T(8,128)(2,1)S(1)} all-to-all(bf16[32,2,32,256]{3,2,1,0:T(8,128)(2,1)S(1)} %bitcast.13), channel_id=1, replica_groups=mesh['chan'=32,'pair'=8,'integ'=2] {'chan'}, dimensions={0} | all-to-all | bytes 2097152 | tf_op jit(solution)/shard_map/all_to_all | solution.py:158
  44.3 0.1 fusion
  44.3 3.5 %collective-permute-start = (bf16[11,2,32,256]{3,2,1,0:T(8,128)(2,1)S(1)}, bf16[11,2,32,256]{3,2,1,0:T(8,128)(2,1)S(1)}, u32[]{:S(2)}, u32[]{:S(2)}) collective-permute-start(bf16[11,2,32,256]{3,2,1,0:T(8,128)(2,1)S(1)} %get-tuple-element.64.refs_0_), channel_id=1, source_target_pairs={{0,2},{2,4},{4,6},{6,8},{8,10},{10,12},{12,14},{14,0},{16,30},{18,... | collective-permute-start | bytes 1081352 | tf_op jit(solution)/shard_map/ppermute | solution.py:68
  47.8 3.5 %collective-permute-start.1 = (bf16[11,2,32,256]{3,2,1,0:T(8,128)(2,1)S(1)}, bf16[11,2,32,256]{3,2,1,0:T(8,128)(2,1)S(1)}, u32[]{:S(2)}, u32[]{:S(2)}) collective-permute-start(bf16[11,2,32,256]{3,2,1,0:T(8,128)(2,1)S(1)} %get-tuple-element.63.refs_1_), channel_id=1, source_target_pairs={{0,2},{2,4},{4,6},{6,8},{8,10},{10,12},{12,14},{14,0},{16,30},{18,... | collective-permute-start | bytes 1081352 | tf_op jit(solution)/shard_map/ppermute | solution.py:68
  51.4 3.5 %collective-permute-start.2 = (bf16[10,2,32,256]{3,2,1,0:T(8,128)(2,1)S(1)}, bf16[10,2,32,256]{3,2,1,0:T(8,128)(2,1)S(1)}, u32[]{:S(2)}, u32[]{:S(2)}) collective-permute-start(bf16[10,2,32,256]{3,2,1,0:T(8,128)(2,1)S(1)} %slice.14.refs_2_), channel_id=1, source_target_pairs={{0,2},{2,4},{4,6},{6,8},{8,10},{10,12},{12,14},{14,0},{16,30},{18,... | collective-permute-start | bytes 983048 | tf_op jit(solution)/shard_map/ppermute | solution.py:68
  54.8 0.3 collective-permute-done.refs_3_
  55.1 4.4 %collective-permute-start.3 = (bf16[11,2,32,256]{3,2,1,0:T(8,128)(2,1)S(1)}, bf16[11,2,32,256]{3,2,1,0:T(8,128)(2,1)S(1)}, u32[]{:S(2)}, u32[]{:S(2)}) collective-permute-start(bf16[11,2,32,256]{3,2,1,0:T(8,128)(2,1)S(1)} %collective-permute-done.refs_3_), channel_id=1, source_target_pairs={{0,2},{2,4},{4,6},{6,8},{8,10},{10,12},{12,14},{14,0},{16,30},{18,... | collective-permute-start | bytes 1081352 | tf_op jit(solution)/shard_map/ppermute | solution.py:68
  59.6 2.6 %collective-permute-start.4 = (bf16[11,2,32,256]{3,2,1,0:T(8,128)(2,1)S(1)}, bf16[11,2,32,256]{3,2,1,0:T(8,128)(2,1)S(1)}, u32[]{:S(2)}, u32[]{:S(2)}) collective-permute-start(bf16[11,2,32,256]{3,2,1,0:T(8,128)(2,1)S(1)} %collective-permute-done.1.refs_4_), channel_id=1, source_target_pairs={{0,2},{2,4},{4,6},{6,8},{8,10},{10,12},{12,14},{14,0},{16,30},{18,... | collective-permute-start | bytes 1081352 | tf_op jit(solution)/shard_map/ppermute | solution.py:68
  62.2 0.3 collective-permute-done.2.refs_5_
  62.5 2.3 %collective-permute-start.5 = (bf16[10,2,32,256]{3,2,1,0:T(8,128)(2,1)S(1)}, bf16[10,2,32,256]{3,2,1,0:T(8,128)(2,1)S(1)}, u32[]{:S(2)}, u32[]{:S(2)}) collective-permute-start(bf16[10,2,32,256]{3,2,1,0:T(8,128)(2,1)S(1)} %collective-permute-done.2.refs_5_), channel_id=1, source_target_pairs={{0,2},{2,4},{4,6},{6,8},{8,10},{10,12},{12,14},{14,0},{16,30},{18,... | collective-permute-start | bytes 983048 | tf_op jit(solution)/shard_map/ppermute | solution.py:68
  64.8 0.8 put.6
  65.6 0.7 collective-permute-done.3.refs_2_
  66.4 4.6 %collective-permute-start.6 = (bf16[11,2,32,256]{3,2,1,0:T(8,128)(2,1)S(1)}, bf16[11,2,32,256]{3,2,1,0:T(8,128)(2,1)S(1)}, u32[]{:S(2)}, u32[]{:S(2)}) collective-permute-start(bf16[11,2,32,256]{3,2,1,0:T(8,128)(2,1)S(1)} %collective-permute-done.3.refs_2_), channel_id=1, source_target_pairs={{0,2},{2,4},{4,6},{6,8},{8,10},{10,12},{12,14},{14,0},{16,30},{18,... | collective-permute-start | bytes 1081352 | tf_op jit(solution)/shard_map/ppermute | solution.py:68
  70.9 0.0 collective-permute-done.4.refs_3_
  70.9 3.8 %collective-permute-start.7 = (bf16[11,2,32,256]{3,2,1,0:T(8,128)(2,1)S(1)}, bf16[11,2,32,256]{3,2,1,0:T(8,128)(2,1)S(1)}, u32[]{:S(2)}, u32[]{:S(2)}) collective-permute-start(bf16[11,2,32,256]{3,2,1,0:T(8,128)(2,1)S(1)} %collective-permute-done.4.refs_3_), channel_id=1, source_target_pairs={{0,2},{2,4},{4,6},{6,8},{8,10},{10,12},{12,14},{14,0},{16,30},{18,... | collective-permute-start | bytes 1081352 | tf_op jit(solution)/shard_map/ppermute | solution.py:68
  74.8 3.5 %collective-permute-start.8 = (bf16[10,2,32,256]{3,2,1,0:T(8,128)(2,1)S(1)}, bf16[10,2,32,256]{3,2,1,0:T(8,128)(2,1)S(1)}, u32[]{:S(2)}, u32[]{:S(2)}) collective-permute-start(bf16[10,2,32,256]{3,2,1,0:T(8,128)(2,1)S(1)} %collective-permute-done.5.refs_4_), channel_id=1, source_target_pairs={{0,2},{2,4},{4,6},{6,8},{8,10},{10,12},{12,14},{14,0},{16,30},{18,... | collective-permute-start | bytes 983048 | tf_op jit(solution)/shard_map/ppermute | solution.py:68
  78.3 0.4 put.7
  78.7 0.0 collective-permute-done.6.refs_2_
  78.7 3.0 %collective-permute-start.9 = (bf16[11,2,32,256]{3,2,1,0:T(8,128)(2,1)S(1)}, bf16[11,2,32,256]{3,2,1,0:T(8,128)(2,1)S(1)}, u32[]{:S(2)}, u32[]{:S(2)}) collective-permute-start(bf16[11,2,32,256]{3,2,1,0:T(8,128)(2,1)S(1)} %collective-permute-done.6.refs_2_), channel_id=1, source_target_pairs={{0,2},{2,4},{4,6},{6,8},{8,10},{10,12},{12,14},{14,0},{16,30},{18,... | collective-permute-start | bytes 1081352 | tf_op jit(solution)/shard_map/ppermute | solution.py:68
  81.8 3.8 %collective-permute-start.10 = (bf16[11,2,32,256]{3,2,1,0:T(8,128)(2,1)S(1)}, bf16[11,2,32,256]{3,2,1,0:T(8,128)(2,1)S(1)}, u32[]{:S(2)}, u32[]{:S(2)}) collective-permute-start(bf16[11,2,32,256]{3,2,1,0:T(8,128)(2,1)S(1)} %collective-permute-done.7.refs_3_), channel_id=1, source_target_pairs={{0,2},{2,4},{4,6},{6,8},{8,10},{10,12},{12,14},{14,0},{16,30},{18,... | collective-permute-start | bytes 1081352 | tf_op jit(solution)/shard_map/ppermute | solution.py:68
  85.6 3.5 %collective-permute-start.11 = (bf16[10,2,32,256]{3,2,1,0:T(8,128)(2,1)S(1)}, bf16[10,2,32,256]{3,2,1,0:T(8,128)(2,1)S(1)}, u32[]{:S(2)}, u32[]{:S(2)}) collective-permute-start(bf16[10,2,32,256]{3,2,1,0:T(8,128)(2,1)S(1)} %collective-permute-done.8.refs_4_), channel_id=1, source_target_pairs={{0,2},{2,4},{4,6},{6,8},{8,10},{10,12},{12,14},{14,0},{16,30},{18,... | collective-permute-start | bytes 983048 | tf_op jit(solution)/shard_map/ppermute | solution.py:68
  89.1 0.4 put.8
  89.6 3.4 %collective-permute-start.12 = (bf16[11,2,32,256]{3,2,1,0:T(8,128)(2,1)S(1)}, bf16[11,2,32,256]{3,2,1,0:T(8,128)(2,1)S(1)}, u32[]{:S(2)}, u32[]{:S(2)}) collective-permute-start(bf16[11,2,32,256]{3,2,1,0:T(8,128)(2,1)S(1)} %collective-permute-done.9.refs_2_), channel_id=1, source_target_pairs={{0,2},{2,4},{4,6},{6,8},{8,10},{10,12},{12,14},{14,0},{16,30},{18,... | collective-permute-start | bytes 1081352 | tf_op jit(solution)/shard_map/ppermute | solution.py:68
  93.0 0.2 collective-permute-done.10.refs_3_
  93.1 3.7 %collective-permute-start.13 = (bf16[11,2,32,256]{3,2,1,0:T(8,128)(2,1)S(1)}, bf16[11,2,32,256]{3,2,1,0:T(8,128)(2,1)S(1)}, u32[]{:S(2)}, u32[]{:S(2)}) collective-permute-start(bf16[11,2,32,256]{3,2,1,0:T(8,128)(2,1)S(1)} %collective-permute-done.10.refs_3_), channel_id=1, source_target_pairs={{0,2},{2,4},{4,6},{6,8},{8,10},{10,12},{12,14},{14,0},{16,30},{18,... | collective-permute-start | bytes 1081352 | tf_op jit(solution)/shard_map/ppermute | solution.py:68
  96.8 3.5 %collective-permute-start.14 = (bf16[10,2,32,256]{3,2,1,0:T(8,128)(2,1)S(1)}, bf16[10,2,32,256]{3,2,1,0:T(8,128)(2,1)S(1)}, u32[]{:S(2)}, u32[]{:S(2)}) collective-permute-start(bf16[10,2,32,256]{3,2,1,0:T(8,128)(2,1)S(1)} %collective-permute-done.11.refs_4_), channel_id=1, source_target_pairs={{0,2},{2,4},{4,6},{6,8},{8,10},{10,12},{12,14},{14,0},{16,30},{18,... | collective-permute-start | bytes 983048 | tf_op jit(solution)/shard_map/ppermute | solution.py:68
  100.3 0.4 put.9
  100.8 3.4 %collective-permute-start.15 = (bf16[11,2,32,256]{3,2,1,0:T(8,128)(2,1)S(1)}, bf16[11,2,32,256]{3,2,1,0:T(8,128)(2,1)S(1)}, u32[]{:S(2)}, u32[]{:S(2)}) collective-permute-start(bf16[11,2,32,256]{3,2,1,0:T(8,128)(2,1)S(1)} %collective-permute-done.12.refs_2_), channel_id=1, source_target_pairs={{0,2},{2,4},{4,6},{6,8},{8,10},{10,12},{12,14},{14,0},{16,30},{18,... | collective-permute-start | bytes 1081352 | tf_op jit(solution)/shard_map/ppermute | solution.py:68
  104.2 0.2 collective-permute-done.13.refs_3_
  104.4 3.7 %collective-permute-start.16 = (bf16[11,2,32,256]{3,2,1,0:T(8,128)(2,1)S(1)}, bf16[11,2,32,256]{3,2,1,0:T(8,128)(2,1)S(1)}, u32[]{:S(2)}, u32[]{:S(2)}) collective-permute-start(bf16[11,2,32,256]{3,2,1,0:T(8,128)(2,1)S(1)} %collective-permute-done.13.refs_3_), channel_id=1, source_target_pairs={{0,2},{2,4},{4,6},{6,8},{8,10},{10,12},{12,14},{14,0},{16,30},{18,... | collective-permute-start | bytes 1081352 | tf_op jit(solution)/shard_map/ppermute | solution.py:68
  108.1 3.5 %collective-permute-start.17 = (bf16[10,2,32,256]{3,2,1,0:T(8,128)(2,1)S(1)}, bf16[10,2,32,256]{3,2,1,0:T(8,128)(2,1)S(1)}, u32[]{:S(2)}, u32[]{:S(2)}) collective-permute-start(bf16[10,2,32,256]{3,2,1,0:T(8,128)(2,1)S(1)} %collective-permute-done.14.refs_4_), channel_id=1, source_target_pairs={{0,2},{2,4},{4,6},{6,8},{8,10},{10,12},{12,14},{14,0},{16,30},{18,... | collective-permute-start | bytes 983048 | tf_op jit(solution)/shard_map/ppermute | solution.py:68
  111.6 0.4 put.10
  112.0 3.4 %collective-permute-start.18 = (bf16[11,2,32,256]{3,2,1,0:T(8,128)(2,1)S(1)}, bf16[11,2,32,256]{3,2,1,0:T(8,128)(2,1)S(1)}, u32[]{:S(2)}, u32[]{:S(2)}) collective-permute-start(bf16[11,2,32,256]{3,2,1,0:T(8,128)(2,1)S(1)} %collective-permute-done.15.refs_2_), channel_id=1, source_target_pairs={{0,2},{2,4},{4,6},{6,8},{8,10},{10,12},{12,14},{14,0},{16,30},{18,... | collective-permute-start | bytes 1081352 | tf_op jit(solution)/shard_map/ppermute | solution.py:68
  115.4 0.2 collective-permute-done.16.refs_3_
  115.6 3.7 %collective-permute-start.19 = (bf16[11,2,32,256]{3,2,1,0:T(8,128)(2,1)S(1)}, bf16[11,2,32,256]{3,2,1,0:T(8,128)(2,1)S(1)}, u32[]{:S(2)}, u32[]{:S(2)}) collective-permute-start(bf16[11,2,32,256]{3,2,1,0:T(8,128)(2,1)S(1)} %collective-permute-done.16.refs_3_), channel_id=1, source_target_pairs={{0,2},{2,4},{4,6},{6,8},{8,10},{10,12},{12,14},{14,0},{16,30},{18,... | collective-permute-start | bytes 1081352 | tf_op jit(solution)/shard_map/ppermute | solution.py:68
  119.3 3.5 %collective-permute-start.20 = (bf16[10,2,32,256]{3,2,1,0:T(8,128)(2,1)S(1)}, bf16[10,2,32,256]{3,2,1,0:T(8,128)(2,1)S(1)}, u32[]{:S(2)}, u32[]{:S(2)}) collective-permute-start(bf16[10,2,32,256]{3,2,1,0:T(8,128)(2,1)S(1)} %collective-permute-done.17.refs_4_), channel_id=1, source_target_pairs={{0,2},{2,4},{4,6},{6,8},{8,10},{10,12},{12,14},{14,0},{16,30},{18,... | collective-permute-start | bytes 983048 | tf_op jit(solution)/shard_map/ppermute | solution.py:68
  122.8 0.0 copy-start
  122.8 1.0 put.11
  123.9 3.0 %collective-permute-done.19.refs_2_ = bf16[11,2,32,256]{3,2,1,0:T(8,128)(2,1)S(1)} collective-permute-done((bf16[11,2,32,256]{3,2,1,0:T(8,128)(2,1)S(1)}, bf16[11,2,32,256]{3,2,1,0:T(8,128)(2,1)S(1)}, u32[]{:S(2)}, u32[]{:S(2)}) %collective-permute-start.19) | collective-permute-done | bytes 360480 | tf_op jit(solution)/shard_map/ppermute | solution.py:68
  126.8 3.0 %most.1 = (bf16[8,32,2,32,256]{4,3,2,1,0:T(8,128)(2,1)S(1)}, f32[17,2,128,128]{3,2,1,0:T(8,128)S(1)}) custom-call(s32[3]{0:T(128)S(1)} %pad_add_fusion.where, s32[2,17]{1,0:T(2,128)S(1)} %bitcast.11, bf16[8,32,2,32,256]{4,3,2,1,0:T(8,128)(2,1)S(1)} %get-tuple-element.57.refs_0_, ...), custom_call_target="tpu_custom_call", output_to_operand_aliasing={{0}: (2, {})} | custom-call | flops 1140850688 | bytes 10485760 | tf_op jit(solution)/shard_map/most/pallas_call | solution.py:128
  129.9 0.5 collective-permute-done.20.last
  130.4 2.3 %rest.1 = (bf16[8,32,2,32,256]{4,3,2,1,0:T(8,128)(2,1)S(1)}, f32[17,2,64,128]{3,2,1,0:T(8,128)S(1)}, s16[17,2,64,128]{3,2,1,0:T(8,128)(2,1)S(1)}, f32[17,2,128]{2,1,0:T(2,128)S(1)}) custom-call(s32[3]{0:T(128)S(1)} %pad_add_fusion.where, s32[2,17]{1,0:T(2,128)S(1)} %bitcast.12, ...), custom_call_target="tpu_custom_call", output_to_operand_aliasing={{0}: (2, {})} | custom-call | flops 1140850688 | bytes 10485760 | tf_op jit(solution)/shard_map/rest/pallas_call | solution.py:138
  132.6 2.5 %collective-permute-start.21 = (s16[17,2,64,128]{3,2,1,0:T(8,128)(2,1)S(1)}, s16[17,2,64,128]{3,2,1,0:T(8,128)(2,1)S(1)}, u32[]{:S(2)}, u32[]{:S(2)}) collective-permute-start(s16[17,2,64,128]{3,2,1,0:T(8,128)(2,1)S(1)} %get-tuple-element.61), channel_id=1, source_target_pairs={{0,1},{1,0},{2,3},{3,2},{4,5},{5,4},{6,7},{7,6},{8,9},{9,8},{10,11... | collective-permute-start | bytes 1671176 | tf_op jit(solution)/shard_map/ppermute | solution.py:160
  135.1 3.3 %collective-permute-start.22 = (f32[17,2,128]{2,1,0:T(2,128)S(1)}, f32[17,2,128]{2,1,0:T(2,128)S(1)}, u32[]{:S(2)}, u32[]{:S(2)}) collective-permute-start(f32[17,2,128]{2,1,0:T(2,128)S(1)} %get-tuple-element.62), channel_id=1, source_target_pairs={{0,1},{1,0},{2,3},{3,2},{4,5},{5,4},{6,7},{7,6},{8,9},{9,8},{10,11... | collective-permute-start | bytes 52232 | tf_op jit(solution)/shard_map/ppermute | solution.py:160
  138.5 8.5 %collective-permute-done.22 = f32[17,2,128]{2,1,0:T(2,128)S(1)} collective-permute-done((f32[17,2,128]{2,1,0:T(2,128)S(1)}, f32[17,2,128]{2,1,0:T(2,128)S(1)}, u32[]{:S(2)}, u32[]{:S(2)}) %collective-permute-start.22) | collective-permute-done | bytes 17440 | tf_op jit(solution)/shard_map/ppermute | solution.py:160
  147.0 1.3 multiply_bitcast_fusion
  (15 shorter events, 0.1 us)
Async XLA Ops:
  44.3 10.8 %collective-permute-start = (bf16[11,2,32,256]{3,2,1,0:T(8,128)(2,1)S(1)}, bf16[11,2,32,256]{3,2,1,0:T(8,128)(2,1)S(1)}, u32[]{:S(2)}, u32[]{:S(2)}) collective-permute-start(bf16[11,2,32,256]{3,2,1,0:T(8,128)(2,1)S(1)} %get-tuple-element.64.refs_0_), channel_id=1, source_target_pairs={{0,2},{2,4},{4,6},{6,8},{8,10},{10,12},{12,14},{14,0},{16,30},{18,... | collective-permute-start | bytes 1081352 | tf_op jit(solution)/shard_map/ppermute | solution.py:68
  47.8 11.7 %collective-permute-start.1 = (bf16[11,2,32,256]{3,2,1,0:T(8,128)(2,1)S(1)}, bf16[11,2,32,256]{3,2,1,0:T(8,128)(2,1)S(1)}, u32[]{:S(2)}, u32[]{:S(2)}) collective-permute-start(bf16[11,2,32,256]{3,2,1,0:T(8,128)(2,1)S(1)} %get-tuple-element.63.refs_1_), channel_id=1, source_target_pairs={{0,2},{2,4},{4,6},{6,8},{8,10},{10,12},{12,14},{14,0},{16,30},{18,... | collective-permute-start | bytes 1081352 | tf_op jit(solution)/shard_map/ppermute | solution.py:68
  51.4 11.1 %collective-permute-start.2 = (bf16[10,2,32,256]{3,2,1,0:T(8,128)(2,1)S(1)}, bf16[10,2,32,256]{3,2,1,0:T(8,128)(2,1)S(1)}, u32[]{:S(2)}, u32[]{:S(2)}) collective-permute-start(bf16[10,2,32,256]{3,2,1,0:T(8,128)(2,1)S(1)} %slice.14.refs_2_), channel_id=1, source_target_pairs={{0,2},{2,4},{4,6},{6,8},{8,10},{10,12},{12,14},{14,0},{16,30},{18,... | collective-permute-start | bytes 983048 | tf_op jit(solution)/shard_map/ppermute | solution.py:68
  55.1 11.2 %collective-permute-start.3 = (bf16[11,2,32,256]{3,2,1,0:T(8,128)(2,1)S(1)}, bf16[11,2,32,256]{3,2,1,0:T(8,128)(2,1)S(1)}, u32[]{:S(2)}, u32[]{:S(2)}) collective-permute-start(bf16[11,2,32,256]{3,2,1,0:T(8,128)(2,1)S(1)} %collective-permute-done.refs_3_), channel_id=1, source_target_pairs={{0,2},{2,4},{4,6},{6,8},{8,10},{10,12},{12,14},{14,0},{16,30},{18,... | collective-permute-start | bytes 1081352 | tf_op jit(solution)/shard_map/ppermute | solution.py:68
  59.6 11.4 %collective-permute-start.4 = (bf16[11,2,32,256]{3,2,1,0:T(8,128)(2,1)S(1)}, bf16[11,2,32,256]{3,2,1,0:T(8,128)(2,1)S(1)}, u32[]{:S(2)}, u32[]{:S(2)}) collective-permute-start(bf16[11,2,32,256]{3,2,1,0:T(8,128)(2,1)S(1)} %collective-permute-done.1.refs_4_), channel_id=1, source_target_pairs={{0,2},{2,4},{4,6},{6,8},{8,10},{10,12},{12,14},{14,0},{16,30},{18,... | collective-permute-start | bytes 1081352 | tf_op jit(solution)/shard_map/ppermute | solution.py:68
  62.5 12.3 %collective-permute-start.5 = (bf16[10,2,32,256]{3,2,1,0:T(8,128)(2,1)S(1)}, bf16[10,2,32,256]{3,2,1,0:T(8,128)(2,1)S(1)}, u32[]{:S(2)}, u32[]{:S(2)}) collective-permute-start(bf16[10,2,32,256]{3,2,1,0:T(8,128)(2,1)S(1)} %collective-permute-done.2.refs_5_), channel_id=1, source_target_pairs={{0,2},{2,4},{4,6},{6,8},{8,10},{10,12},{12,14},{14,0},{16,30},{18,... | collective-permute-start | bytes 983048 | tf_op jit(solution)/shard_map/ppermute | solution.py:68
  66.4 12.4 %collective-permute-start.6 = (bf16[11,2,32,256]{3,2,1,0:T(8,128)(2,1)S(1)}, bf16[11,2,32,256]{3,2,1,0:T(8,128)(2,1)S(1)}, u32[]{:S(2)}, u32[]{:S(2)}) collective-permute-start(bf16[11,2,32,256]{3,2,1,0:T(8,128)(2,1)S(1)} %collective-permute-done.3.refs_2_), channel_id=1, source_target_pairs={{0,2},{2,4},{4,6},{6,8},{8,10},{10,12},{12,14},{14,0},{16,30},{18,... | collective-permute-start | bytes 1081352 | tf_op jit(solution)/shard_map/ppermute | solution.py:68
  70.9 10.8 %collective-permute-start.7 = (bf16[11,2,32,256]{3,2,1,0:T(8,128)(2,1)S(1)}, bf16[11,2,32,256]{3,2,1,0:T(8,128)(2,1)S(1)}, u32[]{:S(2)}, u32[]{:S(2)}) collective-permute-start(bf16[11,2,32,256]{3,2,1,0:T(8,128)(2,1)S(1)} %collective-permute-done.4.refs_3_), channel_id=1, source_target_pairs={{0,2},{2,4},{4,6},{6,8},{8,10},{10,12},{12,14},{14,0},{16,30},{18,... | collective-permute-start | bytes 1081352 | tf_op jit(solution)/shard_map/ppermute | solution.py:68
  74.8 10.8 %collective-permute-start.8 = (bf16[10,2,32,256]{3,2,1,0:T(8,128)(2,1)S(1)}, bf16[10,2,32,256]{3,2,1,0:T(8,128)(2,1)S(1)}, u32[]{:S(2)}, u32[]{:S(2)}) collective-permute-start(bf16[10,2,32,256]{3,2,1,0:T(8,128)(2,1)S(1)} %collective-permute-done.5.refs_4_), channel_id=1, source_target_pairs={{0,2},{2,4},{4,6},{6,8},{8,10},{10,12},{12,14},{14,0},{16,30},{18,... | collective-permute-start | bytes 983048 | tf_op jit(solution)/shard_map/ppermute | solution.py:68
  78.7 10.8 %collective-permute-start.9 = (bf16[11,2,32,256]{3,2,1,0:T(8,128)(2,1)S(1)}, bf16[11,2,32,256]{3,2,1,0:T(8,128)(2,1)S(1)}, u32[]{:S(2)}, u32[]{:S(2)}) collective-permute-start(bf16[11,2,32,256]{3,2,1,0:T(8,128)(2,1)S(1)} %collective-permute-done.6.refs_2_), channel_id=1, source_target_pairs={{0,2},{2,4},{4,6},{6,8},{8,10},{10,12},{12,14},{14,0},{16,30},{18,... | collective-permute-start | bytes 1081352 | tf_op jit(solution)/shard_map/ppermute | solution.py:68
  81.8 11.4 %collective-permute-start.10 = (bf16[11,2,32,256]{3,2,1,0:T(8,128)(2,1)S(1)}, bf16[11,2,32,256]{3,2,1,0:T(8,128)(2,1)S(1)}, u32[]{:S(2)}, u32[]{:S(2)}) collective-permute-start(bf16[11,2,32,256]{3,2,1,0:T(8,128)(2,1)S(1)} %collective-permute-done.7.refs_3_), channel_id=1, source_target_pairs={{0,2},{2,4},{4,6},{6,8},{8,10},{10,12},{12,14},{14,0},{16,30},{18,... | collective-permute-start | bytes 1081352 | tf_op jit(solution)/shard_map/ppermute | solution.py:68
  85.6 11.2 %collective-permute-start.11 = (bf16[10,2,32,256]{3,2,1,0:T(8,128)(2,1)S(1)}, bf16[10,2,32,256]{3,2,1,0:T(8,128)(2,1)S(1)}, u32[]{:S(2)}, u32[]{:S(2)}) collective-permute-start(bf16[10,2,32,256]{3,2,1,0:T(8,128)(2,1)S(1)} %collective-permute-done.8.refs_4_), channel_id=1, source_target_pairs={{0,2},{2,4},{4,6},{6,8},{8,10},{10,12},{12,14},{14,0},{16,30},{18,... | collective-permute-start | bytes 983048 | tf_op jit(solution)/shard_map/ppermute | solution.py:68
  89.6 11.2 %collective-permute-start.12 = (bf16[11,2,32,256]{3,2,1,0:T(8,128)(2,1)S(1)}, bf16[11,2,32,256]{3,2,1,0:T(8,128)(2,1)S(1)}, u32[]{:S(2)}, u32[]{:S(2)}) collective-permute-start(bf16[11,2,32,256]{3,2,1,0:T(8,128)(2,1)S(1)} %collective-permute-done.9.refs_2_), channel_id=1, source_target_pairs={{0,2},{2,4},{4,6},{6,8},{8,10},{10,12},{12,14},{14,0},{16,30},{18,... | collective-permute-start | bytes 1081352 | tf_op jit(solution)/shard_map/ppermute | solution.py:68
  93.1 11.2 %collective-permute-start.13 = (bf16[11,2,32,256]{3,2,1,0:T(8,128)(2,1)S(1)}, bf16[11,2,32,256]{3,2,1,0:T(8,128)(2,1)S(1)}, u32[]{:S(2)}, u32[]{:S(2)}) collective-permute-start(bf16[11,2,32,256]{3,2,1,0:T(8,128)(2,1)S(1)} %collective-permute-done.10.refs_3_), channel_id=1, source_target_pairs={{0,2},{2,4},{4,6},{6,8},{8,10},{10,12},{12,14},{14,0},{16,30},{18,... | collective-permute-start | bytes 1081352 | tf_op jit(solution)/shard_map/ppermute | solution.py:68
  96.8 11.2 %collective-permute-start.14 = (bf16[10,2,32,256]{3,2,1,0:T(8,128)(2,1)S(1)}, bf16[10,2,32,256]{3,2,1,0:T(8,128)(2,1)S(1)}, u32[]{:S(2)}, u32[]{:S(2)}) collective-permute-start(bf16[10,2,32,256]{3,2,1,0:T(8,128)(2,1)S(1)} %collective-permute-done.11.refs_4_), channel_id=1, source_target_pairs={{0,2},{2,4},{4,6},{6,8},{8,10},{10,12},{12,14},{14,0},{16,30},{18,... | collective-permute-start | bytes 983048 | tf_op jit(solution)/shard_map/ppermute | solution.py:68
  100.8 11.2 %collective-permute-start.15 = (bf16[11,2,32,256]{3,2,1,0:T(8,128)(2,1)S(1)}, bf16[11,2,32,256]{3,2,1,0:T(8,128)(2,1)S(1)}, u32[]{:S(2)}, u32[]{:S(2)}) collective-permute-start(bf16[11,2,32,256]{3,2,1,0:T(8,128)(2,1)S(1)} %collective-permute-done.12.refs_2_), channel_id=1, source_target_pairs={{0,2},{2,4},{4,6},{6,8},{8,10},{10,12},{12,14},{14,0},{16,30},{18,... | collective-permute-start | bytes 1081352 | tf_op jit(solution)/shard_map/ppermute | solution.py:68
  104.4 11.2 %collective-permute-start.16 = (bf16[11,2,32,256]{3,2,1,0:T(8,128)(2,1)S(1)}, bf16[11,2,32,256]{3,2,1,0:T(8,128)(2,1)S(1)}, u32[]{:S(2)}, u32[]{:S(2)}) collective-permute-start(bf16[11,2,32,256]{3,2,1,0:T(8,128)(2,1)S(1)} %collective-permute-done.13.refs_3_), channel_id=1, source_target_pairs={{0,2},{2,4},{4,6},{6,8},{8,10},{10,12},{12,14},{14,0},{16,30},{18,... | collective-permute-start | bytes 1081352 | tf_op jit(solution)/shard_map/ppermute | solution.py:68
  108.1 11.2 %collective-permute-start.17 = (bf16[10,2,32,256]{3,2,1,0:T(8,128)(2,1)S(1)}, bf16[10,2,32,256]{3,2,1,0:T(8,128)(2,1)S(1)}, u32[]{:S(2)}, u32[]{:S(2)}) collective-permute-start(bf16[10,2,32,256]{3,2,1,0:T(8,128)(2,1)S(1)} %collective-permute-done.14.refs_4_), channel_id=1, source_target_pairs={{0,2},{2,4},{4,6},{6,8},{8,10},{10,12},{12,14},{14,0},{16,30},{18,... | collective-permute-start | bytes 983048 | tf_op jit(solution)/shard_map/ppermute | solution.py:68
  112.0 11.8 %collective-permute-start.18 = (bf16[11,2,32,256]{3,2,1,0:T(8,128)(2,1)S(1)}, bf16[11,2,32,256]{3,2,1,0:T(8,128)(2,1)S(1)}, u32[]{:S(2)}, u32[]{:S(2)}) collective-permute-start(bf16[11,2,32,256]{3,2,1,0:T(8,128)(2,1)S(1)} %collective-permute-done.15.refs_2_), channel_id=1, source_target_pairs={{0,2},{2,4},{4,6},{6,8},{8,10},{10,12},{12,14},{14,0},{16,30},{18,... | collective-permute-start | bytes 1081352 | tf_op jit(solution)/shard_map/ppermute | solution.py:68
  115.6 11.2 %collective-permute-start.19 = (bf16[11,2,32,256]{3,2,1,0:T(8,128)(2,1)S(1)}, bf16[11,2,32,256]{3,2,1,0:T(8,128)(2,1)S(1)}, u32[]{:S(2)}, u32[]{:S(2)}) collective-permute-start(bf16[11,2,32,256]{3,2,1,0:T(8,128)(2,1)S(1)} %collective-permute-done.16.refs_3_), channel_id=1, source_target_pairs={{0,2},{2,4},{4,6},{6,8},{8,10},{10,12},{12,14},{14,0},{16,30},{18,... | collective-permute-start | bytes 1081352 | tf_op jit(solution)/shard_map/ppermute | solution.py:68
  119.3 11.0 %collective-permute-start.20 = (bf16[10,2,32,256]{3,2,1,0:T(8,128)(2,1)S(1)}, bf16[10,2,32,256]{3,2,1,0:T(8,128)(2,1)S(1)}, u32[]{:S(2)}, u32[]{:S(2)}) collective-permute-start(bf16[10,2,32,256]{3,2,1,0:T(8,128)(2,1)S(1)} %collective-permute-done.17.refs_4_), channel_id=1, source_target_pairs={{0,2},{2,4},{4,6},{6,8},{8,10},{10,12},{12,14},{14,0},{16,30},{18,... | collective-permute-start | bytes 983048 | tf_op jit(solution)/shard_map/ppermute | solution.py:68
  122.8 4.0 %copy-start = (s32[17,2]{0,1:T(2,128)S(1)}, s32[17,2]{0,1:T(2,128)}, u32[]{:S(2)}) copy-start(s32[17,2]{0,1:T(2,128)} %param.3) | copy-start | bytes 412
  132.6 14.4 %collective-permute-start.21 = (s16[17,2,64,128]{3,2,1,0:T(8,128)(2,1)S(1)}, s16[17,2,64,128]{3,2,1,0:T(8,128)(2,1)S(1)}, u32[]{:S(2)}, u32[]{:S(2)}) collective-permute-start(s16[17,2,64,128]{3,2,1,0:T(8,128)(2,1)S(1)} %get-tuple-element.61), channel_id=1, source_target_pairs={{0,1},{1,0},{2,3},{3,2},{4,5},{5,4},{6,7},{7,6},{8,9},{9,8},{10,11... | collective-permute-start | bytes 1671176 | tf_op jit(solution)/shard_map/ppermute | solution.py:160
  135.1 11.9 %collective-permute-start.22 = (f32[17,2,128]{2,1,0:T(2,128)S(1)}, f32[17,2,128]{2,1,0:T(2,128)S(1)}, u32[]{:S(2)}, u32[]{:S(2)}) collective-permute-start(f32[17,2,128]{2,1,0:T(2,128)S(1)} %get-tuple-element.62), channel_id=1, source_target_pairs={{0,1},{1,0},{2,3},{3,2},{4,5},{5,4},{6,7},{7,6},{8,9},{9,8},{10,11... | collective-permute-start | bytes 52232 | tf_op jit(solution)/shard_map/ppermute | solution.py:160
